TPU v7x, 32 devices: a whole 2x2x4 slice. The times are simulated.
32 devices in a mesh: row: 4 (over y, x), col: 2 (over core), scan: 4 (over z).
Axes of the slice: x: 2, y: 2, z: 4, core: 2. Of those that a mesh axis runs over, the one named last changes fastest.
Arguments:
- object_field: float32 [2, 2, 2048, 1024], P(None, None, 'row', 'col'), may hold values from -6 to 6
- probe_field: float32 [2, 256, 256], replicated, may hold values from -6 to 6
- prop_phase: float32 [256, 256], replicated, may hold values from -3.140625 to 3.140625
- measured: float32 [4, 2, 4, 3, 256, 256], P('row', 'col', 'scan'), may hold values from 0.3 to 3
- positions: int32 [4, 2, 4, 3, 2], P('row', 'col', 'scan'), may hold values from -64 to 320, as said below
- counts: int32 [4, 2, 4], P('row', 'col', 'scan'), may hold values from 1 to 3, as said below
Outputs:
- object_grad: float32 [2, 2, 2048, 1024], P(None, None, ('row', 'scan'), 'col')
Inputs may be any that keep to these rules, and one draw needn't show every extreme that they name: `positions`: every patch lies inside the object; slots at and past the device's count are unused. `counts`: loads are uneven: some devices hold 3 patches while others of the same tile hold one.
All inputs are finite; a program needn't handle non-finite values.
Results may differ from a plain program's by a relative error of at most 0.018.
Values sent between devices are 32-bit elements; how exact they have to be, the bound alone decides.
No kernel may reach another device: no remote copies, remote signals or barrier semaphores. Data moves between devices by JAX's collectives and lax.ppermute only.
A program may use at most 64 MiB of HBM per device.

v0:
```python
import math

import jax
import jax.numpy as jnp
from jax import lax
from jax.sharding import PartitionSpec as P

PATCH = 256
HALO = 64
PMAX = 3


def from_behind(block, axis, distance):
    devices = range(lax.axis_size(axis))
    route = [(i - distance, i) for i in devices if i - distance in devices]
    return lax.ppermute(block, axis, route)


def extended_2(array, sides, width):
    for axis, dim in sides:
        size, length = (lax.axis_size(axis), array.shape[dim])
        up = [(i, (i + 1) % size) for i in range(size - 1)]
        down = [(j, i) for i, j in up]
        last = lax.slice_in_dim(array, length - width, length, axis=dim)
        first = lax.slice_in_dim(array, 0, width, axis=dim)
        before = lax.ppermute(last, axis, up)
        after = lax.ppermute(first, axis, down)
        array = jnp.concatenate([before, array, after], axis=dim)
    return array


def partner(value, axis, stride):
    mask = 2**stride
    pairs = [(source, source ^ mask) for source in range(lax.axis_size(axis))]
    return lax.ppermute(value, axis, pairs)


def dft_tables(length):
    index_line = jnp.arange(length, dtype=jnp.int32)
    product = index_line[:, None] * index_line[None, :] % length
    angles = product.astype(jnp.float32) * (2.0 * math.pi / length)
    cosines = jnp.cos(angles) / math.sqrt(length)
    sines = jnp.sin(angles) / math.sqrt(length)
    left_fwd = jnp.stack([jnp.stack([cosines, sines], 1), jnp.stack([-sines, cosines], 1)], 0)
    right_fwd = jnp.stack([jnp.stack([cosines, -sines], 1), jnp.stack([sines, cosines], 1)], 0)
    left_inv = jnp.stack([jnp.stack([cosines, -sines], 1), jnp.stack([sines, cosines], 1)], 0)
    right_inv = jnp.stack([jnp.stack([cosines, sines], 1), jnp.stack([-sines, cosines], 1)], 0)
    return (
        left_fwd.astype(jnp.bfloat16),
        right_fwd.astype(jnp.bfloat16),
        left_inv.astype(jnp.bfloat16),
        right_inv.astype(jnp.bfloat16),
    )


def transform(values, left_table, right_table):
    middle = jnp.einsum("qapb,pbc->qac", left_table, values, preferred_element_type=jnp.float32)
    middle = middle.astype(jnp.bfloat16)
    return jnp.einsum("pab,pbqc->qac", middle, right_table, preferred_element_type=jnp.float32)


def complex_mul(first, second):
    return jnp.stack(
        [first[0] * second[0] - first[1] * second[1], first[0] * second[1] + first[1] * second[0]]
    )


def conj_mul(first, second):
    return jnp.stack(
        [first[0] * second[0] + first[1] * second[1], first[0] * second[1] - first[1] * second[0]]
    )


def patch_grads(first_slice, second_slice, probe_field, propagator, intensity, tables):
    left_fwd, right_fwd, left_inv, right_inv = tables
    entrance = complex_mul(probe_field, first_slice).astype(jnp.bfloat16)
    spectrum = complex_mul(propagator, transform(entrance, left_fwd, right_fwd)).astype(
        jnp.bfloat16
    )
    arrived = transform(spectrum, left_inv, right_inv)
    leaving = complex_mul(second_slice, arrived).astype(jnp.bfloat16)
    far_field = transform(leaving, left_fwd, right_fwd)
    power = far_field[0] * far_field[0] + far_field[1] * far_field[1]
    residual = ((power - intensity)[None] * far_field).astype(jnp.bfloat16)
    back_second = transform(residual, left_inv, right_inv)
    grad_second = conj_mul(arrived, back_second)
    through = conj_mul(second_slice, back_second).astype(jnp.bfloat16)
    back_spectrum = conj_mul(propagator, transform(through, left_fwd, right_fwd)).astype(
        jnp.bfloat16
    )
    back_first = transform(back_spectrum, left_inv, right_inv)
    grad_first = conj_mul(probe_field, back_first)
    return jnp.stack([grad_first, grad_second])


def pass_rows(strip, offset):
    return from_behind(strip, "row", offset)


def pass_cols(strip, offset):
    return from_behind(strip, "col", offset)


def fold_rows(gradient, tile_size):
    top_rim = gradient[:, :HALO]
    bottom_rim = gradient[:, tile_size + HALO :]
    core_rows = gradient[:, HALO : tile_size + HALO]
    core_rows = core_rows.at[:, :HALO].add(pass_rows(bottom_rim, 1))
    return core_rows.at[:, tile_size - HALO :].add(pass_rows(top_rim, -1))


def fold_cols(gradient, tile_size):
    left_rim = gradient[:, :, :HALO]
    right_rim = gradient[:, :, tile_size + HALO :]
    core_cols = gradient[:, :, HALO : tile_size + HALO]
    core_cols = core_cols.at[:, :, :HALO].add(pass_cols(right_rim, 1))
    return core_cols.at[:, :, tile_size - HALO :].add(pass_cols(left_rim, -1))


def shards(object_field, probe_field, prop_phase, measured, positions, counts):
    tile_size = object_field.shape[2]
    extended = extended_2(object_field, (("row", 2), ("col", 3)), HALO)
    tables = dft_tables(PATCH)
    propagator = jnp.stack([jnp.cos(prop_phase), jnp.sin(prop_phase)])
    own_intensity = measured.reshape(PMAX, PATCH, PATCH)
    own_corners = positions.reshape(PMAX, 2)
    own_count = counts.reshape(())
    zero_index = jnp.zeros((), jnp.int32)
    gradient = jnp.zeros(extended.shape, jnp.float32)

    def add_patch(current, intensity, corner):
        starts = (zero_index, zero_index, corner[0] + HALO, corner[1] + HALO)
        window = lax.dynamic_slice(extended, starts, (2, 2, PATCH, PATCH))
        update = patch_grads(window[0], window[1], probe_field, propagator, intensity, tables)
        present = lax.dynamic_slice(current, starts, (2, 2, PATCH, PATCH))
        return lax.dynamic_update_slice(current, present + update, starts)

    which_bit = lax.axis_size("scan").bit_length() - 2
    last_slot = jnp.maximum(own_count - 1, 0)
    spare_intensity = lax.dynamic_index_in_dim(own_intensity, last_slot, 0, keepdims=False)
    spare_corner = lax.dynamic_index_in_dim(own_corners, last_slot, 0, keepdims=False)
    spare_info = jnp.concatenate([spare_corner, own_count[None]]).astype(jnp.float32)
    got_intensity, got_info = partner((spare_intensity, spare_info), "scan", which_bit)
    peer_corner = got_info[:2].astype(jnp.int32)
    peer_count = got_info[2].astype(jnp.int32)
    gives = (own_count - peer_count >= 2).astype(jnp.int32)
    takes = (peer_count - own_count >= 2).astype(jnp.int32)
    keep_count = own_count - gives
    total_count = keep_count + takes

    def run_slot(index, current):
        own_slot = jnp.minimum(index, PMAX - 1)
        mine = index < keep_count
        intensity = jnp.where(
            mine,
            lax.dynamic_index_in_dim(own_intensity, own_slot, 0, keepdims=False),
            got_intensity,
        )
        corner = jnp.where(
            mine, lax.dynamic_index_in_dim(own_corners, own_slot, 0, keepdims=False), peer_corner
        )
        return add_patch(current, intensity, corner)

    gradient = lax.fori_loop(0, total_count, run_slot, gradient)
    planes = gradient.reshape(4, tile_size + 2 * HALO, tile_size + 2 * HALO)
    core_rows = fold_rows(planes, tile_size)
    operand = fold_cols(core_rows, tile_size)
    summed = lax.psum_scatter(operand, "scan", scatter_dimension=1, tiled=True)
    return summed.reshape(2, 2, summed.shape[1], tile_size)


def solution(mesh):
    placed = (
        P(None, None, "row", "col"),
        P(),
        P(),
        P("row", "col", "scan", None, None, None),
        P("row", "col", "scan", None, None),
        P("row", "col", "scan"),
    )
    return jax.shard_map(
        shards,
        mesh=mesh,
        in_specs=placed,
        out_specs=P(None, None, ("row", "scan"), "col"),
        check_vma=False,
    )
```

profile of v0, /device:TPU:0, one launch (start us, length us, event | category | flops | bytes accessed | tf_op | source)
XLA Modules:
  0.0 274.3 jit_solution(8968757156441511860)
XLA Ops:
  6.5 1.3 fusion.87
  7.8 4.9 %collective-permute-start.1 = (f32[2,2,64,512]{3,2,1,0:T(8,128)S(1)}, f32[2,2,64,512]{3,2,1,0:T(8,128)S(1)}, u32[]{:S(2)}, u32[]{:S(2)}) collective-permute-start(f32[2,2,64,512]{3,2,1,0:T(8,128)S(1)} %get-tuple-element.401), channel_id=1, source_target_pairs={{0,8},{8,16},{16,24},{1,9},{9,17},{17,25},{2,10},{10,18},{18,26},{... | collective-permute-start | bytes 1572872 | tf_op jit(solution)/shard_map/ppermute | solution.py:26
  12.7 1.3 collective-permute-start.2
  14.7 0.9 dynamic-slice_reduce_fusion
  15.6 2.6 collective-permute-start
  18.2 1.7 dynamic-slice_bitcast_fusion.4
  20.2 5.2 %copy.38 = f32[2,2,512,512]{2,3,1,0:T(8,128)} copy(f32[2,2,512,512]{3,2,1,0:T(8,128)} %param.16) | data formatting | bytes 8388608 | tf_op args[0]
  25.5 1.0 fusion.83
  26.5 1.6 multiply_convert_fusion.1
  28.1 1.6 negate_convert_fusion
  30.1 7.0 %collective-permute-done.2 = f32[2,2,64,512]{3,2,1,0:T(8,128)S(1)} collective-permute-done((f32[2,2,64,512]{3,2,1,0:T(8,128)S(1)}, f32[2,2,64,512]{3,2,1,0:T(8,128)S(1)}, u32[]{:S(2)}, u32[]{:S(2)}) %collective-permute-start.2) | collective-permute-done | bytes 524320 | tf_op jit(solution)/shard_map/ppermute | solution.py:27
  37.4 2.8 %pad_maximum_fusion.3 = (f32[2,2,640,64]{2,3,1,0:T(8,128)}, f32[2,2,640,64]{2,3,1,0:T(8,128)}) fusion(f32[2,2,64,512]{2,3,1,0:T(8,128)S(1)} %copy.39, f32[2,2,512,512]{2,3,1,0:T(8,128)} %copy.38, f32[2,2,64,512]{2,3,1,0:T(8,128)S(1)} %copy.37), kind=kLoop, calls=%fused_computation.102 | loop fusion | flops 655360 | bytes 6553600 | tf_op jit(solution)/shard_map/slice | solution.py:24
  40.2 2.1 collective-permute-start.3
  42.3 1.3 collective-permute-start.4
  43.6 0.8 fusion.76
  44.5 2.0 copy.41
  46.5 1.0 pad_maximum_fusion.4
  47.6 2.5 fusion.88
  50.1 0.7 slice.340
  51.5 5.9 %pad_maximum_fusion = f32[2,2,640,640]{2,3,1,0:T(8,128)} fusion(f32[2,2,640,64]{2,3,1,0:T(8,128)} %collective-permute-done.4, f32[2,2,64,512]{2,3,1,0:T(8,128)S(1)} %copy.39, f32[2,2,512,512]{2,3,1,0:T(8,128)} %copy.38, f32[2,2,64,512]{2,3,1,0:T(8,128)S(1)} %copy.37, f32[2,2,640,64]{2,3,1,0:T(8,128)} %collective-permute-done.3), kind=kLoop, calls=%fused_computation.93 | loop fusion | flops 6553600 | bytes 13107200 | tf_op jit(solution)/shard_map/concatenate | solution.py:28
  57.5 3.2 %broadcast_in_dim.3.clone = f32[2,2,640,640]{3,2,1,0:T(8,128)} broadcast(f32[]{:T(128)} %constant.192.clone.1), dimensions={} | broadcast | bytes 6553604 | tf_op jit(solution)/shard_map/broadcast_in_dim | solution.py:129
  60.7 59.7 %while.18 = (s32[]{:T(128)}, f32[2,2,640,640]{3,2,1,0:T(8,128)}, s32[]{:T(128)}, s32[]{:T(128)}, s32[3,2]{1,0:T(4,128)S(1)}, /*index=5*/s32[2]{0:T(128)S(1)}, f3...) while((s32[]{:T(128)}, f32[2,2,640,640]{3,2,1,0:T(8,128)}, ...), condition=%wide.region_1.2_spmd, body=%wide.region_0.1_spmd.sunk | while | flops 1618804736 | bytes 35652036 | solution.py:164
  63.8 1.4 subtract_convert_fusion.5
  65.2 0.6 convolution_bitcast_fusion.18
  65.9 1.0 fusion.138
  67.5 1.3 subtract_convert_fusion.6
  69.4 1.1 fusion.139
  71.2 1.3 add_convert_fusion.5
  72.5 0.6 convolution_bitcast_fusion.22
  73.1 1.0 fusion.140
  74.8 1.1 multiply_add_fusion.3
  75.9 1.0 maximum_bitcast_fusion.13
  76.9 1.6 constant_dynamic-slice_fusion.3
  78.8 1.3 maximum_add_fusion.2
  80.5 7.6 %dynamic_update_slice.9 = f32[2,2,640,640]{3,2,1,0:T(8,128)} dynamic-update-slice(f32[2,2,640,640]{3,2,1,0:T(8,128)} %get-tuple-element.557, f32[2,2,256,256]{3,2,1,0:T(8,128)S(1)} %copy.87, s32[]{:T(128)} %constant.191.clone.1..sunk, s32[]{:T(128)} %constant.191.clone.1..sunk, s32[]{:T(128)S(6)} %select_n.134, s32[]{:T(128)S(6)} %select_n.135) | dynamic-update-slice | bytes 2097156 | tf_op jit(solution)/shard_map/while/body/dynamic_update_slice | solution.py:136
  91.4 1.5 subtract_convert_fusion.5
  93.5 1.0 fusion.138
  95.2 1.3 subtract_convert_fusion.6
  97.2 1.1 fusion.139
  98.9 1.4 add_convert_fusion.5
  100.9 1.0 fusion.140
  102.6 1.1 multiply_add_fusion.3
  103.7 1.0 maximum_bitcast_fusion.13
  104.7 1.8 constant_dynamic-slice_fusion.3
  106.8 1.3 maximum_add_fusion.2
  108.5 11.8 %dynamic_update_slice.9 = f32[2,2,640,640]{3,2,1,0:T(8,128)} dynamic-update-slice(f32[2,2,640,640]{3,2,1,0:T(8,128)} %get-tuple-element.557, f32[2,2,256,256]{3,2,1,0:T(8,128)S(1)} %copy.87, s32[]{:T(128)} %constant.191.clone.1..sunk, s32[]{:T(128)} %constant.191.clone.1..sunk, s32[]{:T(128)S(6)} %select_n.134, s32[]{:T(128)S(6)} %select_n.135) | dynamic-update-slice | bytes 2097156 | tf_op jit(solution)/shard_map/while/body/dynamic_update_slice | solution.py:136
  120.4 1.4 fusion.85
  121.7 8.6 %collective-permute-start.6 = (f32[4,64,640]{2,1,0:T(8,128)S(1)}, f32[4,64,640]{2,1,0:T(8,128)S(1)}, u32[]{:S(2)}, u32[]{:S(2)}) collective-permute-start(f32[4,64,640]{2,1,0:T(8,128)S(1)} %get-tuple-element.396), channel_id=1, source_target_pairs={{0,8},{8,16},{16,24},{1,9},{9,17},{17,25},{2,10},{10,18},{18,26},{... | collective-permute-start | bytes 1966088 | tf_op jit(solution)/shard_map/ppermute | solution.py:16
  130.3 1.3 collective-permute-start.7
  131.6 2.8 %slice.368 = f32[4,512,640]{2,1,0:T(8,128)S(1)} slice(f32[4,640,640]{2,1,0:T(8,128)} %bitcast.392), slice={[0:4], [64:576], [0:640]} | slice | bytes 10485760 | tf_op jit(solution)/shard_map/slice | solution.py:107
  134.5 10.7 %collective-permute-done.6 = f32[4,64,640]{2,1,0:T(8,128)S(1)} collective-permute-done((f32[4,64,640]{2,1,0:T(8,128)S(1)}, f32[4,64,640]{2,1,0:T(8,128)S(1)}, u32[]{:S(2)}, u32[]{:S(2)}) %collective-permute-start.6) | collective-permute-done | bytes 655392 | tf_op jit(solution)/shard_map/ppermute | solution.py:16
  145.1 1.2 fusion.72
  146.3 13.1 %collective-permute-done.7 = f32[4,64,640]{2,1,0:T(8,128)S(1)} collective-permute-done((f32[4,64,640]{2,1,0:T(8,128)S(1)}, f32[4,64,640]{2,1,0:T(8,128)S(1)}, u32[]{:S(2)}, u32[]{:S(2)}) %collective-permute-start.7) | collective-permute-done | bytes 655392 | tf_op jit(solution)/shard_map/ppermute | solution.py:16
  159.6 2.3 copy-done
  162.3 1.1 copy.44
  163.4 3.0 %collective-permute-start.8 = (f32[4,512,64]{1,2,0:T(8,128)}, f32[4,512,64]{1,2,0:T(8,128)}, u32[]{:S(2)}, u32[]{:S(2)}) collective-permute-start(f32[4,512,64]{1,2,0:T(8,128)} %copy.44), channel_id=1, source_target_pairs={{0,4},{1,5},{2,6},{3,7},{8,12},{9,13},{10,14},{11,15},{16,20},{17,... | collective-permute-start | bytes 1572872 | tf_op jit(solution)/shard_map/ppermute | solution.py:16
  166.7 1.3 collective-permute-start.9
  168.0 5.7 %slice.373 = f32[4,512,512]{2,1,0:T(8,128)} slice(f32[4,512,640]{2,1,0:T(8,128)} %copy-done), slice={[0:4], [0:512], [64:576]} | slice | bytes 8388608 | tf_op jit(solution)/shard_map/slice | solution.py:115
  173.7 1.4 copy.45
  175.1 1.6 slice_add_fusion.1
  176.6 5.8 %scatter-add.16 = f32[4,512,512]{2,1,0:T(8,128)} dynamic-update-slice(f32[4,512,512]{2,1,0:T(8,128)} %slice.373, f32[4,512,64]{2,1,0:T(8,128)S(1)} %slice_add_fusion.1, s32[]{:T(128)} %constant.191.clone.1, s32[]{:T(128)} %constant.191.clone.1, s32[]{:T(128)} %constant.191.clone.1) | dynamic-update-slice | bytes 1048580 | tf_op jit(solution)/shard_map/scatter-add | solution.py:116
  182.8 1.6 slice_add_fusion
  184.3 5.8 %scatter-add.19 = f32[4,512,512]{2,1,0:T(8,128)} dynamic-update-slice(f32[4,512,512]{2,1,0:T(8,128)} %scatter-add.16, f32[4,512,64]{2,1,0:T(8,128)S(1)} %slice_add_fusion, s32[]{:T(128)} %constant.191.clone.1, s32[]{:T(128)} %constant.191.clone.1, s32[]{:T(128)} %constant.199.clone.1) | dynamic-update-slice | bytes 1048580 | tf_op jit(solution)/shard_map/scatter-add | solution.py:117
  190.2 77.3 %reduce-scatter.2.cloned.1.call-done = f32[4,128,512]{2,1,0:T(8,128)} async-done(((f32[4,512,512]{2,1,0:T(8,128)}), f32[4,128,512]{2,1,0:T(8,128)}) %reduce-scatter.2.cloned.1.call-update) | async-done | bytes 1048592 | tf_op jit(solution)/shard_map/reduce_scatter | solution.py:168
  (45 shorter events, 11.2 us)
Async XLA Ops:
  6.5 261.0 %reduce-scatter.2.cloned.1.call-start = ((), (), s32[]{:S(2)}) async-start(), calls=%async_computation.1 | async-start | bytes 5242880 | tf_op jit(solution)/shard_map/reduce_scatter | solution.py:168
  7.8 21.9 %collective-permute-start.1 = (f32[2,2,64,512]{3,2,1,0:T(8,128)S(1)}, f32[2,2,64,512]{3,2,1,0:T(8,128)S(1)}, u32[]{:S(2)}, u32[]{:S(2)}) collective-permute-start(f32[2,2,64,512]{3,2,1,0:T(8,128)S(1)} %get-tuple-element.401), channel_id=1, source_target_pairs={{0,8},{8,16},{16,24},{1,9},{9,17},{17,25},{2,10},{10,18},{18,26},{... | collective-permute-start | bytes 1572872 | tf_op jit(solution)/shard_map/ppermute | solution.py:26
  12.7 24.3 %collective-permute-start.2 = (f32[2,2,64,512]{3,2,1,0:T(8,128)S(1)}, f32[2,2,64,512]{3,2,1,0:T(8,128)S(1)}, u32[]{:S(2)}, u32[]{:S(2)}) collective-permute-start(f32[2,2,64,512]{3,2,1,0:T(8,128)S(1)} %get-tuple-element.402), channel_id=1, source_target_pairs={{8,0},{16,8},{24,16},{9,1},{17,9},{25,17},{10,2},{18,10},{26,18},{... | collective-permute-start | bytes 1572872 | tf_op jit(solution)/shard_map/ppermute | solution.py:27
  15.6 34.5 %collective-permute-start = (f32[3]{0:T(128)S(1)}, f32[3]{0:T(128)S(1)}, u32[]{:S(2)}, u32[]{:S(2)}) collective-permute-start(f32[3]{0:T(128)S(1)} %add_convert_fusion.3), channel_id=1, source_target_pairs={{0,2},{1,3},{2,0},{3,1},{4,6},{5,7},{6,4},{7,5},{8,10},{9,11},{10,... | collective-permute-start | bytes 44 | tf_op jit(solution)/shard_map/ppermute | solution.py:35
  19.9 37.6 %collective-permute-start.5 = (f32[256,256]{1,0:T(8,128)}, f32[256,256]{1,0:T(8,128)}, u32[]{:S(2)}, u32[]{:S(2)}) collective-permute-start(f32[256,256]{1,0:T(8,128)} %dynamic-slice_bitcast_fusion.4), channel_id=1, source_target_pairs={{0,2},{1,3},{2,0},{3,1},{4,6},{5,7},{6,4},{7,5},{8,10},{9,11},{10,... | collective-permute-start | bytes 786440 | tf_op jit(solution)/shard_map/ppermute | solution.py:35
  25.5 18.9 %copy-start.3 = (s32[1,1,1,3,2]{3,4,2,1,0:T(2,128)S(1)}, s32[1,1,1,3,2]{3,4,2,1,0:T(2,128)}, u32[]{:S(2)}) copy-start(s32[1,1,1,3,2]{3,4,2,1,0:T(2,128)} %param.20) | copy-start | bytes 76
  37.4 6.2 %copy-start.1 = (bf16[256,1,256]{2,0,1:T(8,128)(2,1)S(1)}, bf16[256,1,256]{2,0,1:T(8,128)(2,1)}, u32[]{:S(2)}) copy-start(bf16[256,1,256]{2,0,1:T(8,128)(2,1)} %multiply_convert_fusion.1) | copy-start | bytes 393220
  37.4 6.2 %copy-start.2 = (bf16[256,1,256]{2,0,1:T(8,128)(2,1)S(1)}, bf16[256,1,256]{2,0,1:T(8,128)(2,1)}, u32[]{:S(2)}) copy-start(bf16[256,1,256]{2,0,1:T(8,128)(2,1)} %negate_convert_fusion) | copy-start | bytes 393220
  40.2 11.3 %collective-permute-start.3 = (f32[2,2,640,64]{2,3,1,0:T(8,128)}, f32[2,2,640,64]{2,3,1,0:T(8,128)}, u32[]{:S(2)}, u32[]{:S(2)}) collective-permute-start(f32[2,2,640,64]{2,3,1,0:T(8,128)} %get-tuple-element.397), channel_id=1, source_target_pairs={{0,4},{1,5},{2,6},{3,7},{8,12},{9,13},{10,14},{11,15},{16,20},{17,... | collective-permute-start | bytes 1966088 | tf_op jit(solution)/shard_map/ppermute | solution.py:26
  42.3 9.2 %collective-permute-start.4 = (f32[2,2,640,64]{2,3,1,0:T(8,128)}, f32[2,2,640,64]{2,3,1,0:T(8,128)}, u32[]{:S(2)}, u32[]{:S(2)}) collective-permute-start(f32[2,2,640,64]{2,3,1,0:T(8,128)} %get-tuple-element.398), channel_id=1, source_target_pairs={{4,0},{5,1},{6,2},{7,3},{12,8},{13,9},{14,10},{15,11},{20,16},{21,... | collective-permute-start | bytes 1966088 | tf_op jit(solution)/shard_map/ppermute | solution.py:27
  121.7 23.4 %collective-permute-start.6 = (f32[4,64,640]{2,1,0:T(8,128)S(1)}, f32[4,64,640]{2,1,0:T(8,128)S(1)}, u32[]{:S(2)}, u32[]{:S(2)}) collective-permute-start(f32[4,64,640]{2,1,0:T(8,128)S(1)} %get-tuple-element.396), channel_id=1, source_target_pairs={{0,8},{8,16},{16,24},{1,9},{9,17},{17,25},{2,10},{10,18},{18,26},{... | collective-permute-start | bytes 1966088 | tf_op jit(solution)/shard_map/ppermute | solution.py:16
  130.3 29.1 %collective-permute-start.7 = (f32[4,64,640]{2,1,0:T(8,128)S(1)}, f32[4,64,640]{2,1,0:T(8,128)S(1)}, u32[]{:S(2)}, u32[]{:S(2)}) collective-permute-start(f32[4,64,640]{2,1,0:T(8,128)S(1)} %get-tuple-element.395), channel_id=1, source_target_pairs={{8,0},{16,8},{24,16},{9,1},{17,9},{25,17},{10,2},{18,10},{26,18},{... | collective-permute-start | bytes 1966088 | tf_op jit(solution)/shard_map/ppermute | solution.py:16
  159.6 2.3 copy-start
  163.4 10.3 %collective-permute-start.8 = (f32[4,512,64]{1,2,0:T(8,128)}, f32[4,512,64]{1,2,0:T(8,128)}, u32[]{:S(2)}, u32[]{:S(2)}) collective-permute-start(f32[4,512,64]{1,2,0:T(8,128)} %copy.44), channel_id=1, source_target_pairs={{0,4},{1,5},{2,6},{3,7},{8,12},{9,13},{10,14},{11,15},{16,20},{17,... | collective-permute-start | bytes 1572872 | tf_op jit(solution)/shard_map/ppermute | solution.py:16
  166.7 15.7 %collective-permute-start.9 = (f32[4,512,64]{1,2,0:T(8,128)S(1)}, f32[4,512,64]{1,2,0:T(8,128)S(1)}, u32[]{:S(2)}, u32[]{:S(2)}) collective-permute-start(f32[4,512,64]{1,2,0:T(8,128)S(1)} %copy.46), channel_id=1, source_target_pairs={{4,0},{5,1},{6,2},{7,3},{12,8},{13,9},{14,10},{15,11},{20,16},{21,... | collective-permute-start | bytes 1572872 | tf_op jit(solution)/shard_map/ppermute | solution.py:16
Sparse Core Ops, SparseCore 0:
  190.3 77.1 reduce-scatter.1
where the time goes:
time: 276 us; the launch traced here: 274 us
  waiting for transfers between devices  108 us (39%)
  local copies, waits for them, and re-layouts  70.9 us (26%)
  other arithmetic  40.8 us (15%)
  starting transfers between devices  26.7 us (10%)
  between operations  15 us (5%)
  matrix products  7.58 us (3%)
  loops' own time  5.34 us (2%)
    reduce_scatter x1, waiting for transfers between devices, shards(): summed = lax.psum_scatter(operand, 'scan', scatter_dimension=1, tiled=True)  77.3 us
    ppermute x4, waiting for transfers between devices, from_behind(): return lax.ppermute(block, axis, route)  23.8 us
    dynamic_update_slice x4, local copies, waits for them, and re-layouts, add_patch(): return lax.dynamic_update_slice(current, present + update, starts)  20.1 us
    another operation x13, other arithmetic  16.6 us
    ppermute x4, starting transfers between devices, from_behind(): return lax.ppermute(block, axis, route)  14.2 us
    unnamed x9, local copies, waits for them, and re-layouts  7.58 us
    dot_general x12, matrix products, transform(): jnp.einsum('pab,pbqc->qac', middle, right_table, preferred_element_type=j...  7.58 us
    ppermute x2, starting transfers between devices, extended_2(): before = lax.ppermute(last, axis, up)  7.01 us
  transfers between devices with their start and end apart: 11, of which 4 were waited for; matrix products, arithmetic and copies ran while one was open for 17% of the time, Pallas kernels for 0%

commit v1 on v0

v1 whole, which is shorter than its diff:
```python
import functools
import math

import jax
import jax.numpy as jnp
import numpy as np
from jax import lax
from jax.experimental import pallas as pl
from jax.experimental.pallas import tpu as pltpu
from jax.sharding import PartitionSpec as P

PATCH = 256
HALO = 64
PMAX = 3
LANE = 128
VMEM_LIMIT = 32 * 1024 * 1024
VMEM_LITTLE = 8 * 1024 * 1024
NOTE_ROWS = 8


def block_tables():
    line = np.arange(PATCH)
    angles = (line[:, None] * line[None, :] % PATCH) * (2.0 * math.pi / PATCH)
    cosines = np.cos(angles) / math.sqrt(PATCH)
    sines = np.sin(angles) / math.sqrt(PATCH)
    turn = np.block([[cosines, sines], [-sines, cosines]])
    back = np.block([[cosines, -sines], [sines, cosines]])
    return (jnp.asarray(turn.astype(np.float32)).astype(jnp.bfloat16), jnp.asarray(back.astype(np.float32)).astype(jnp.bfloat16))


def pair_of(index, phase):
    return index + 1 if index % 2 == phase else index - 1


def pairings(size):
    return range(1 if size <= 2 else 2)


def joint_permute(value, names, targets):
    sizes = [lax.axis_size(name) for name in names]
    route = []
    for flat in range(math.prod(sizes)):
        place = np.unravel_index(flat, sizes)
        goal = targets(*[int(i) for i in place])
        if goal is None or any(not 0 <= g < s for g, s in zip(goal, sizes)):
            continue
        route.append((flat, int(np.ravel_multi_index(goal, sizes))))
    return lax.ppermute(value, tuple(names) if len(names) > 1 else names[0], route)


OUTER = -1


def transform(pairs, left, right):
    stacked = jnp.concatenate(
        [jnp.concatenate([pair[part] for pair in pairs], axis=1) for part in range(2)], axis=0
    )
    middle = jnp.dot(left[...], stacked, preferred_element_type=jnp.float32).astype(jnp.bfloat16)
    size = PATCH
    middle = jnp.concatenate(
        [
            jnp.concatenate(
                [middle[p * size : (p + 1) * size, i * size : (i + 1) * size] for p in range(2)],
                axis=1,
            )
            for i in range(len(pairs))
        ],
        axis=0,
    )
    result = jnp.dot(middle, right[...], preferred_element_type=jnp.float32)
    return [
        (
            result[i * size : (i + 1) * size, :size],
            result[i * size : (i + 1) * size, size:],
        )
        for i in range(len(pairs))
    ]


def rounded(pair):
    return pair[0].astype(jnp.bfloat16), pair[1].astype(jnp.bfloat16)


def product(a, b):
    return a[0] * b[0] - a[1] * b[1], a[0] * b[1] + a[1] * b[0]


def conj_product(a, b):
    return a[0] * b[0] + a[1] * b[1], a[0] * b[1] - a[1] * b[0]


def lanes():
    return lax.broadcasted_iota(jnp.int32, (PATCH, LANE), 1)


def corner_of(row, col):
    return row + HALO, (col + LANE) // LANE, lax.rem(col + LANE, LANE)


def window(ext, slice_at, row, col):
    top, tile, shift = corner_of(row, col)
    turn = lax.rem(LANE - shift, LANE)
    inside = lanes() < LANE - shift

    def plane(index):
        moved = [
            pltpu.roll(ext[index, tile + j, pl.ds(top, PATCH), :], turn, 1) for j in range(3)
        ]
        return jnp.concatenate([jnp.where(inside, moved[j], moved[j + 1]) for j in range(2)], axis=1)

    return plane(2 * slice_at), plane(2 * slice_at + 1)


def deposit(acc, slice_at, row, col, pair):
    top, tile, shift = corner_of(row, col)
    inside = lanes() >= shift
    blank = jnp.zeros((PATCH, LANE), jnp.float32)
    for part in range(2):
        moved = [
            pltpu.roll(pair[part][:, j * LANE : (j + 1) * LANE], shift, 1) for j in range(2)
        ]
        moved = [blank, *moved, blank]
        for j in range(3):
            acc[2 * slice_at + part, tile + j, pl.ds(top, PATCH), :] += jnp.where(
                inside, moved[j + 1], moved[j]
            )


def forward(ext, corners, probe, wave, turn, back):
    lamp = (probe[0], probe[1])
    prop = (wave[0][...], wave[1][...])
    entrance = [rounded(product(lamp, window(ext, 0, *corner))) for corner in corners]
    spectra = transform(entrance, turn, back)
    arrived = transform([rounded(product(prop, x)) for x in spectra], back, turn)
    seconds = [window(ext, 1, *corner) for corner in corners]
    far = transform([rounded(product(o, w)) for o, w in zip(seconds, arrived)], turn, back)
    return far, arrived, seconds


def backward(far, arrived, seconds, intensities, probe, wave, turn, back, put):
    lamp = (probe[0], probe[1])
    prop = (wave[0][...], wave[1][...])
    residuals = []
    for psi, intensity in zip(far, intensities):
        misfit = psi[0] * psi[0] + psi[1] * psi[1] - intensity
        residuals.append(rounded((misfit * psi[0], misfit * psi[1])))
    back_seconds = transform(residuals, back, turn)
    for i, (w, g) in enumerate(zip(arrived, back_seconds)):
        put(i, 1, conj_product(w, g))
    through = [rounded(conj_product(o, g)) for o, g in zip(seconds, back_seconds)]
    spectra = transform(through, turn, back)
    back_firsts = transform([rounded(conj_product(prop, x)) for x in spectra], back, turn)
    for i, g in enumerate(back_firsts):
        put(i, 0, conj_product(lamp, g))


def place_of(height):
    shard_count = lax.axis_size("scan")
    scan_at = lax.axis_index("scan")
    band = height // shard_count
    upper = scan_at < shard_count // 2
    even = scan_at % 2 == 0
    open_at = jnp.where(upper, HALO, 0)
    shut_at = jnp.where(upper, 0, band - HALO)
    other_at = jnp.where(even, band, 0)
    return [
        jnp.where(upper, 0, height // 2),
        jnp.where(upper, height, -HALO),
        lax.axis_index("row") % 2,
        lax.axis_index("col") % 2,
        jnp.where(even, 0, band),
        other_at + open_at,
        other_at + shut_at,
        ((scan_at == 0) | (scan_at == shard_count - 1)).astype(jnp.int32),
        shut_at,
        open_at,
    ]


def wanted(place, row, half_rows):
    inner = (row < place[0] + half_rows) & (row + PATCH > place[0])
    outer = (row < place[1] + HALO) & (row + PATCH > place[1])
    return inner | outer


def far_tile(place, phase, tiles):
    return jnp.where(place[3] == phase, tiles - 1, 0)


class Copies:
    def __init__(self, sems):
        self.sems, self.all = sems, []

    def start(self, source, target):
        copy = pltpu.make_async_copy(source, target, self.sems.at[len(self.all)])
        copy.start()
        self.all.append(copy)
        return copy

    def wait(self):
        for copy in self.all:
            copy.wait()


def staging_kernel(sides, core, *refs):
    col_refs, refs = refs[:sides], refs[sides:]
    near, (ext, *near_to), sems = refs[:4], refs[4:-1], refs[-1]
    height, width = core.shape[1], core.shape[2]
    tiles = ext.shape[1]
    place = place_of(height)
    copies = Copies(sems)
    for t in range(width // LANE):
        part = core.at[:, :, pl.ds(t * LANE, LANE)]
        copies.start(part, ext.at[:, t + 1, pl.ds(HALO, height), :])
    for j, ref in enumerate(col_refs):
        copies.start(ref, ext.at[:, far_tile(place, j, tiles), pl.ds(HALO, height), :])
    for source, target in zip(near, near_to):
        copies.start(source, target)
    copies.wait()


def patches_kernel(sides, cuts, peer, *refs):
    row_refs, refs = refs[: sides[0]], refs[sides[0] :]
    corner_refs, refs = refs[: sides[0] * sides[1]], refs[sides[0] * sides[1] :]
    own_corners, own_count, ext, own, probe, cosine, sine, turn, back = refs[:9]
    outs, (acc, note, queue, sems) = refs[10:-4], refs[-4:]
    wave = (cosine, sine)
    tiles, height = ext.shape[1], ext.shape[2] - 2 * HALO
    half_rows = height // 2
    place = place_of(height)
    copies = Copies(sems)

    def far_row(phase):
        return pl.multiple_of(jnp.where(place[2] == phase, height + HALO, 0), 8)

    for i, ref in enumerate(row_refs):
        for t in range(tiles - 2):
            part = ref.at[:, :, pl.ds(t * LANE, LANE)]
            copies.start(part, ext.at[:, t + 1, pl.ds(far_row(i), HALO), :])
    for k, ref in enumerate(corner_refs):
        i, j = divmod(k, sides[1])
        copies.start(ref, ext.at[:, far_tile(place, j, tiles), pl.ds(far_row(i), HALO), :])
    note_at = pl.ds(PMAX * PATCH, NOTE_ROWS)
    copies.start(peer.at[note_at, pl.ds(0, LANE)], note)
    first = pl.multiple_of(place[0] + HALO, 8)
    outer = pl.multiple_of(place[1] + HALO, 8)
    acc[:, :, pl.ds(first, half_rows), :] = jnp.zeros((4, tiles, half_rows, LANE), jnp.float32)
    acc[:, :, pl.ds(outer, HALO), :] = jnp.zeros((4, tiles, HALO, LANE), jnp.float32)

    def intensity(index):
        mine = own[jnp.minimum(index, PMAX - 1)]
        start = pl.multiple_of(jnp.maximum(index - PMAX, 0) * PATCH, PATCH)
        return jnp.where(index < PMAX, mine, peer[pl.ds(start, PATCH), :])

    copies.wait()
    length = jnp.int32(0)
    for index in range(2 * PMAX):
        slot = index % PMAX
        if index < PMAX:
            row, col, count = own_corners[slot, 0], own_corners[slot, 1], own_count[0]
        else:
            row, col, count = [
                note[0, at].astype(jnp.int32) for at in (2 * slot, 2 * slot + 1, 2 * PMAX)
            ]
        queue[3 * length] = index
        queue[3 * length + 1] = row
        queue[3 * length + 2] = col
        length = length + ((slot < count) & wanted(place, row, half_rows)).astype(jnp.int32)

    def step(turn_at, carry):
        items = [2 * turn_at, jnp.minimum(2 * turn_at + 1, length - 1)]
        whole = 2 * turn_at + 1 < length
        corners = [(queue[3 * i + 1], queue[3 * i + 2]) for i in items]
        far, arrived, seconds = forward(ext, corners, probe, wave, turn, back)

        def put(i, slice_at, pair):
            if i == 0:
                deposit(acc, slice_at, *corners[i], pair)
            else:
                pl.when(whole)(lambda: deposit(acc, slice_at, *corners[i], pair))

        intensities = [intensity(queue[3 * i]) for i in items]
        backward(far, arrived, seconds, intensities, probe, wave, turn, back, put)
        return carry

    lax.fori_loop(0, (length + 1) // 2, step, 0)
    gifts = Copies(sems)
    for target, parts in zip(outs, cuts):
        row_to = 0
        for tile, at, count in parts:
            tile = far_tile(place, tile[0], tiles) if isinstance(tile, tuple) else tile
            row = outer if at == OUTER else first
            row = row if at in (OUTER, None) else pl.multiple_of(first + place[at], 8)
            gifts.start(
                acc.at[:, pl.ds(tile, target.shape[1]), pl.ds(row, count), :],
                target.at[:, :, pl.ds(row_to, count), :],
            )
            row_to += count
    gifts.wait()


def near_tile(place, phase, tiles):
    return jnp.where(place[3] == phase, tiles - 1, 0)


def add_rims(place, out, rims, rim_row):
    _, tiles, rows, _ = out.shape
    for j, rim in enumerate(rims):
        at = near_tile(place, j, tiles)
        out[:, at, :, :] += rim[:, 0, pl.ds(rim_row, rows), :]


def edge_kernel(height, sides, open_left, open_right, outer_left, outer_right, *refs):
    place = place_of(height)
    rims, (open_out, outer_out) = refs[:sides], refs[-2:]
    open_out[:, 0:1] = open_left[...]
    open_out[:, 1:2] = open_right[...]
    add_rims(place, open_out, rims, pl.multiple_of(place[5], 8))
    outer_out[:, 0:1] = outer_left[...]
    outer_out[:, 1:2] = outer_right[...]
    add_rims(place, outer_out, rims, height // 2)


def shut_inner_kernel(height, part, strip, out):
    place = place_of(height)
    out[...] = part[...]

    @pl.when(place[7] == 0)
    def _():
        out[...] += strip[...]


def shut_edge_kernel(height, sides, left, right, strip, *refs):
    place = place_of(height)
    rims, out = refs[:sides], refs[sides]
    out[:, 0:1] = left[...]
    out[:, 1:2] = right[...]
    add_rims(place, out, rims, pl.multiple_of(place[6], 8))

    @pl.when(place[7] == 0)
    def _():
        out[...] += strip[...]


def final_kernel(height, sides, part, *refs):
    place = place_of(height)
    open_got, shut_got, strip, rims = refs[:2], refs[2:4], refs[4:6], refs[6 : 6 + sides]
    out, work = refs[6 + sides :]
    work[...] = part[...]
    tiles = work.shape[1]
    add_rims(place, work, rims, pl.multiple_of(place[4], 8))

    def add(at, inner, edge):
        rows = pl.ds(pl.multiple_of(at, 8), inner.shape[2])
        work[:, 1 : tiles - 1, rows, :] += inner[...]
        work[:, 0:1, rows, :] += edge[:, 0:1]
        work[:, tiles - 1 : tiles, rows, :] += edge[:, 1:2]

    add(place[9], *open_got)
    add(place[8], *shut_got)

    @pl.when(place[7] == 1)
    def _():
        add(place[8], *strip)

    for t in range(tiles):
        out[:, :, t * LANE : (t + 1) * LANE] = work[:, t]


def half_kernel(height, sides, part, inner, edge, *refs):
    place = place_of(height)
    rims, out = refs[:sides], refs[sides]
    out[...] = part[...]
    add_rims(place, out, rims, 0)
    tiles = out.shape[1]
    rows = pl.ds(pl.multiple_of(jnp.where(place[0] == 0, 0, out.shape[2] - HALO), 8), HALO)
    out[:, 1 : tiles - 1, rows, :] += inner[...]
    out[:, 0:1, rows, :] += edge[:, 0:1]
    out[:, tiles - 1 : tiles, rows, :] += edge[:, 1:2]


def near_rows(place, phase, height):
    return pl.ds(pl.multiple_of(jnp.where(place[2] == phase, height - HALO, 0), HALO), HALO)


def near_cols(place, phase, width):
    return pl.ds(pl.multiple_of(jnp.where(place[3] == phase, width - LANE, 0), LANE), LANE)


def note_kernel(corners, count, own, out, sems):
    copies = Copies(sems)
    for slot in range(PMAX):
        copies.start(own.at[slot], out.at[pl.ds(slot * PATCH, PATCH), :])
    lane = lax.broadcasted_iota(jnp.int32, (NOTE_ROWS, PATCH), 1)
    values = jnp.where(lane == 2 * PMAX, count[0], 0)
    for index in range(2 * PMAX):
        values = jnp.where(lane == index, corners[index // 2, index % 2], values)
    out[PMAX * PATCH :, :] = values.astype(jnp.float32)
    copies.wait()


def columns_kernel(core, *refs):
    outs, copies = refs[:-1], Copies(refs[-1])
    place = place_of(core.shape[1])
    for j, out in enumerate(outs):
        copies.start(core.at[:, :, near_cols(place, j, core.shape[2])], out)
    copies.wait()


def rows_kernel(sides, core, *refs):
    outs, copies = refs[:-1], Copies(refs[-1])
    height, width = core.shape[1:]
    place = place_of(height)
    for i in range(sides[0]):
        rows = near_rows(place, i, height)
        copies.start(core.at[:, rows, :], outs[i])
        for j in range(sides[1]):
            target = outs[sides[0] + i * sides[1] + j]
            copies.start(core.at[:, rows, near_cols(place, j, width)], target)
    copies.wait()


ANY = pl.BlockSpec(memory_space=pl.ANY)
VMEM = pl.BlockSpec(memory_space=pltpu.VMEM)
SMEM = pl.BlockSpec(memory_space=pltpu.SMEM)


def block(*shape):
    return jax.ShapeDtypeStruct(shape, jnp.float32)


def call(kernel, out_shapes, in_specs, out_specs, scratch, *operands, limit=VMEM_LIMIT, aliases=None):
    return pl.pallas_call(
        kernel,
        out_shape=out_shapes,
        in_specs=in_specs,
        out_specs=out_specs,
        scratch_shapes=scratch,
        input_output_aliases=aliases or {},
        compiler_params=pltpu.CompilerParams(vmem_limit_bytes=limit),
        cost_estimate=pl.CostEstimate(flops=0, bytes_accessed=0, transcendentals=0),
    )(*operands)


def shards(object_field, probe_field, prop_phase, measured, positions, counts):
    height, width = object_field.shape[2:]
    shard_count = lax.axis_size("scan")
    half_rows = height // 2
    band = height // shard_count
    rest = band - HALO
    tiles = width // LANE
    row_sides = pairings(lax.axis_size("row"))
    col_sides = pairings(lax.axis_size("col"))
    sides = len(col_sides)
    both = (len(row_sides), sides)
    stride = shard_count // 2
    scan_at = lax.axis_index("scan")
    planes = object_field.reshape(4, height, width)
    own = measured.reshape(PMAX, PATCH, PATCH)
    own_corners, own_count = positions.reshape(PMAX, 2), counts.reshape(1)

    def across(value):
        return lax.ppermute(value, "scan", [(i, i ^ stride) for i in range(shard_count)])

    def to_cols(value, j):
        return joint_permute(value, ("col",), lambda c: (pair_of(c, j),))

    def to_rows(value, i):
        return joint_permute(value, ("row",), lambda r: (pair_of(r, i),))

    def to_corner(value, i, j):
        return joint_permute(value, ("row", "col"), lambda r, c: (pair_of(r, i), pair_of(c, j)))

    def cut_edges(kernel, shapes):
        return call(
            kernel,
            shapes,
            [ANY],
            [VMEM] * len(shapes),
            [pltpu.SemaphoreType.DMA((len(shapes),))],
            planes,
            limit=VMEM_LITTLE,
        )

    noted = call(
        note_kernel,
        block(PMAX * PATCH + NOTE_ROWS, PATCH),
        [SMEM, SMEM, ANY],
        VMEM,
        [pltpu.SemaphoreType.DMA((PMAX,))],
        own_corners,
        own_count,
        own,
        limit=VMEM_LITTLE,
    )
    peer = across(noted)
    row_edges = cut_edges(
        functools.partial(rows_kernel, both),
        [block(4, HALO, width)] * both[0] + [block(4, HALO, LANE)] * (both[0] * sides),
    )
    row_halos = [to_rows(row_edges[i], i) for i in row_sides]
    col_edges = cut_edges(columns_kernel, [block(4, height, LANE)] * sides)
    col_halos = [to_cols(edge, j) for j, edge in zip(col_sides, col_edges)]
    corner_halos = [
        to_corner(row_edges[both[0] + i * sides + j], i, j) for i in row_sides for j in col_sides
    ]
    cosine, sine = jnp.cos(prop_phase), jnp.sin(prop_phase)
    turn, back = block_tables()

    two_bands = shard_count == 4 and rest > 0
    inner = tiles - 2
    cuts = [(inner, [(2, OUTER, HALO)]), (1, [(1, OUTER, HALO)]), (1, [(tiles, OUTER, HALO)])]
    cuts += [(1, [((j,), None, half_rows), ((j,), OUTER, HALO)]) for j in col_sides]
    if two_bands:
        for at, rows in ((5, rest), (6, HALO)):
            cuts += [(inner, [(2, at, rows)]), (1, [(1, at, rows)]), (1, [(tiles, at, rows)])]
        cuts += [(tiles, [(1, 4, band)])]
    else:
        cuts += [(tiles, [(1, None, half_rows)]), (1, [(1, None, HALO)]), (1, [(1, None, HALO)])]
    full = (4, tiles + 2, height + 2 * HALO, LANE)
    table = jax.ShapeDtypeStruct(turn.shape, turn.dtype)
    staged = call(
        functools.partial(staging_kernel, sides),
        [block(*full), block(*own.shape), block(*probe_field.shape), table, table],
        [ANY] * (sides + 5),
        [VMEM] * 5,
        [pltpu.SemaphoreType.DMA((tiles + sides + 4,))],
        planes,
        *col_halos,
        own,
        probe_field,
        turn,
        back,
        limit=VMEM_LITTLE,
    )
    ext, own, lamp, turn, back = staged
    arrivals = [peer, *row_halos, *corner_halos]
    copy_count = max(
        (tiles + sides) * both[0] + 1, sum(len(parts) for _, parts in cuts)
    )
    outs = call(
        functools.partial(patches_kernel, both, [parts for _, parts in cuts]),
        [block(*full)] + [block(4, wide, sum(part[2] for part in parts), LANE) for wide, parts in cuts],
        [VMEM] + [ANY] * (len(arrivals) - 1) + [SMEM, SMEM] + [VMEM] * 7,
        [VMEM] + [ANY] * len(cuts),
        [
            pltpu.VMEM(full, jnp.float32),
            pltpu.SMEM((NOTE_ROWS, LANE), jnp.float32),
            pltpu.SMEM((3 * (2 * PMAX + 1),), jnp.int32),
            pltpu.SemaphoreType.DMA((copy_count,)),
        ],
        *arrivals,
        own_corners,
        own_count,
        ext,
        own,
        lamp,
        cosine,
        sine,
        turn,
        back,
        aliases={len(arrivals) + 2: 0},
    )[1:]
    outer_inner, outer_left, outer_right = outs[:3]
    rims, pieces = outs[3 : 3 + sides], outs[3 + sides :]

    def to_next(value):
        return joint_permute(
            value, ("row", "scan"), lambda r, s: (r + 1 if s < stride else r - 1, s)
        )

    def beside(value, mask=1):
        return lax.ppermute(value, "scan", [(i, i ^ mask) for i in range(shard_count)])

    def fold(kernel, out_shapes, *operands, scratch=()):
        many = isinstance(out_shapes, tuple)
        return call(
            functools.partial(kernel, height),
            out_shapes,
            [VMEM] * len(operands),
            (VMEM,) * len(out_shapes) if many else VMEM,
            list(scratch),
            *operands,
            limit=VMEM_LITTLE,
        )

    got_rims = [to_cols(rim, j) for j, rim in zip(col_sides, rims)]
    got_inner = to_next(outer_inner)
    open_edge, outer_edge = fold(
        lambda *refs: edge_kernel(refs[0], sides, *refs[1:]),
        (block(4, 2, pieces[1].shape[2], LANE), block(4, 2, HALO, LANE)),
        pieces[1],
        pieces[2],
        outer_left,
        outer_right,
        *got_rims,
    )
    got_edge = to_next(outer_edge)
    if not two_bands:
        half = fold(
            lambda *refs: half_kernel(refs[0], sides, *refs[1:]),
            block(4, tiles, half_rows, LANE),
            pieces[0],
            got_inner,
            got_edge,
            *got_rims,
        )
        mask = stride // 2
        while mask > 0:
            size = half.shape[2] // 2
            low = (scan_at & mask) == 0
            keep = lax.dynamic_slice_in_dim(half, jnp.where(low, 0, size), size, axis=2)
            send = lax.dynamic_slice_in_dim(half, jnp.where(low, size, 0), size, axis=2)
            half = keep + beside(send, mask)
            mask //= 2
        return half.transpose(0, 2, 1, 3).reshape(2, 2, band, width)
    got_open = [beside(pieces[0]), beside(open_edge)]
    got_inner, *got_open = lax.optimization_barrier((got_inner, *got_open))
    shut_inner = fold(shut_inner_kernel, block(4, inner, HALO, LANE), pieces[3], got_inner)
    got_shut = [beside(shut_inner)]
    shut_edge = fold(
        lambda *refs: shut_edge_kernel(refs[0], sides, *refs[1:]),
        block(4, 2, HALO, LANE),
        pieces[4],
        pieces[5],
        got_edge,
        *got_rims,
    )
    got_shut.append(beside(shut_edge))
    total = fold(
        lambda *refs: final_kernel(refs[0], sides, *refs[1:]),
        block(4, band, width),
        pieces[6],
        *got_open,
        *got_shut,
        got_inner,
        got_edge,
        *got_rims,
        scratch=[pltpu.VMEM((4, tiles, band, LANE), jnp.float32)],
    )
    return total.reshape(2, 2, band, width)


def solution(mesh):
    placed = (
        P(None, None, "row", "col"),
        P(),
        P(),
        P("row", "col", "scan", None, None, None),
        P("row", "col", "scan", None, None),
        P("row", "col", "scan"),
    )
    return jax.shard_map(
        shards,
        mesh=mesh,
        in_specs=placed,
        out_specs=P(None, None, ("row", "scan"), "col"),
        check_vma=False,
    )
```

time: 276 us -> 91 us (0.33)
  waiting for transfers between devices: 108 us -> 41.7 us
  local copies, waits for them, and re-layouts: 70.9 us -> 10.2 us
  other arithmetic: 40.8 us -> 0 us
  Pallas kernels: 0 us -> 16.3 us
  between operations: 15 us -> 0.81 us
  matrix products: 7.58 us -> 0 us
  loops' own time: 5.34 us -> 0 us
  starting transfers between devices: 26.7 us -> 21.5 us
    reduce_scatter x1 -> x0, waiting for transfers between devices: 77.3 us -> none  [shards(): summed = lax.psum_scatter(operand, 'scan', scatter_dimension=1, tiled=True)]
    another operation x17 -> x0, other arithmetic: 20.5 us -> none
    dynamic_update_slice x4 -> x0, local copies, waits for them, and re-layouts: 20.1 us -> none  [add_patch(): return lax.dynamic_update_slice(current, present + update, starts)]
    pallas_call x0 -> x9, Pallas kernels: none -> 16.3 us  [call(): pl.pallas_call(kernel, out_shape=out_shapes, in_specs=in_specs, out_specs...]
    slice x10 -> x0, local copies, waits for them, and re-layouts: 14.8 us -> none  [the longest x1 5.67 us: fold_cols(): core_cols = gradient[:, :, HALO:tile_size + HALO]]
    scatter-add x2 -> x0, local copies, waits for them, and re-layouts: 11.6 us -> none  [the longest x1 5.82 us: fold_cols(): return core_cols.at[:, :, tile_size - HALO:].add(pass_cols(left_rim, -1))]
    ppermute x10 -> x13, waiting for transfers between devices: 30.7 us -> 41.7 us  [the longest x4 18.5 us: beside(): lax.ppermute(value, 'scan', [(i, i ^ mask) for i in range(shard_count)])]
    add x6 -> x0, other arithmetic: 8 us -> none  [the longest x2 2.67 us: add_patch(): return lax.dynamic_update_slice(current, present + update, starts)]
  transfers between devices with their start and end apart: 11 -> 13, of which waited for: 4 -> 7; matrix products, arithmetic and copies ran while one was open for 17% -> 3% of each run, Pallas kernels for 0% -> 2%
where the time goes in v1:
time: 91 us; the launch traced here: 90.5 us
  waiting for transfers between devices  41.7 us (46%)
  starting transfers between devices  21.5 us (24%)
  Pallas kernels  16.3 us (18%)
  local copies, waits for them, and re-layouts  10.2 us (11%)
    ppermute x4, waiting for transfers between devices, beside(): lax.ppermute(value, 'scan', [(i, i ^ mask) for i in range(shard_count)])  18.5 us
    ppermute x8, waiting for transfers between devices, joint_permute(): lax.ppermute(value, tuple(names) if len(names) > 1 else names[0], route)  17.4 us
    pallas_call x9, Pallas kernels, call(): pl.pallas_call(kernel, out_shape=out_shapes, in_specs=in_specs, out_specs...  16.3 us
    ppermute x8, starting transfers between devices, joint_permute(): lax.ppermute(value, tuple(names) if len(names) > 1 else names[0], route)  13.4 us
    unnamed x16, local copies, waits for them, and re-layouts  7.6 us
    ppermute x1, waiting for transfers between devices, across(): lax.ppermute(value, 'scan', [(i, i ^ stride) for i in range(shard_count)])  5.76 us
    ppermute x4, starting transfers between devices, beside(): lax.ppermute(value, 'scan', [(i, i ^ mask) for i in range(shard_count)])  4.35 us
    ppermute x1, starting transfers between devices, across(): lax.ppermute(value, 'scan', [(i, i ^ stride) for i in range(shard_count)])  3.8 us
  transfers between devices with their start and end apart: 13, of which 7 were waited for; matrix products, arithmetic and copies ran while one was open for 3% of the time, Pallas kernels for 2%

profile of v1, /device:TPU:0, one launch (start us, length us, event | category | flops | bytes accessed | tf_op | source)
XLA Modules:
  0.0 90.5 jit_solution(14771154989110164793)
XLA Ops:
  0.0 0.0 copy-start
  0.0 2.2 %copy-done = f32[2,2,512,512]{3,2,1,0:T(8,128)S(1)} copy-done((f32[2,2,512,512]{3,2,1,0:T(8,128)S(1)}, f32[2,2,512,512]{3,2,1,0:T(8,128)}, u32[]{:S(2)}) %copy-start) | copy-done | bytes 4194328
  2.2 0.0 copy-start.4
  2.2 0.0 copy-start.5
  2.2 0.1 shard_map.84
  2.3 0.5 collective-permute-start.5
  3.5 0.8 copy.10.corners.refs_4_
  4.3 0.0 copy-start.3
  4.3 1.1 %copy-done.3 = f32[1,1,1,3,256,256]{5,4,3,2,1,0:T(8,128)S(1)} copy-done((f32[1,1,1,3,256,256]{5,4,3,2,1,0:T(8,128)S(1)}, f32[1,1,1,3,256,256]{5,4,3,2,1,0:T(8,128)}, u32[]{:S(2)}) %copy-start.3) | copy-done | bytes 786456
  5.4 0.7 shard_map.82
  6.1 3.8 %collective-permute-start = (f32[776,256]{1,0:T(8,128)S(1)}, f32[776,256]{1,0:T(8,128)S(1)}, u32[]{:S(2)}, u32[]{:S(2)}) collective-permute-start(f32[776,256]{1,0:T(8,128)S(1)} %shard_map.82), channel_id=1, source_target_pairs={{0,2},{1,3},{2,0},{3,1},{4,6},{5,7},{6,4},{7,5},{8,10},{9,11},{10,... | collective-permute-start | bytes 2383880 | tf_op jit(solution)/shard_map/ppermute | solution.py:463
  9.9 0.0 copy-start.1
  9.9 2.2 %copy-done.1 = f32[2,2,512,512]{3,2,1,0:T(8,128)S(1)} copy-done((f32[2,2,512,512]{3,2,1,0:T(8,128)S(1)}, f32[2,2,512,512]{3,2,1,0:T(8,128)}, u32[]{:S(2)}) %copy-start.1) | copy-done | bytes 4194328
  12.1 0.0 copy-start.2
  12.1 0.2 shard_map.83
  12.2 1.6 %collective-permute-start.1 = (f32[4,64,512]{2,1,0:T(8,128)S(1)}, f32[4,64,512]{2,1,0:T(8,128)S(1)}, u32[]{:S(2)}, u32[]{:S(2)}) collective-permute-start(f32[4,64,512]{2,1,0:T(8,128)S(1)} %get-tuple-element.30), channel_id=1, source_target_pairs={{0,8},{8,0},{16,24},{24,16},{1,9},{9,1},{17,25},{25,17},{2,10},{10... | collective-permute-start | bytes 1572872 | tf_op jit(solution)/shard_map/ppermute | solution.py:48
  13.8 0.7 collective-permute-start.2
  14.5 3.4 %collective-permute-start.3 = (f32[4,64,128]{2,1,0:T(8,128)S(1)}, f32[4,64,128]{2,1,0:T(8,128)S(1)}, u32[]{:S(2)}, u32[]{:S(2)}) collective-permute-start(f32[4,64,128]{2,1,0:T(8,128)S(1)} %get-tuple-element.32), channel_id=1, source_target_pairs={{0,12},{4,8},{8,4},{12,0},{16,28},{20,24},{24,20},{28,16},{1,13},{... | collective-permute-start | bytes 393224 | tf_op jit(solution)/shard_map/ppermute | solution.py:48
  17.9 0.0 collective-permute-done.5.refs_0_
  17.9 0.7 collective-permute-start.4
  18.5 1.9 %fusion = (f32[256,256]{1,0:T(8,128)S(1)}, f32[256,256]{1,0:T(8,128)S(1)}) fusion(f32[256,256]{1,0:T(8,128)} %param.10), kind=kLoop, calls=%fused_computation | loop fusion | bytes 786432 | tf_op jit(solution)/shard_map/sin | solution.py:507
  20.4 0.0 copy-done.4
  20.4 0.0 copy-done.5
  20.4 0.0 copy-done.2
  20.4 0.0 copy-start.6
  20.4 1.0 %copy-done.6 = bf16[512,512]{1,0:T(8,128)(2,1)S(1)} copy-done((bf16[512,512]{1,0:T(8,128)(2,1)S(1)}, bf16[512,512]{1,0:T(8,128)(2,1)}, u32[]{:S(2)}) %copy-start.6) | copy-done | bytes 524312
  21.5 0.0 copy-start.7
  21.5 1.0 %copy-done.7 = bf16[512,512]{1,0:T(8,128)(2,1)S(1)} copy-done((bf16[512,512]{1,0:T(8,128)(2,1)S(1)}, bf16[512,512]{1,0:T(8,128)(2,1)}, u32[]{:S(2)}) %copy-start.7) | copy-done | bytes 524312
  22.5 0.9 shard_map.85
  23.4 16.0 %collective-permute-done.3.refs_2_ = f32[4,64,128]{2,1,0:T(8,128)S(1)} collective-permute-done((f32[4,64,128]{2,1,0:T(8,128)S(1)}, f32[4,64,128]{2,1,0:T(8,128)S(1)}, u32[]{:S(2)}, u32[]{:S(2)}) %collective-permute-start.3) | collective-permute-done | bytes 131104 | tf_op jit(solution)/shard_map/ppermute | solution.py:48
  39.4 0.0 collective-permute-done.4.refs_3_
  39.4 0.0 collective-permute-done.1.refs_0_
  39.4 0.0 collective-permute-done.2.refs_1_
  39.4 5.8 %collective-permute-done.peer = f32[776,256]{1,0:T(8,128)S(1)} collective-permute-done((f32[776,256]{1,0:T(8,128)S(1)}, f32[776,256]{1,0:T(8,128)S(1)}, u32[]{:S(2)}, u32[]{:S(2)}) %collective-permute-start) | collective-permute-done | bytes 794656 | tf_op jit(solution)/shard_map/ppermute | solution.py:463
  45.2 13.0 %shard_map.86 = (f32[4,6,640,128]{3,2,1,0:T(8,128)S(1)}, f32[4,2,64,128]{3,2,1,0:T(8,128)S(1)}, f32[4,1,64,128]{3,2,1,0:T(8,128)S(1)}, f32[4,1,64,128]{3,2,1,0:T...) custom-call(f32[776,256]{1,0:T(8,128)S(1)} %collective-permute-done., ...), custom_call_target="tpu_custom_call", output_to_operand_aliasing={{0}: (7, {})} | custom-call | tf_op jit(solution)/shard_map/pallas_call | solution.py:433
  58.2 0.1 collective-permute-start.8
  58.2 3.5 %collective-permute-start.6 = (f32[4,2,64,128]{3,2,1,0:T(8,128)S(1)}, f32[4,2,64,128]{3,2,1,0:T(8,128)S(1)}, u32[]{:S(2)}, u32[]{:S(2)}) collective-permute-start(f32[4,2,64,128]{3,2,1,0:T(8,128)S(1)} %get-tuple-element.40), channel_id=1, source_target_pairs={{0,8},{1,9},{8,16},{9,17},{10,2},{11,3},{16,24},{17,25},{18,10},{1... | collective-permute-start | bytes 786440 | tf_op jit(solution)/shard_map/ppermute | solution.py:48
  61.8 0.8 collective-permute-start.7
  62.6 0.0 collective-permute-done.8.refs_4_.refs_3_.refs_7_
  62.6 0.1 shard_map.87
  62.6 1.4 %collective-permute-start.9 = (f32[4,2,64,128]{3,2,1,0:T(8,128)S(1)}, f32[4,2,64,128]{3,2,1,0:T(8,128)S(1)}, u32[]{:S(2)}, u32[]{:S(2)}) collective-permute-start(f32[4,2,64,128]{3,2,1,0:T(8,128)S(1)} %get-tuple-element.47), channel_id=1, source_target_pairs={{0,1},{1,0},{2,3},{3,2},{4,5},{5,4},{6,7},{7,6},{8,9},{9,8},{10,11... | collective-permute-start | bytes 786440 | tf_op jit(solution)/shard_map/ppermute | solution.py:573
  64.0 3.0 %collective-permute-start.11 = (f32[4,2,64,128]{3,2,1,0:T(8,128)S(1)}, f32[4,2,64,128]{3,2,1,0:T(8,128)S(1)}, u32[]{:S(2)}, u32[]{:S(2)}) collective-permute-start(f32[4,2,64,128]{3,2,1,0:T(8,128)S(1)} %get-tuple-element.54), channel_id=1, source_target_pairs={{0,8},{1,9},{8,16},{9,17},{10,2},{11,3},{16,24},{17,25},{18,10},{1... | collective-permute-start | bytes 786440 | tf_op jit(solution)/shard_map/ppermute | solution.py:48
  67.0 1.4 %collective-permute-done.6.strip.refs_5_ = f32[4,2,64,128]{3,2,1,0:T(8,128)S(1)} collective-permute-done((f32[4,2,64,128]{3,2,1,0:T(8,128)S(1)}, f32[4,2,64,128]{3,2,1,0:T(8,128)S(1)}, u32[]{:S(2)}, u32[]{:S(2)}) %collective-permute-start.6) | collective-permute-done | bytes 262176 | tf_op jit(solution)/shard_map/ppermute | solution.py:48
  68.4 2.6 %collective-permute-done.7.refs_1_ = f32[4,2,64,128]{3,2,1,0:T(8,128)S(1)} collective-permute-done((f32[4,2,64,128]{3,2,1,0:T(8,128)S(1)}, f32[4,2,64,128]{3,2,1,0:T(8,128)S(1)}, u32[]{:S(2)}, u32[]{:S(2)}) %collective-permute-start.7) | collective-permute-done | bytes 262176 | tf_op jit(solution)/shard_map/ppermute | solution.py:573
  71.0 4.9 %collective-permute-done.9.refs_2_ = f32[4,2,64,128]{3,2,1,0:T(8,128)S(1)} collective-permute-done((f32[4,2,64,128]{3,2,1,0:T(8,128)S(1)}, f32[4,2,64,128]{3,2,1,0:T(8,128)S(1)}, u32[]{:S(2)}, u32[]{:S(2)}) %collective-permute-start.9) | collective-permute-done | bytes 262176 | tf_op jit(solution)/shard_map/ppermute | solution.py:573
  75.9 0.4 collective-permute-start.10
  76.3 0.0 collective-permute-done.11.refs_2_.refs_6_
  76.3 1.8 %collective-permute-start.12 = (f32[4,2,64,128]{3,2,1,0:T(8,128)S(1)}, f32[4,2,64,128]{3,2,1,0:T(8,128)S(1)}, u32[]{:S(2)}, u32[]{:S(2)}) collective-permute-start(f32[4,2,64,128]{3,2,1,0:T(8,128)S(1)} %shard_map.89), channel_id=1, source_target_pairs={{0,1},{1,0},{2,3},{3,2},{4,5},{5,4},{6,7},{7,6},{8,9},{9,8},{10,11... | collective-permute-start | bytes 786440 | tf_op jit(solution)/shard_map/ppermute | solution.py:573
  78.1 7.1 %collective-permute-done.10.refs_3_ = f32[4,2,64,128]{3,2,1,0:T(8,128)S(1)} collective-permute-done((f32[4,2,64,128]{3,2,1,0:T(8,128)S(1)}, f32[4,2,64,128]{3,2,1,0:T(8,128)S(1)}, u32[]{:S(2)}, u32[]{:S(2)}) %collective-permute-start.10) | collective-permute-done | bytes 262176 | tf_op jit(solution)/shard_map/ppermute | solution.py:573
  85.2 3.9 %collective-permute-done.12.refs_4_ = f32[4,2,64,128]{3,2,1,0:T(8,128)S(1)} collective-permute-done((f32[4,2,64,128]{3,2,1,0:T(8,128)S(1)}, f32[4,2,64,128]{3,2,1,0:T(8,128)S(1)}, u32[]{:S(2)}, u32[]{:S(2)}) %collective-permute-start.12) | collective-permute-done | bytes 262176 | tf_op jit(solution)/shard_map/ppermute | solution.py:573
  89.2 1.4 %shard_map.90 = f32[4,128,512]{2,1,0:T(8,128)} custom-call(f32[4,4,128,128]{3,2,1,0:T(8,128)S(1)} %get-tuple-element.39.refs_0_, f32[4,2,64,128]{3,2,1,0:T(8,128)S(1)} %collective-permute-done.7.refs_1_, f32[4,2,64,128]{3,2,1,0:T(8,128)S(1)} %collective-permute-done.9.refs_2_, f32[4,2,64,128]{3,2,1,0:T(8,128)S(1)} %collective-permute-done.10.refs_3_, ...), custom_call_target="tpu_custom_call" | custom-call | tf_op jit(solution)/shard_map/pallas_call | solution.py:433
  (2 shorter events, 0.1 us)
Async XLA Ops:
  0.0 2.2 %copy-start = (f32[2,2,512,512]{3,2,1,0:T(8,128)S(1)}, f32[2,2,512,512]{3,2,1,0:T(8,128)}, u32[]{:S(2)}) copy-start(f32[2,2,512,512]{3,2,1,0:T(8,128)} %param.8) | copy-start | bytes 12582916
  2.2 18.2 %copy-start.4 = (f32[1,1,1,3,256,256]{5,4,3,2,1,0:T(8,128)S(1)}, f32[1,1,1,3,256,256]{5,4,3,2,1,0:T(8,128)}, u32[]{:S(2)}) copy-start(f32[1,1,1,3,256,256]{5,4,3,2,1,0:T(8,128)} %param.11) | copy-start | bytes 2359300
  2.2 18.2 %copy-start.5 = (f32[2,256,256]{2,1,0:T(8,128)S(1)}, f32[2,256,256]{2,1,0:T(8,128)}, u32[]{:S(2)}) copy-start(f32[2,256,256]{2,1,0:T(8,128)} %refs_2_.1) | copy-start | bytes 1572868
  2.3 15.5 %collective-permute-start.5 = (f32[4,512,128]{2,1,0:T(8,128)S(1)}, f32[4,512,128]{2,1,0:T(8,128)S(1)}, u32[]{:S(2)}, u32[]{:S(2)}) collective-permute-start(f32[4,512,128]{2,1,0:T(8,128)S(1)} %shard_map.84), channel_id=1, source_target_pairs={{0,4},{4,0},{1,5},{5,1},{2,6},{6,2},{3,7},{7,3},{8,12},{12,8},{9,1... | collective-permute-start | bytes 3145736 | tf_op jit(solution)/shard_map/ppermute | solution.py:48
  4.3 1.1 %copy-start.3 = (f32[1,1,1,3,256,256]{5,4,3,2,1,0:T(8,128)S(1)}, f32[1,1,1,3,256,256]{5,4,3,2,1,0:T(8,128)}, u32[]{:S(2)}) copy-start(f32[1,1,1,3,256,256]{5,4,3,2,1,0:T(8,128)} %param.11) | copy-start | bytes 2359300
  6.1 39.1 %collective-permute-start = (f32[776,256]{1,0:T(8,128)S(1)}, f32[776,256]{1,0:T(8,128)S(1)}, u32[]{:S(2)}, u32[]{:S(2)}) collective-permute-start(f32[776,256]{1,0:T(8,128)S(1)} %shard_map.82), channel_id=1, source_target_pairs={{0,2},{1,3},{2,0},{3,1},{4,6},{5,7},{6,4},{7,5},{8,10},{9,11},{10,... | collective-permute-start | bytes 2383880 | tf_op jit(solution)/shard_map/ppermute | solution.py:463
  9.9 2.2 %copy-start.1 = (f32[2,2,512,512]{3,2,1,0:T(8,128)S(1)}, f32[2,2,512,512]{3,2,1,0:T(8,128)}, u32[]{:S(2)}) copy-start(f32[2,2,512,512]{3,2,1,0:T(8,128)} %param.8) | copy-start | bytes 12582916
  12.1 8.4 %copy-start.2 = (f32[2,2,512,512]{3,2,1,0:T(8,128)S(1)}, f32[2,2,512,512]{3,2,1,0:T(8,128)}, u32[]{:S(2)}) copy-start(f32[2,2,512,512]{3,2,1,0:T(8,128)} %param.8) | copy-start | bytes 12582916
  12.2 27.2 %collective-permute-start.1 = (f32[4,64,512]{2,1,0:T(8,128)S(1)}, f32[4,64,512]{2,1,0:T(8,128)S(1)}, u32[]{:S(2)}, u32[]{:S(2)}) collective-permute-start(f32[4,64,512]{2,1,0:T(8,128)S(1)} %get-tuple-element.30), channel_id=1, source_target_pairs={{0,8},{8,0},{16,24},{24,16},{1,9},{9,1},{17,25},{25,17},{2,10},{10... | collective-permute-start | bytes 1572872 | tf_op jit(solution)/shard_map/ppermute | solution.py:48
  13.8 25.6 %collective-permute-start.2 = (f32[4,64,512]{2,1,0:T(8,128)S(1)}, f32[4,64,512]{2,1,0:T(8,128)S(1)}, u32[]{:S(2)}, u32[]{:S(2)}) collective-permute-start(f32[4,64,512]{2,1,0:T(8,128)S(1)} %get-tuple-element.31), channel_id=1, source_target_pairs={{8,16},{16,8},{9,17},{17,9},{10,18},{18,10},{11,19},{19,11},{12,20... | collective-permute-start | bytes 1572872 | tf_op jit(solution)/shard_map/ppermute | solution.py:48
  14.5 24.9 %collective-permute-start.3 = (f32[4,64,128]{2,1,0:T(8,128)S(1)}, f32[4,64,128]{2,1,0:T(8,128)S(1)}, u32[]{:S(2)}, u32[]{:S(2)}) collective-permute-start(f32[4,64,128]{2,1,0:T(8,128)S(1)} %get-tuple-element.32), channel_id=1, source_target_pairs={{0,12},{4,8},{8,4},{12,0},{16,28},{20,24},{24,20},{28,16},{1,13},{... | collective-permute-start | bytes 393224 | tf_op jit(solution)/shard_map/ppermute | solution.py:48
  17.9 21.5 %collective-permute-start.4 = (f32[4,64,128]{2,1,0:T(8,128)S(1)}, f32[4,64,128]{2,1,0:T(8,128)S(1)}, u32[]{:S(2)}, u32[]{:S(2)}) collective-permute-start(f32[4,64,128]{2,1,0:T(8,128)S(1)} %get-tuple-element.33), channel_id=1, source_target_pairs={{8,20},{12,16},{16,12},{20,8},{9,21},{13,17},{17,13},{21,9},{10,22... | collective-permute-start | bytes 393224 | tf_op jit(solution)/shard_map/ppermute | solution.py:48
  20.4 1.0 %copy-start.6 = (bf16[512,512]{1,0:T(8,128)(2,1)S(1)}, bf16[512,512]{1,0:T(8,128)(2,1)}, u32[]{:S(2)}) copy-start(bf16[512,512]{1,0:T(8,128)(2,1)} %constant.10.refs_4_) | copy-start | bytes 1572868
  21.5 1.0 %copy-start.7 = (bf16[512,512]{1,0:T(8,128)(2,1)S(1)}, bf16[512,512]{1,0:T(8,128)(2,1)}, u32[]{:S(2)}) copy-start(bf16[512,512]{1,0:T(8,128)(2,1)} %constant.9.refs_3_) | copy-start | bytes 1572868
  58.2 4.4 %collective-permute-start.8 = (f32[4,1,320,128]{3,2,1,0:T(8,128)S(1)}, f32[4,1,320,128]{3,2,1,0:T(8,128)S(1)}, u32[]{:S(2)}, u32[]{:S(2)}) collective-permute-start(f32[4,1,320,128]{3,2,1,0:T(8,128)S(1)} %get-tuple-element.46), channel_id=1, source_target_pairs={{0,4},{4,0},{1,5},{5,1},{2,6},{6,2},{3,7},{7,3},{8,12},{12,8},{9,1... | collective-permute-start | bytes 1966088 | tf_op jit(solution)/shard_map/ppermute | solution.py:48
  58.2 10.1 %collective-permute-start.6 = (f32[4,2,64,128]{3,2,1,0:T(8,128)S(1)}, f32[4,2,64,128]{3,2,1,0:T(8,128)S(1)}, u32[]{:S(2)}, u32[]{:S(2)}) collective-permute-start(f32[4,2,64,128]{3,2,1,0:T(8,128)S(1)} %get-tuple-element.40), channel_id=1, source_target_pairs={{0,8},{1,9},{8,16},{9,17},{10,2},{11,3},{16,24},{17,25},{18,10},{1... | collective-permute-start | bytes 786440 | tf_op jit(solution)/shard_map/ppermute | solution.py:48
  61.8 9.2 %collective-permute-start.7 = (f32[4,2,64,128]{3,2,1,0:T(8,128)S(1)}, f32[4,2,64,128]{3,2,1,0:T(8,128)S(1)}, u32[]{:S(2)}, u32[]{:S(2)}) collective-permute-start(f32[4,2,64,128]{3,2,1,0:T(8,128)S(1)} %get-tuple-element.41), channel_id=1, source_target_pairs={{0,1},{1,0},{2,3},{3,2},{4,5},{5,4},{6,7},{7,6},{8,9},{9,8},{10,11... | collective-permute-start | bytes 786440 | tf_op jit(solution)/shard_map/ppermute | solution.py:573
  62.6 13.2 %collective-permute-start.9 = (f32[4,2,64,128]{3,2,1,0:T(8,128)S(1)}, f32[4,2,64,128]{3,2,1,0:T(8,128)S(1)}, u32[]{:S(2)}, u32[]{:S(2)}) collective-permute-start(f32[4,2,64,128]{3,2,1,0:T(8,128)S(1)} %get-tuple-element.47), channel_id=1, source_target_pairs={{0,1},{1,0},{2,3},{3,2},{4,5},{5,4},{6,7},{7,6},{8,9},{9,8},{10,11... | collective-permute-start | bytes 786440 | tf_op jit(solution)/shard_map/ppermute | solution.py:573
  64.0 12.3 %collective-permute-start.11 = (f32[4,2,64,128]{3,2,1,0:T(8,128)S(1)}, f32[4,2,64,128]{3,2,1,0:T(8,128)S(1)}, u32[]{:S(2)}, u32[]{:S(2)}) collective-permute-start(f32[4,2,64,128]{3,2,1,0:T(8,128)S(1)} %get-tuple-element.54), channel_id=1, source_target_pairs={{0,8},{1,9},{8,16},{9,17},{10,2},{11,3},{16,24},{17,25},{18,10},{1... | collective-permute-start | bytes 786440 | tf_op jit(solution)/shard_map/ppermute | solution.py:48
  75.9 9.3 %collective-permute-start.10 = (f32[4,2,64,128]{3,2,1,0:T(8,128)S(1)}, f32[4,2,64,128]{3,2,1,0:T(8,128)S(1)}, u32[]{:S(2)}, u32[]{:S(2)}) collective-permute-start(f32[4,2,64,128]{3,2,1,0:T(8,128)S(1)} %shard_map.88), channel_id=1, source_target_pairs={{0,1},{1,0},{2,3},{3,2},{4,5},{5,4},{6,7},{7,6},{8,9},{9,8},{10,11... | collective-permute-start | bytes 786440 | tf_op jit(solution)/shard_map/ppermute | solution.py:573
  76.3 12.8 %collective-permute-start.12 = (f32[4,2,64,128]{3,2,1,0:T(8,128)S(1)}, f32[4,2,64,128]{3,2,1,0:T(8,128)S(1)}, u32[]{:S(2)}, u32[]{:S(2)}) collective-permute-start(f32[4,2,64,128]{3,2,1,0:T(8,128)S(1)} %shard_map.89), channel_id=1, source_target_pairs={{0,1},{1,0},{2,3},{3,2},{4,5},{5,4},{6,7},{7,6},{8,9},{9,8},{10,11... | collective-permute-start | bytes 786440 | tf_op jit(solution)/shard_map/ppermute | solution.py:573

commit v2 on v1

--- a/solution.py
+++ b/solution.py
@@ -13,19 +13,29 @@
 HALO = 64
 PMAX = 3
 LANE = 128
+HALF = PATCH // 2
 VMEM_LIMIT = 32 * 1024 * 1024
 VMEM_LITTLE = 8 * 1024 * 1024
-NOTE_ROWS = 8
+GROUP = 4
 
 
 def block_tables():
-    line = np.arange(PATCH)
-    angles = (line[:, None] * line[None, :] % PATCH) * (2.0 * math.pi / PATCH)
-    cosines = np.cos(angles) / math.sqrt(PATCH)
-    sines = np.sin(angles) / math.sqrt(PATCH)
-    turn = np.block([[cosines, sines], [-sines, cosines]])
-    back = np.block([[cosines, -sines], [sines, cosines]])
-    return (jnp.asarray(turn.astype(np.float32)).astype(jnp.bfloat16), jnp.asarray(back.astype(np.float32)).astype(jnp.bfloat16))
+    index = np.arange(HALF)
+    tables = []
+    for odd in range(2):
+        angles = ((2 * index[:, None] + odd) * index[None, :] % PATCH) * (2.0 * math.pi / PATCH)
+        cosines = np.cos(angles) / math.sqrt(PATCH)
+        sines = np.sin(angles) / math.sqrt(PATCH)
+        tables.append(np.block([[cosines, sines], [-sines, cosines]]))
+    tables += [table.T for table in tables]
+    return jnp.asarray(np.stack(tables).astype(np.float32)).astype(jnp.bfloat16)
+
+
+def sorted_columns():
+    index = np.arange(PATCH)
+    matrix = np.zeros((PATCH, PATCH), np.float32)
+    matrix[index, index % 2 * HALF + index // 2] = 1.0
+    return jnp.asarray(np.stack([matrix, matrix.T])).astype(jnp.bfloat16)
 
 
 def pair_of(index, phase):
@@ -51,34 +61,65 @@
 OUTER = -1
 
 
-def transform(pairs, left, right):
-    stacked = jnp.concatenate(
-        [jnp.concatenate([pair[part] for pair in pairs], axis=1) for part in range(2)], axis=0
-    )
-    middle = jnp.dot(left[...], stacked, preferred_element_type=jnp.float32).astype(jnp.bfloat16)
-    size = PATCH
-    middle = jnp.concatenate(
-        [
-            jnp.concatenate(
-                [middle[p * size : (p + 1) * size, i * size : (i + 1) * size] for p in range(2)],
-                axis=1,
-            )
-            for i in range(len(pairs))
-        ],
-        axis=0,
-    )
-    result = jnp.dot(middle, right[...], preferred_element_type=jnp.float32)
+def times(a, b):
+    return jnp.dot(
+        a.astype(jnp.bfloat16), b.astype(jnp.bfloat16), preferred_element_type=jnp.float32
+    )
+
+
+def side(parts, axis):
+    return jnp.concatenate(parts, axis=axis)
+
+
+def to_frequencies(pairs, tables):
+    tall = []
+    for odd in range(2):
+        halves = [
+            [x[:HALF] - x[HALF:] if odd else x[:HALF] + x[HALF:] for x in pair] for pair in pairs
+        ]
+        tall.append(times(tables[odd], side([side(half, 0) for half in halves], 1)))
+    wide = []
+    for odd in range(2):
+        rows = []
+        for i in range(len(pairs)):
+            first, second = 2 * i * HALF, (2 * i + 1) * HALF
+            for y in tall:
+                parts = []
+                for part in range(2):
+                    x = y[part * HALF : (part + 1) * HALF]
+                    low, high = x[:, first:second], x[:, second : second + HALF]
+                    parts.append(low - high if odd else low + high)
+                rows.append(side(parts, 1))
+        wide.append(times(side(rows, 0), tables[2 + odd]))
     return [
-        (
-            result[i * size : (i + 1) * size, :size],
-            result[i * size : (i + 1) * size, size:],
-        )
+        [(z[i * PATCH : (i + 1) * PATCH, :HALF], z[i * PATCH : (i + 1) * PATCH, HALF:]) for z in wide]
         for i in range(len(pairs))
     ]
 
 
-def rounded(pair):
-    return pair[0].astype(jnp.bfloat16), pair[1].astype(jnp.bfloat16)
+def from_frequencies(spectra, tables):
+    parts = []
+    for odd in range(2):
+        rows = slice(odd * HALF, (odd + 1) * HALF)
+        columns = [side([x[rows] for x in pair], 0) for spectrum in spectra for pair in spectrum]
+        parts.append(times(tables[2 + odd], side(columns, 1)))
+    halves = [parts[0] + parts[1], parts[0] - parts[1]]
+    sums = []
+    for odd in range(2):
+        rows = []
+        for i in range(len(spectra)):
+            at = (2 * i + odd) * HALF
+            for half in halves:
+                rows.append(side([half[:HALF, at : at + HALF], half[HALF:, at : at + HALF]], 1))
+        sums.append(times(side(rows, 0), tables[odd]))
+    low, high = sums[0] + sums[1], sums[0] - sums[1]
+    results = []
+    for i in range(len(spectra)):
+        rows = slice(i * PATCH, (i + 1) * PATCH)
+        results.append(
+            tuple(side([x[rows, p * HALF : (p + 1) * HALF] for x in (low, high)], 1) for p in range(2))
+        )
+    return results
 
 
 def product(a, b):
@@ -126,31 +167,27 @@
             )
 
 
-def forward(ext, corners, probe, wave, turn, back):
+def patch_gradients(ext, corners, intensities, probe, waves, tables, put):
     lamp = (probe[0], probe[1])
-    prop = (wave[0][...], wave[1][...])
-    entrance = [rounded(product(lamp, window(ext, 0, *corner))) for corner in corners]
-    spectra = transform(entrance, turn, back)
-    arrived = transform([rounded(product(prop, x)) for x in spectra], back, turn)
+    prop = [(waves[0, odd], waves[1, odd]) for odd in range(2)]
+
+    def through_prop(multiply, spectra):
+        return [[multiply(h, z) for h, z in zip(prop, spectrum)] for spectrum in spectra]
+
+    entrance = [product(lamp, window(ext, 0, *corner)) for corner in corners]
+    arrived = from_frequencies(through_prop(product, to_frequencies(entrance, tables)), tables)
     seconds = [window(ext, 1, *corner) for corner in corners]
-    far = transform([rounded(product(o, w)) for o, w in zip(seconds, arrived)], turn, back)
-    return far, arrived, seconds
-
-
-def backward(far, arrived, seconds, intensities, probe, wave, turn, back, put):
-    lamp = (probe[0], probe[1])
-    prop = (wave[0][...], wave[1][...])
+    far = to_frequencies([product(o, w) for o, w in zip(seconds, arrived)], tables)
     residuals = []
-    for psi, intensity in zip(far, intensities):
-        misfit = psi[0] * psi[0] + psi[1] * psi[1] - intensity
-        residuals.append(rounded((misfit * psi[0], misfit * psi[1])))
-    back_seconds = transform(residuals, back, turn)
+    for spectrum, intensity in zip(far, intensities):
+        misfits = [z[0] * z[0] + z[1] * z[1] - i for z, i in zip(spectrum, intensity)]
+        residuals.append([(m * z[0], m * z[1]) for m, z in zip(misfits, spectrum)])
+    back_seconds = from_frequencies(residuals, tables)
     for i, (w, g) in enumerate(zip(arrived, back_seconds)):
         put(i, 1, conj_product(w, g))
-    through = [rounded(conj_product(o, g)) for o, g in zip(seconds, back_seconds)]
-    spectra = transform(through, turn, back)
-    back_firsts = transform([rounded(conj_product(prop, x)) for x in spectra], back, turn)
-    for i, g in enumerate(back_firsts):
+    through = [conj_product(o, g) for o, g in zip(seconds, back_seconds)]
+    back_spectra = through_prop(conj_product, to_frequencies(through, tables))
+    for i, g in enumerate(from_frequencies(back_spectra, tables)):
         put(i, 0, conj_product(lamp, g))
 
 
@@ -202,9 +239,13 @@
             copy.wait()
 
 
-def staging_kernel(sides, core, *refs):
+def staging_kernel(sides, _, core, *refs):
     col_refs, refs = refs[:sides], refs[sides:]
-    near, (ext, *near_to), sems = refs[:4], refs[4:-1], refs[-1]
+    cosine, sine, order, near, (ext, waves, *near_to), sems = *refs[:3], refs[3:7], refs[7:-1], refs[-1]
+    for k, wave in enumerate((cosine, sine)):
+        sorted_wave = sort_frequencies([wave[...]], order)
+        for odd in range(2):
+            waves[k, odd] = sorted_wave[:, odd * HALF : (odd + 1) * HALF]
     height, width = core.shape[1], core.shape[2]
     tiles = ext.shape[1]
     place = place_of(height)
@@ -212,19 +253,21 @@
     for t in range(width // LANE):
         part = core.at[:, :, pl.ds(t * LANE, LANE)]
         copies.start(part, ext.at[:, t + 1, pl.ds(HALO, height), :])
-    for j, ref in enumerate(col_refs):
-        copies.start(ref, ext.at[:, far_tile(place, j, tiles), pl.ds(HALO, height), :])
     for source, target in zip(near, near_to):
         copies.start(source, target)
+    for j, ref in enumerate(col_refs):
+        tile = far_tile(place, j, tiles)
+        for p in range(2):
+            for k, half in enumerate(unpacked(ref[p], place[3] != j)):
+                ext[p + 2 * k, tile, HALO : HALO + height, :] = half
     copies.wait()
 
 
 def patches_kernel(sides, cuts, peer, *refs):
     row_refs, refs = refs[: sides[0]], refs[sides[0] :]
-    corner_refs, refs = refs[: sides[0] * sides[1]], refs[sides[0] * sides[1] :]
-    own_corners, own_count, ext, own, probe, cosine, sine, turn, back = refs[:9]
-    outs, (acc, note, queue, sems) = refs[10:-4], refs[-4:]
-    wave = (cosine, sine)
+    corner_refs, refs = refs[: sides[1]], refs[sides[1] :]
+    own_info, peer_info, ext, own, probe, waves, tables, order = refs[:8]
+    outs, (acc, queue, sems) = refs[9:-3], refs[-3:]
     tiles, height = ext.shape[1], ext.shape[2] - 2 * HALO
     half_rows = height // 2
     place = place_of(height)
@@ -237,53 +280,50 @@
         for t in range(tiles - 2):
             part = ref.at[:, :, pl.ds(t * LANE, LANE)]
             copies.start(part, ext.at[:, t + 1, pl.ds(far_row(i), HALO), :])
-    for k, ref in enumerate(corner_refs):
-        i, j = divmod(k, sides[1])
-        copies.start(ref, ext.at[:, far_tile(place, j, tiles), pl.ds(far_row(i), HALO), :])
-    note_at = pl.ds(PMAX * PATCH, NOTE_ROWS)
-    copies.start(peer.at[note_at, pl.ds(0, LANE)], note)
+    for j, ref in enumerate(corner_refs):
+        tile = far_tile(place, j, tiles)
+        for i in range(sides[0]):
+            rows = pl.ds(far_row(i), HALO)
+            for p in range(2):
+                for q, half in enumerate(unpacked(ref[i, p], place[3] != j)):
+                    ext[p + 2 * q, tile, rows, :] = half
     first = pl.multiple_of(place[0] + HALO, 8)
     outer = pl.multiple_of(place[1] + HALO, 8)
     acc[:, :, pl.ds(first, half_rows), :] = jnp.zeros((4, tiles, half_rows, LANE), jnp.float32)
     acc[:, :, pl.ds(outer, HALO), :] = jnp.zeros((4, tiles, HALO, LANE), jnp.float32)
 
     def intensity(index):
-        mine = own[jnp.minimum(index, PMAX - 1)]
-        start = pl.multiple_of(jnp.maximum(index - PMAX, 0) * PATCH, PATCH)
-        return jnp.where(index < PMAX, mine, peer[pl.ds(start, PATCH), :])
+        mine, theirs = jnp.minimum(index, PMAX - 1), jnp.maximum(index - PMAX, 0)
+        return jnp.where(index < PMAX, own[mine], peer[theirs])
 
     copies.wait()
     length = jnp.int32(0)
     for index in range(2 * PMAX):
-        slot = index % PMAX
-        if index < PMAX:
-            row, col, count = own_corners[slot, 0], own_corners[slot, 1], own_count[0]
-        else:
-            row, col, count = [
-                note[0, at].astype(jnp.int32) for at in (2 * slot, 2 * slot + 1, 2 * PMAX)
-            ]
+        info, slot = (own_info, index) if index < PMAX else (peer_info, index - PMAX)
+        row, col, count = info[slot], info[PMAX + slot], info[2 * PMAX]
         queue[3 * length] = index
         queue[3 * length + 1] = row
         queue[3 * length + 2] = col
         length = length + ((slot < count) & wanted(place, row, half_rows)).astype(jnp.int32)
 
     def step(turn_at, carry):
-        items = [2 * turn_at, jnp.minimum(2 * turn_at + 1, length - 1)]
-        whole = 2 * turn_at + 1 < length
+        start = GROUP * turn_at
+        items = [start] + [jnp.minimum(start + i, length - 1) for i in range(1, GROUP)]
         corners = [(queue[3 * i + 1], queue[3 * i + 2]) for i in items]
-        far, arrived, seconds = forward(ext, corners, probe, wave, turn, back)
+        ordered = sort_frequencies([intensity(queue[3 * i]) for i in items], order)
+        rows = [ordered[i * PATCH : (i + 1) * PATCH] for i in range(GROUP)]
+        intensities = [(x[:, :HALF], x[:, HALF:]) for x in rows]
 
         def put(i, slice_at, pair):
             if i == 0:
                 deposit(acc, slice_at, *corners[i], pair)
             else:
-                pl.when(whole)(lambda: deposit(acc, slice_at, *corners[i], pair))
-
-        intensities = [intensity(queue[3 * i]) for i in items]
-        backward(far, arrived, seconds, intensities, probe, wave, turn, back, put)
+                pl.when(start + i < length)(lambda: deposit(acc, slice_at, *corners[i], pair))
+
+        patch_gradients(ext, corners, intensities, probe, waves, tables, put)
         return carry
 
-    lax.fori_loop(0, (length + 1) // 2, step, 0)
+    lax.fori_loop(0, (length + GROUP - 1) // GROUP, step, 0)
     gifts = Copies(sems)
     for target, parts in zip(outs, cuts):
         row_to = 0
@@ -314,7 +354,7 @@
     place = place_of(height)
     rims, (open_out, outer_out) = refs[:sides], refs[-2:]
     open_out[:, 0:1] = open_left[...]
-    open_out[:, 1:2] = open_right[...]
+    open_out[:, 1:] = open_right[...]
     add_rims(place, open_out, rims, pl.multiple_of(place[5], 8))
     outer_out[:, 0:1] = outer_left[...]
     outer_out[:, 1:2] = outer_right[...]
@@ -344,7 +384,7 @@
 
 def final_kernel(height, sides, part, *refs):
     place = place_of(height)
-    open_got, shut_got, strip, rims = refs[:2], refs[2:4], refs[4:6], refs[6 : 6 + sides]
+    shut_got, open_got, strip, rims = refs[:2], refs[2:4], refs[4:6], refs[6 : 6 + sides]
     out, work = refs[6 + sides :]
     work[...] = part[...]
     tiles = work.shape[1]
@@ -352,9 +392,10 @@
 
     def add(at, inner, edge):
         rows = pl.ds(pl.multiple_of(at, 8), inner.shape[2])
-        work[:, 1 : tiles - 1, rows, :] += inner[...]
+        split = 1 + inner.shape[1]
+        work[:, 1:split, rows, :] += inner[...]
         work[:, 0:1, rows, :] += edge[:, 0:1]
-        work[:, tiles - 1 : tiles, rows, :] += edge[:, 1:2]
+        work[:, split:, rows, :] += edge[:, 1:]
 
     add(place[9], *open_got)
     add(place[8], *shut_got)
@@ -387,37 +428,58 @@
     return pl.ds(pl.multiple_of(jnp.where(place[3] == phase, width - LANE, 0), LANE), LANE)
 
 
-def note_kernel(corners, count, own, out, sems):
+def sort_frequencies(arrays, order):
+    values = side(arrays, 1)
+    total = None
+    for _ in range(3):
+        part = values.astype(jnp.bfloat16)
+        values = values - part.astype(jnp.float32)
+        rows = times(order[1], part)
+        rows = side([rows[:, i * PATCH : (i + 1) * PATCH] for i in range(len(arrays))], 0)
+        moved = times(rows, order[0])
+        total = moved if total is None else total + moved
+    return total
+
+
+def packed(strips, high):
+    low_lanes = lax.broadcasted_iota(jnp.int32, strips[0].shape, 1) < HALO
+    turns = [jnp.where(high, LANE - HALO, 0), jnp.where(high, 0, HALO)]
+    parts = [pltpu.roll(strip, turn, 1) for strip, turn in zip(strips, turns)]
+    return jnp.where(low_lanes, *parts)
+
+
+def unpacked(tile, high):
+    return [
+        pltpu.roll(tile, turn, 1)
+        for turn in (jnp.where(high, HALO, 0), jnp.where(high, 0, LANE - HALO))
+    ]
+
+
+def edges_kernel(sides, core, *refs):
+    outs, (cols, sems) = refs[:-2], refs[-2:]
     copies = Copies(sems)
-    for slot in range(PMAX):
-        copies.start(own.at[slot], out.at[pl.ds(slot * PATCH, PATCH), :])
-    lane = lax.broadcasted_iota(jnp.int32, (NOTE_ROWS, PATCH), 1)
-    values = jnp.where(lane == 2 * PMAX, count[0], 0)
-    for index in range(2 * PMAX):
-        values = jnp.where(lane == index, corners[index // 2, index % 2], values)
-    out[PMAX * PATCH :, :] = values.astype(jnp.float32)
-    copies.wait()
-
-
-def columns_kernel(core, *refs):
-    outs, copies = refs[:-1], Copies(refs[-1])
-    place = place_of(core.shape[1])
-    for j, out in enumerate(outs):
-        copies.start(core.at[:, :, near_cols(place, j, core.shape[2])], out)
-    copies.wait()
-
-
-def rows_kernel(sides, core, *refs):
-    outs, copies = refs[:-1], Copies(refs[-1])
     height, width = core.shape[1:]
     place = place_of(height)
+    for j in range(sides[1]):
+        copies.start(core.at[:, :, near_cols(place, j, width)], cols.at[j])
     for i in range(sides[0]):
-        rows = near_rows(place, i, height)
-        copies.start(core.at[:, rows, :], outs[i])
-        for j in range(sides[1]):
-            target = outs[sides[0] + i * sides[1] + j]
-            copies.start(core.at[:, rows, near_cols(place, j, width)], target)
+        copies.start(core.at[:, near_rows(place, i, height), :], outs[i])
     copies.wait()
+    for j in range(sides[1]):
+        high = place[3] == j
+        for p in range(2):
+            outs[sides[0] + j][p] = packed([cols[j, p], cols[j, p + 2]], high)
+
+
+def corners_kernel(sides, _, *refs):
+    strips, outs = refs[: sides[0]], refs[sides[0] :]
+    width = strips[0].shape[2]
+    for j, out in enumerate(outs):
+        high = lax.axis_index("col") % 2 == j
+        cols = pl.ds(pl.multiple_of(jnp.where(high, width - LANE, 0), LANE), LANE)
+        for i, strip in enumerate(strips):
+            for p in range(2):
+                out[i, p] = packed([strip[p, :, cols], strip[p + 2, :, cols]], high)
 
 
 ANY = pl.BlockSpec(memory_space=pl.ANY)
@@ -457,7 +519,10 @@
     scan_at = lax.axis_index("scan")
     planes = object_field.reshape(4, height, width)
     own = measured.reshape(PMAX, PATCH, PATCH)
-    own_corners, own_count = positions.reshape(PMAX, 2), counts.reshape(1)
+    order = sorted_columns()
+    own_info = jnp.concatenate(
+        [positions.reshape(PMAX, 2).T.reshape(-1), counts.reshape(1), jnp.zeros((1,), jnp.int32)]
+    ).astype(jnp.int32)
 
     def across(value):
         return lax.ppermute(value, "scan", [(i, i ^ stride) for i in range(shard_count)])
@@ -468,97 +533,98 @@
     def to_rows(value, i):
         return joint_permute(value, ("row",), lambda r: (pair_of(r, i),))
 
-    def to_corner(value, i, j):
-        return joint_permute(value, ("row", "col"), lambda r, c: (pair_of(r, i), pair_of(c, j)))
-
-    def cut_edges(kernel, shapes):
-        return call(
-            kernel,
-            shapes,
-            [ANY],
-            [VMEM] * len(shapes),
-            [pltpu.SemaphoreType.DMA((len(shapes),))],
-            planes,
-            limit=VMEM_LITTLE,
-        )
-
-    noted = call(
-        note_kernel,
-        block(PMAX * PATCH + NOTE_ROWS, PATCH),
-        [SMEM, SMEM, ANY],
-        VMEM,
-        [pltpu.SemaphoreType.DMA((PMAX,))],
-        own_corners,
-        own_count,
-        own,
+    peer = across(own)
+    peer_info = across(own_info)
+    edge_shapes = (
+        [block(4, HALO, width)] * both[0]
+        + [block(2, height, LANE)] * sides
+    )
+    edges = call(
+        functools.partial(edges_kernel, both),
+        edge_shapes,
+        [ANY],
+        [VMEM] * len(edge_shapes),
+        [pltpu.VMEM((sides, 4, height, LANE), jnp.float32), pltpu.SemaphoreType.DMA((sum(both),))],
+        planes,
         limit=VMEM_LITTLE,
     )
-    peer = across(noted)
-    row_edges = cut_edges(
-        functools.partial(rows_kernel, both),
-        [block(4, HALO, width)] * both[0] + [block(4, HALO, LANE)] * (both[0] * sides),
-    )
-    row_halos = [to_rows(row_edges[i], i) for i in row_sides]
-    col_edges = cut_edges(columns_kernel, [block(4, height, LANE)] * sides)
-    col_halos = [to_cols(edge, j) for j, edge in zip(col_sides, col_edges)]
-    corner_halos = [
-        to_corner(row_edges[both[0] + i * sides + j], i, j) for i in row_sides for j in col_sides
-    ]
+    row_halos = [to_rows(edges[i], i) for i in row_sides]
+    col_halos = [to_cols(edges[both[0] + j], j) for j in col_sides]
     cosine, sine = jnp.cos(prop_phase), jnp.sin(prop_phase)
-    turn, back = block_tables()
+    tables = block_tables()
 
     two_bands = shard_count == 4 and rest > 0
     inner = tiles - 2
     cuts = [(inner, [(2, OUTER, HALO)]), (1, [(1, OUTER, HALO)]), (1, [(tiles, OUTER, HALO)])]
     cuts += [(1, [((j,), None, half_rows), ((j,), OUTER, HALO)]) for j in col_sides]
     if two_bands:
-        for at, rows in ((5, rest), (6, HALO)):
-            cuts += [(inner, [(2, at, rows)]), (1, [(1, at, rows)]), (1, [(tiles, at, rows)])]
+        early = inner
+        right = tiles - early - 1
+        cuts += [(early, [(2, 5, rest)]), (1, [(1, 5, rest)]), (right, [(2 + early, 5, rest)])]
+        cuts += [(inner, [(2, 6, HALO)]), (1, [(1, 6, HALO)]), (1, [(tiles, 6, HALO)])]
         cuts += [(tiles, [(1, 4, band)])]
     else:
         cuts += [(tiles, [(1, None, half_rows)]), (1, [(1, None, HALO)]), (1, [(1, None, HALO)])]
     full = (4, tiles + 2, height + 2 * HALO, LANE)
-    table = jax.ShapeDtypeStruct(turn.shape, turn.dtype)
-    staged = call(
+    ext, waves, lamp, near_tables, near_own, near_order = call(
         functools.partial(staging_kernel, sides),
-        [block(*full), block(*own.shape), block(*probe_field.shape), table, table],
-        [ANY] * (sides + 5),
-        [VMEM] * 5,
-        [pltpu.SemaphoreType.DMA((tiles + sides + 4,))],
+        [
+            block(*full),
+            block(2, 2, PATCH, HALF),
+            block(*probe_field.shape),
+            jax.ShapeDtypeStruct(tables.shape, tables.dtype),
+            block(*own.shape),
+            jax.ShapeDtypeStruct(order.shape, order.dtype),
+        ],
+        [SMEM, ANY] + [VMEM] * (sides + 3) + [ANY] * 4,
+        [VMEM] * 6,
+        [pltpu.SemaphoreType.DMA((tiles + 4,))],
+        own_info,
         planes,
         *col_halos,
+        cosine,
+        sine,
+        order,
+        probe_field,
+        tables,
         own,
-        probe_field,
-        turn,
-        back,
+        order,
         limit=VMEM_LITTLE,
     )
-    ext, own, lamp, turn, back = staged
+    row_ends = call(
+        functools.partial(corners_kernel, both),
+        [block(both[0], 2, HALO, LANE)] * sides,
+        [VMEM] * (1 + both[0]),
+        [VMEM] * sides,
+        [],
+        near_order,
+        *row_halos,
+        limit=VMEM_LITTLE,
+    )
+    corner_halos = [to_cols(ends, j) for j, ends in zip(col_sides, row_ends)]
     arrivals = [peer, *row_halos, *corner_halos]
     copy_count = max(
-        (tiles + sides) * both[0] + 1, sum(len(parts) for _, parts in cuts)
+        tiles * both[0], sum(len(parts) for _, parts in cuts)
     )
     outs = call(
         functools.partial(patches_kernel, both, [parts for _, parts in cuts]),
         [block(*full)] + [block(4, wide, sum(part[2] for part in parts), LANE) for wide, parts in cuts],
-        [VMEM] + [ANY] * (len(arrivals) - 1) + [SMEM, SMEM] + [VMEM] * 7,
+        [VMEM] + [ANY] * both[0] + [VMEM] * sides + [SMEM, SMEM] + [VMEM] * 6,
         [VMEM] + [ANY] * len(cuts),
         [
             pltpu.VMEM(full, jnp.float32),
-            pltpu.SMEM((NOTE_ROWS, LANE), jnp.float32),
             pltpu.SMEM((3 * (2 * PMAX + 1),), jnp.int32),
             pltpu.SemaphoreType.DMA((copy_count,)),
         ],
         *arrivals,
-        own_corners,
-        own_count,
+        own_info,
+        peer_info,
         ext,
-        own,
+        near_own,
         lamp,
-        cosine,
-        sine,
-        turn,
-        back,
+        waves,
+        near_tables,
+        near_order,
         aliases={len(arrivals) + 2: 0},
     )[1:]
     outer_inner, outer_left, outer_right = outs[:3]
@@ -588,7 +654,10 @@
     got_inner = to_next(outer_inner)
     open_edge, outer_edge = fold(
         lambda *refs: edge_kernel(refs[0], sides, *refs[1:]),
-        (block(4, 2, pieces[1].shape[2], LANE), block(4, 2, HALO, LANE)),
+        (
+            block(4, 1 + pieces[2].shape[1], pieces[1].shape[2], LANE),
+            block(4, 2, HALO, LANE),
+        ),
         pieces[1],
         pieces[2],
         outer_left,
@@ -615,7 +684,8 @@
             mask //= 2
         return half.transpose(0, 2, 1, 3).reshape(2, 2, band, width)
     got_open = [beside(pieces[0]), beside(open_edge)]
-    got_inner, *got_open = lax.optimization_barrier((got_inner, *got_open))
+    got_open[0], got_inner = lax.optimization_barrier((got_open[0], got_inner))
+    got_open[1], got_edge = lax.optimization_barrier((got_open[1], got_edge))
     shut_inner = fold(shut_inner_kernel, block(4, inner, HALO, LANE), pieces[3], got_inner)
     got_shut = [beside(shut_inner)]
     shut_edge = fold(
@@ -631,8 +701,8 @@
         lambda *refs: final_kernel(refs[0], sides, *refs[1:]),
         block(4, band, width),
         pieces[6],
+        *got_shut,
         *got_open,
-        *got_shut,
         got_inner,
         got_edge,
         *got_rims,

time: 91 us -> 76.2 us (0.84)
  waiting for transfers between devices: 41.7 us -> 31.7 us
  starting transfers between devices: 21.5 us -> 16.6 us
  local copies, waits for them, and re-layouts: 10.2 us -> 11.2 us
    ppermute x8 -> x7, waiting for transfers between devices: 17.4 us -> 4.44 us  [joint_permute(): lax.ppermute(value, tuple(names) if len(names) > 1 else names[0], route)]
    ppermute x1 -> x2, waiting for transfers between devices: 5.76 us -> 15.9 us  [across(): lax.ppermute(value, 'scan', [(i, i ^ stride) for i in range(shard_count)])]
    ppermute x4, waiting for transfers between devices: 18.5 us -> 11.4 us  [beside(): lax.ppermute(value, 'scan', [(i, i ^ mask) for i in range(shard_count)])]
    ppermute x8 -> x7, starting transfers between devices: 13.4 us -> 10.5 us  [joint_permute(): lax.ppermute(value, tuple(names) if len(names) > 1 else names[0], route)]
    ppermute x4, starting transfers between devices: 4.35 us -> 1.99 us  [beside(): lax.ppermute(value, 'scan', [(i, i ^ mask) for i in range(shard_count)])]
    unnamed x16 -> x12, local copies, waits for them, and re-layouts: 7.6 us -> 8.53 us
    pallas_call x9 -> x8, Pallas kernels: 16.3 us -> 15.5 us  [call(): pl.pallas_call(kernel, out_shape=out_shapes, in_specs=in_specs, out_specs...]
    ppermute x1 -> x2, starting transfers between devices: 3.8 us -> 4.17 us  [across(): lax.ppermute(value, 'scan', [(i, i ^ stride) for i in range(shard_count)])]
  transfers between devices with their start and end apart: 13 -> 13, of which waited for: 7 -> 7; matrix products, arithmetic and copies ran while one was open for 3% -> 4% of each run, Pallas kernels for 2% -> 5%
where the time goes in v2:
time: 76.2 us; the launch traced here: 75.9 us
  waiting for transfers between devices  31.7 us (42%)
  starting transfers between devices  16.6 us (22%)
  Pallas kernels  15.5 us (20%)
  local copies, waits for them, and re-layouts  11.2 us (15%)
  between operations  0.8 us (1%)
    ppermute x2, waiting for transfers between devices, across(): lax.ppermute(value, 'scan', [(i, i ^ stride) for i in range(shard_count)])  15.9 us
    pallas_call x8, Pallas kernels, call(): pl.pallas_call(kernel, out_shape=out_shapes, in_specs=in_specs, out_specs...  15.5 us
    ppermute x4, waiting for transfers between devices, beside(): lax.ppermute(value, 'scan', [(i, i ^ mask) for i in range(shard_count)])  11.4 us
    ppermute x7, starting transfers between devices, joint_permute(): lax.ppermute(value, tuple(names) if len(names) > 1 else names[0], route)  10.5 us
    unnamed x12, local copies, waits for them, and re-layouts  8.53 us
    ppermute x7, waiting for transfers between devices, joint_permute(): lax.ppermute(value, tuple(names) if len(names) > 1 else names[0], route)  4.44 us
    ppermute x2, starting transfers between devices, across(): lax.ppermute(value, 'scan', [(i, i ^ stride) for i in range(shard_count)])  4.17 us
    ppermute x4, starting transfers between devices, beside(): lax.ppermute(value, 'scan', [(i, i ^ mask) for i in range(shard_count)])  1.99 us
  transfers between devices with their start and end apart: 13, of which 7 were waited for; matrix products, arithmetic and copies ran while one was open for 4% of the time, Pallas kernels for 5%

profile of v2, /device:TPU:0, one launch (start us, length us, event | category | flops | bytes accessed | tf_op | source)
XLA Modules:
  0.0 75.9 jit_solution(14275403458948910752)
XLA Ops:
  0.0 4.0 %collective-permute-start = (f32[3,256,256]{2,1,0:T(8,128)}, f32[3,256,256]{2,1,0:T(8,128)S(1)}, u32[]{:S(2)}, u32[]{:S(2)}) collective-permute-start(f32[3,256,256]{2,1,0:T(8,128)} %bitcast.10), channel_id=1, source_target_pairs={{0,2},{1,3},{2,0},{3,1},{4,6},{5,7},{6,4},{7,5},{8,10},{9,11},{10,... | collective-permute-start | bytes 2359304 | tf_op jit(solution)/shard_map/ppermute | solution.py:528
  4.0 0.0 copy-start
  4.0 2.2 %copy-done = f32[2,2,512,512]{3,2,1,0:T(8,128)S(1)} copy-done((f32[2,2,512,512]{3,2,1,0:T(8,128)S(1)}, f32[2,2,512,512]{3,2,1,0:T(8,128)}, u32[]{:S(2)}) %copy-start) | copy-done | bytes 4194328
  6.2 1.4 %shard_map.82 = (f32[4,64,512]{2,1,0:T(8,128)S(1)}, f32[4,64,512]{2,1,0:T(8,128)S(1)}, f32[2,512,128]{2,1,0:T(8,128)}) custom-call(f32[4,512,512]{2,1,0:T(8,128)S(1)} %bitcast.8), custom_call_target="tpu_custom_call" | custom-call | tf_op jit(solution)/shard_map/pallas_call | solution.py:495
  7.6 0.1 collective-permute-start.3
  7.7 1.6 %collective-permute-start.1 = (f32[4,64,512]{2,1,0:T(8,128)S(1)}, f32[4,64,512]{2,1,0:T(8,128)S(1)}, u32[]{:S(2)}, u32[]{:S(2)}) collective-permute-start(f32[4,64,512]{2,1,0:T(8,128)S(1)} %get-tuple-element.31), channel_id=1, source_target_pairs={{0,8},{8,0},{16,24},{24,16},{1,9},{9,1},{17,25},{25,17},{2,10},{10... | collective-permute-start | bytes 1572872 | tf_op jit(solution)/shard_map/ppermute | solution.py:58
  9.2 0.7 collective-permute-start.2
  10.6 0.8 %reshape.21 = s32[6]{0:T(128)S(1)} reshape(s32[2,3]{1,0:T(2,128)} %bitcast.12) | data formatting | bytes 48 | tf_op jit(solution)/shard_map/reshape | solution.py:524
  11.3 0.1 pad_add_fusion._.refs_3_
  11.4 1.9 %fusion = (f32[256,256]{1,0:T(8,128)S(1)}, f32[256,256]{1,0:T(8,128)S(1)}) fusion(f32[256,256]{1,0:T(8,128)} %param.10), kind=kLoop, calls=%fused_computation.1 | loop fusion | bytes 786432 | tf_op jit(solution)/shard_map/sin | solution.py:553
  13.3 0.0 collective-permute-done.3.refs_0_
  13.3 0.0 copy-start.1
  13.3 2.2 %copy-done.1 = f32[2,2,512,512]{3,2,1,0:T(8,128)S(1)} copy-done((f32[2,2,512,512]{3,2,1,0:T(8,128)S(1)}, f32[2,2,512,512]{3,2,1,0:T(8,128)}, u32[]{:S(2)}) %copy-start.1) | copy-done | bytes 4194328
  15.5 0.0 copy-start.2
  15.5 0.9 %copy-done.2 = bf16[2,256,256]{2,1,0:T(8,128)(2,1)S(1)} copy-done((bf16[2,256,256]{2,1,0:T(8,128)(2,1)S(1)}, bf16[2,256,256]{2,1,0:T(8,128)(2,1)}, u32[]{:S(2)}) %copy-start.2) | copy-done | bytes 262168
  16.4 0.0 copy-start.3
  16.4 1.1 %copy-done.3 = f32[1,1,1,3,256,256]{5,4,3,2,1,0:T(8,128)S(1)} copy-done((f32[1,1,1,3,256,256]{5,4,3,2,1,0:T(8,128)S(1)}, f32[1,1,1,3,256,256]{5,4,3,2,1,0:T(8,128)}, u32[]{:S(2)}) %copy-start.3) | copy-done | bytes 786456
  17.6 0.0 copy-start.4
  17.6 1.0 %copy-done.4 = f32[2,256,256]{2,1,0:T(8,128)S(1)} copy-done((f32[2,256,256]{2,1,0:T(8,128)S(1)}, f32[2,256,256]{2,1,0:T(8,128)}, u32[]{:S(2)}) %copy-start.4) | copy-done | bytes 524312
  18.6 0.0 copy-start.5
  18.6 1.0 %copy-done.5 = bf16[4,256,256]{2,1,0:T(8,128)(2,1)S(1)} copy-done((bf16[4,256,256]{2,1,0:T(8,128)(2,1)S(1)}, bf16[4,256,256]{2,1,0:T(8,128)(2,1)}, u32[]{:S(2)}) %copy-start.5) | copy-done | bytes 524312
  19.6 2.4 %shard_map.83 = (f32[4,6,640,128]{3,2,1,0:T(8,128)S(1)}, f32[2,2,256,128]{3,2,1,0:T(8,128)S(1)}, f32[2,256,256]{2,1,0:T(8,128)S(1)}, bf16[4,256,256]{2,1,0:T(8,1...) custom-call(s32[8]{0:T(128)S(1)} %pad_add_fusion._.refs_3_, f32[4,512,512]{2,1,0:T(8,128)S(1)} %bitcast.9, ...), custom_call_target="tpu_custom_call" | custom-call | tf_op jit(solution)/shard_map/pallas_call | solution.py:495
  22.1 0.4 collective-permute-done.1.refs_0_
  22.5 0.0 collective-permute-done.2.refs_1_
  22.5 0.1 shard_map.84
  22.6 0.1 collective-permute-start.4
  22.7 0.1 collective-permute-start.5
  22.8 15.9 %collective-permute-done.5.refs_4_ = s32[8]{0:T(128)S(1)} collective-permute-done((s32[8]{0:T(128)S(1)}, s32[8]{0:T(128)S(1)}, u32[]{:S(2)}, u32[]{:S(2)}) %collective-permute-start.5) | collective-permute-done | bytes 64 | tf_op jit(solution)/shard_map/ppermute | solution.py:528
  38.7 0.0 collective-permute-done.4.refs_2_
  38.7 0.0 collective-permute-done.peer
  38.7 10.1 %shard_map.85 = (f32[4,6,640,128]{3,2,1,0:T(8,128)S(1)}, f32[4,2,64,128]{3,2,1,0:T(8,128)S(1)}, f32[4,1,64,128]{3,2,1,0:T(8,128)S(1)}, f32[4,1,64,128]{3,2,1,0:T...) custom-call(f32[3,256,256]{2,1,0:T(8,128)S(1)} %collective-permute-d, ...), custom_call_target="tpu_custom_call", output_to_operand_aliasing={{0}: (6, {})} | custom-call | tf_op jit(solution)/shard_map/pallas_call | solution.py:495
  48.8 0.1 collective-permute-start.9
  48.9 0.6 collective-permute-start.6
  49.5 4.4 %collective-permute-start.7 = (f32[4,2,64,128]{3,2,1,0:T(8,128)S(1)}, f32[4,2,64,128]{3,2,1,0:T(8,128)S(1)}, u32[]{:S(2)}, u32[]{:S(2)}) collective-permute-start(f32[4,2,64,128]{3,2,1,0:T(8,128)S(1)} %get-tuple-element.43), channel_id=1, source_target_pairs={{0,8},{1,9},{8,16},{9,17},{10,2},{11,3},{16,24},{17,25},{18,10},{1... | collective-permute-start | bytes 786440 | tf_op jit(solution)/shard_map/ppermute | solution.py:58
  53.9 0.0 collective-permute-done.9.refs_4_.refs_3_.refs_7_
  53.9 0.1 shard_map.87
  53.9 0.5 collective-permute-start.10
  54.4 3.6 %collective-permute-start.11 = (f32[4,2,64,128]{3,2,1,0:T(8,128)S(1)}, f32[4,2,64,128]{3,2,1,0:T(8,128)S(1)}, u32[]{:S(2)}, u32[]{:S(2)}) collective-permute-start(f32[4,2,64,128]{3,2,1,0:T(8,128)S(1)} %get-tuple-element.53), channel_id=1, source_target_pairs={{0,8},{1,9},{8,16},{9,17},{10,2},{11,3},{16,24},{17,25},{18,10},{1... | collective-permute-start | bytes 786440 | tf_op jit(solution)/shard_map/ppermute | solution.py:58
  58.1 0.0 collective-permute-done.6.refs_3_
  58.1 2.4 %collective-permute-done.7.strip.refs_5_ = f32[4,2,64,128]{3,2,1,0:T(8,128)S(1)} collective-permute-done((f32[4,2,64,128]{3,2,1,0:T(8,128)S(1)}, f32[4,2,64,128]{3,2,1,0:T(8,128)S(1)}, u32[]{:S(2)}, u32[]{:S(2)}) %collective-permute-start.7) | collective-permute-done | bytes 262176 | tf_op jit(solution)/shard_map/ppermute | solution.py:58
  60.5 0.5 collective-permute-start.8
  61.1 2.6 %collective-permute-done.10.refs_4_ = f32[4,2,64,128]{3,2,1,0:T(8,128)S(1)} collective-permute-done((f32[4,2,64,128]{3,2,1,0:T(8,128)S(1)}, f32[4,2,64,128]{3,2,1,0:T(8,128)S(1)}, u32[]{:S(2)}, u32[]{:S(2)}) %collective-permute-start.10) | collective-permute-done | bytes 262176 | tf_op jit(solution)/shard_map/ppermute | solution.py:639
  63.7 1.6 %collective-permute-done.11.refs_2_.refs_6_ = f32[4,2,64,128]{3,2,1,0:T(8,128)S(1)} collective-permute-done((f32[4,2,64,128]{3,2,1,0:T(8,128)S(1)}, f32[4,2,64,128]{3,2,1,0:T(8,128)S(1)}, u32[]{:S(2)}, u32[]{:S(2)}) %collective-permute-start.11) | collective-permute-done | bytes 262176 | tf_op jit(solution)/shard_map/ppermute | solution.py:58
  65.4 0.4 collective-permute-start.12
  65.8 4.1 %collective-permute-done.8.refs_1_ = f32[4,2,64,128]{3,2,1,0:T(8,128)S(1)} collective-permute-done((f32[4,2,64,128]{3,2,1,0:T(8,128)S(1)}, f32[4,2,64,128]{3,2,1,0:T(8,128)S(1)}, u32[]{:S(2)}, u32[]{:S(2)}) %collective-permute-start.8) | collective-permute-done | bytes 262176 | tf_op jit(solution)/shard_map/ppermute | solution.py:639
  69.8 4.7 %collective-permute-done.12.refs_2_ = f32[4,2,64,128]{3,2,1,0:T(8,128)S(1)} collective-permute-done((f32[4,2,64,128]{3,2,1,0:T(8,128)S(1)}, f32[4,2,64,128]{3,2,1,0:T(8,128)S(1)}, u32[]{:S(2)}, u32[]{:S(2)}) %collective-permute-start.12) | collective-permute-done | bytes 262176 | tf_op jit(solution)/shard_map/ppermute | solution.py:639
  74.5 1.4 %shard_map.89 = f32[4,128,512]{2,1,0:T(8,128)} custom-call(f32[4,4,128,128]{3,2,1,0:T(8,128)S(1)} %get-tuple-element.40.refs_0_, f32[4,2,64,128]{3,2,1,0:T(8,128)S(1)} %collective-permute-done.8.refs_1_, f32[4,2,64,128]{3,2,1,0:T(8,128)S(1)} %collective-permute-done.12.refs_2_, f32[4,2,64,128]{3,2,1,0:T(8,128)S(1)} %collective-permute-done.6.refs_3_, ...), custom_call_target="tpu_custom_call" | custom-call | tf_op jit(solution)/shard_map/pallas_call | solution.py:495
  (2 shorter events, 0.1 us)
Async XLA Ops:
  0.0 38.7 %collective-permute-start = (f32[3,256,256]{2,1,0:T(8,128)}, f32[3,256,256]{2,1,0:T(8,128)S(1)}, u32[]{:S(2)}, u32[]{:S(2)}) collective-permute-start(f32[3,256,256]{2,1,0:T(8,128)} %bitcast.10), channel_id=1, source_target_pairs={{0,2},{1,3},{2,0},{3,1},{4,6},{5,7},{6,4},{7,5},{8,10},{9,11},{10,... | collective-permute-start | bytes 2359304 | tf_op jit(solution)/shard_map/ppermute | solution.py:528
  4.0 2.2 %copy-start = (f32[2,2,512,512]{3,2,1,0:T(8,128)S(1)}, f32[2,2,512,512]{3,2,1,0:T(8,128)}, u32[]{:S(2)}) copy-start(f32[2,2,512,512]{3,2,1,0:T(8,128)} %param.8) | copy-start | bytes 12582916
  7.6 5.7 %collective-permute-start.3 = (f32[2,512,128]{2,1,0:T(8,128)}, f32[2,512,128]{2,1,0:T(8,128)S(1)}, u32[]{:S(2)}, u32[]{:S(2)}) collective-permute-start(f32[2,512,128]{2,1,0:T(8,128)} %get-tuple-element.33), channel_id=1, source_target_pairs={{0,4},{4,0},{1,5},{5,1},{2,6},{6,2},{3,7},{7,3},{8,12},{12,8},{9,1... | collective-permute-start | bytes 1572872 | tf_op jit(solution)/shard_map/ppermute | solution.py:58
  7.7 14.8 %collective-permute-start.1 = (f32[4,64,512]{2,1,0:T(8,128)S(1)}, f32[4,64,512]{2,1,0:T(8,128)S(1)}, u32[]{:S(2)}, u32[]{:S(2)}) collective-permute-start(f32[4,64,512]{2,1,0:T(8,128)S(1)} %get-tuple-element.31), channel_id=1, source_target_pairs={{0,8},{8,0},{16,24},{24,16},{1,9},{9,1},{17,25},{25,17},{2,10},{10... | collective-permute-start | bytes 1572872 | tf_op jit(solution)/shard_map/ppermute | solution.py:58
  9.2 13.2 %collective-permute-start.2 = (f32[4,64,512]{2,1,0:T(8,128)S(1)}, f32[4,64,512]{2,1,0:T(8,128)S(1)}, u32[]{:S(2)}, u32[]{:S(2)}) collective-permute-start(f32[4,64,512]{2,1,0:T(8,128)S(1)} %get-tuple-element.32), channel_id=1, source_target_pairs={{8,16},{16,8},{9,17},{17,9},{10,18},{18,10},{11,19},{19,11},{12,20... | collective-permute-start | bytes 1572872 | tf_op jit(solution)/shard_map/ppermute | solution.py:58
  13.3 2.2 %copy-start.1 = (f32[2,2,512,512]{3,2,1,0:T(8,128)S(1)}, f32[2,2,512,512]{3,2,1,0:T(8,128)}, u32[]{:S(2)}) copy-start(f32[2,2,512,512]{3,2,1,0:T(8,128)} %param.8) | copy-start | bytes 12582916
  15.5 0.9 %copy-start.2 = (bf16[2,256,256]{2,1,0:T(8,128)(2,1)S(1)}, bf16[2,256,256]{2,1,0:T(8,128)(2,1)}, u32[]{:S(2)}) copy-start(bf16[2,256,256]{2,1,0:T(8,128)(2,1)} %constant.11.refs_3_.refs_7_) | copy-start | bytes 786436
  16.4 1.1 %copy-start.3 = (f32[1,1,1,3,256,256]{5,4,3,2,1,0:T(8,128)S(1)}, f32[1,1,1,3,256,256]{5,4,3,2,1,0:T(8,128)}, u32[]{:S(2)}) copy-start(f32[1,1,1,3,256,256]{5,4,3,2,1,0:T(8,128)} %param.11) | copy-start | bytes 2359300
  17.6 1.0 %copy-start.4 = (f32[2,256,256]{2,1,0:T(8,128)S(1)}, f32[2,256,256]{2,1,0:T(8,128)}, u32[]{:S(2)}) copy-start(f32[2,256,256]{2,1,0:T(8,128)} %refs_4_.1) | copy-start | bytes 1572868
  18.6 1.0 %copy-start.5 = (bf16[4,256,256]{2,1,0:T(8,128)(2,1)S(1)}, bf16[4,256,256]{2,1,0:T(8,128)(2,1)}, u32[]{:S(2)}) copy-start(bf16[4,256,256]{2,1,0:T(8,128)(2,1)} %constant.12.refs_5_) | copy-start | bytes 1572868
  22.6 16.1 %collective-permute-start.4 = (f32[2,2,64,128]{3,2,1,0:T(8,128)S(1)}, f32[2,2,64,128]{3,2,1,0:T(8,128)S(1)}, u32[]{:S(2)}, u32[]{:S(2)}) collective-permute-start(f32[2,2,64,128]{3,2,1,0:T(8,128)S(1)} %shard_map.84), channel_id=1, source_target_pairs={{0,4},{4,0},{1,5},{5,1},{2,6},{6,2},{3,7},{7,3},{8,12},{12,8},{9,1... | collective-permute-start | bytes 393224 | tf_op jit(solution)/shard_map/ppermute | solution.py:58
  22.7 16.0 %collective-permute-start.5 = (s32[8]{0:T(128)S(1)}, s32[8]{0:T(128)S(1)}, u32[]{:S(2)}, u32[]{:S(2)}) collective-permute-start(s32[8]{0:T(128)S(1)} %pad_add_fusion._.refs_3_), channel_id=1, source_target_pairs={{0,2},{1,3},{2,0},{3,1},{4,6},{5,7},{6,4},{7,5},{8,10},{9,11},{10,... | collective-permute-start | bytes 104 | tf_op jit(solution)/shard_map/ppermute | solution.py:528
  48.8 5.0 %collective-permute-start.9 = (f32[4,1,320,128]{3,2,1,0:T(8,128)S(1)}, f32[4,1,320,128]{3,2,1,0:T(8,128)S(1)}, u32[]{:S(2)}, u32[]{:S(2)}) collective-permute-start(f32[4,1,320,128]{3,2,1,0:T(8,128)S(1)} %get-tuple-element.51), channel_id=1, source_target_pairs={{0,4},{4,0},{1,5},{5,1},{2,6},{6,2},{3,7},{7,3},{8,12},{12,8},{9,1... | collective-permute-start | bytes 1966088 | tf_op jit(solution)/shard_map/ppermute | solution.py:58
  48.9 9.2 %collective-permute-start.6 = (f32[4,2,64,128]{3,2,1,0:T(8,128)S(1)}, f32[4,2,64,128]{3,2,1,0:T(8,128)S(1)}, u32[]{:S(2)}, u32[]{:S(2)}) collective-permute-start(f32[4,2,64,128]{3,2,1,0:T(8,128)S(1)} %get-tuple-element.42), channel_id=1, source_target_pairs={{0,1},{1,0},{2,3},{3,2},{4,5},{5,4},{6,7},{7,6},{8,9},{9,8},{10,11... | collective-permute-start | bytes 786440 | tf_op jit(solution)/shard_map/ppermute | solution.py:639
  49.5 11.0 %collective-permute-start.7 = (f32[4,2,64,128]{3,2,1,0:T(8,128)S(1)}, f32[4,2,64,128]{3,2,1,0:T(8,128)S(1)}, u32[]{:S(2)}, u32[]{:S(2)}) collective-permute-start(f32[4,2,64,128]{3,2,1,0:T(8,128)S(1)} %get-tuple-element.43), channel_id=1, source_target_pairs={{0,8},{1,9},{8,16},{9,17},{10,2},{11,3},{16,24},{17,25},{18,10},{1... | collective-permute-start | bytes 786440 | tf_op jit(solution)/shard_map/ppermute | solution.py:58
  53.9 9.8 %collective-permute-start.10 = (f32[4,2,64,128]{3,2,1,0:T(8,128)S(1)}, f32[4,2,64,128]{3,2,1,0:T(8,128)S(1)}, u32[]{:S(2)}, u32[]{:S(2)}) collective-permute-start(f32[4,2,64,128]{3,2,1,0:T(8,128)S(1)} %get-tuple-element.52), channel_id=1, source_target_pairs={{0,1},{1,0},{2,3},{3,2},{4,5},{5,4},{6,7},{7,6},{8,9},{9,8},{10,11... | collective-permute-start | bytes 786440 | tf_op jit(solution)/shard_map/ppermute | solution.py:639
  54.4 10.9 %collective-permute-start.11 = (f32[4,2,64,128]{3,2,1,0:T(8,128)S(1)}, f32[4,2,64,128]{3,2,1,0:T(8,128)S(1)}, u32[]{:S(2)}, u32[]{:S(2)}) collective-permute-start(f32[4,2,64,128]{3,2,1,0:T(8,128)S(1)} %get-tuple-element.53), channel_id=1, source_target_pairs={{0,8},{1,9},{8,16},{9,17},{10,2},{11,3},{16,24},{17,25},{18,10},{1... | collective-permute-start | bytes 786440 | tf_op jit(solution)/shard_map/ppermute | solution.py:58
  60.5 9.3 %collective-permute-start.8 = (f32[4,2,64,128]{3,2,1,0:T(8,128)S(1)}, f32[4,2,64,128]{3,2,1,0:T(8,128)S(1)}, u32[]{:S(2)}, u32[]{:S(2)}) collective-permute-start(f32[4,2,64,128]{3,2,1,0:T(8,128)S(1)} %shard_map.86), channel_id=1, source_target_pairs={{0,1},{1,0},{2,3},{3,2},{4,5},{5,4},{6,7},{7,6},{8,9},{9,8},{10,11... | collective-permute-start | bytes 786440 | tf_op jit(solution)/shard_map/ppermute | solution.py:639
  65.4 9.1 %collective-permute-start.12 = (f32[4,2,64,128]{3,2,1,0:T(8,128)S(1)}, f32[4,2,64,128]{3,2,1,0:T(8,128)S(1)}, u32[]{:S(2)}, u32[]{:S(2)}) collective-permute-start(f32[4,2,64,128]{3,2,1,0:T(8,128)S(1)} %shard_map.88), channel_id=1, source_target_pairs={{0,1},{1,0},{2,3},{3,2},{4,5},{5,4},{6,7},{7,6},{8,9},{9,8},{10,11... | collective-permute-start | bytes 786440 | tf_op jit(solution)/shard_map/ppermute | solution.py:639

commit v3 on v2

--- a/solution.py
+++ b/solution.py
@@ -17,6 +17,7 @@
 VMEM_LIMIT = 32 * 1024 * 1024
 VMEM_LITTLE = 8 * 1024 * 1024
 GROUP = 4
+ROWS = 16
 
 
 def block_tables():
@@ -62,66 +63,13 @@
 
 
 def times(a, b):
-    return jnp.dot(
-        a.astype(jnp.bfloat16), b.astype(jnp.bfloat16), preferred_element_type=jnp.float32
-    )
+    return jnp.dot(a, b, preferred_element_type=jnp.float32)
 
 
 def side(parts, axis):
     return jnp.concatenate(parts, axis=axis)
 
 
-def to_frequencies(pairs, tables):
-    tall = []
-    for odd in range(2):
-        halves = [
-            [x[:HALF] - x[HALF:] if odd else x[:HALF] + x[HALF:] for x in pair] for pair in pairs
-        ]
-        tall.append(times(tables[odd], side([side(half, 0) for half in halves], 1)))
-    wide = []
-    for odd in range(2):
-        rows = []
-        for i in range(len(pairs)):
-            first, second = 2 * i * HALF, (2 * i + 1) * HALF
-            for y in tall:
-                parts = []
-                for part in range(2):
-                    x = y[part * HALF : (part + 1) * HALF]
-                    low, high = x[:, first:second], x[:, second : second + HALF]
-                    parts.append(low - high if odd else low + high)
-                rows.append(side(parts, 1))
-        wide.append(times(side(rows, 0), tables[2 + odd]))
-    return [
-        [(z[i * PATCH : (i + 1) * PATCH, :HALF], z[i * PATCH : (i + 1) * PATCH, HALF:]) for z in wide]
-        for i in range(len(pairs))
-    ]
-
-
-def from_frequencies(spectra, tables):
-    parts = []
-    for odd in range(2):
-        rows = slice(odd * HALF, (odd + 1) * HALF)
-        columns = [side([x[rows] for x in pair], 0) for spectrum in spectra for pair in spectrum]
-        parts.append(times(tables[2 + odd], side(columns, 1)))
-    halves = [parts[0] + parts[1], parts[0] - parts[1]]
-    sums = []
-    for odd in range(2):
-        rows = []
-        for i in range(len(spectra)):
-            at = (2 * i + odd) * HALF
-            for half in halves:
-                rows.append(side([half[:HALF, at : at + HALF], half[HALF:, at : at + HALF]], 1))
-        sums.append(times(side(rows, 0), tables[odd]))
-    low, high = sums[0] + sums[1], sums[0] - sums[1]
-    results = []
-    for i in range(len(spectra)):
-        rows = slice(i * PATCH, (i + 1) * PATCH)
-        results.append(
-            tuple(side([x[rows, p * HALF : (p + 1) * HALF] for x in (low, high)], 1) for p in range(2))
-        )
-    return results
-
-
 def product(a, b):
     return a[0] * b[0] - a[1] * b[1], a[0] * b[1] + a[1] * b[0]
 
@@ -130,65 +78,216 @@
     return a[0] * b[0] + a[1] * b[1], a[0] * b[1] - a[1] * b[0]
 
 
-def lanes():
-    return lax.broadcasted_iota(jnp.int32, (PATCH, LANE), 1)
+def by_lanes(multiply, a, b):
+    pairs = [multiply([x[k] for x in a], [x[k] for x in b]) for k in range(2)]
+    return [[pair[part] for pair in pairs] for part in range(2)]
+
+
+def at_rows(start, count=ROWS):
+    return slice(start, start + count)
+
+
+def at_lanes(tile):
+    return slice(tile * LANE, (tile + 1) * LANE)
 
 
 def corner_of(row, col):
     return row + HALO, (col + LANE) // LANE, lax.rem(col + LANE, LANE)
 
 
-def window(ext, slice_at, row, col):
-    top, tile, shift = corner_of(row, col)
-    turn = lax.rem(LANE - shift, LANE)
-    inside = lanes() < LANE - shift
-
-    def plane(index):
-        moved = [
-            pltpu.roll(ext[index, tile + j, pl.ds(top, PATCH), :], turn, 1) for j in range(3)
-        ]
-        return jnp.concatenate([jnp.where(inside, moved[j], moved[j + 1]) for j in range(2)], axis=1)
-
-    return plane(2 * slice_at), plane(2 * slice_at + 1)
-
-
-def deposit(acc, slice_at, row, col, pair):
-    top, tile, shift = corner_of(row, col)
-    inside = lanes() >= shift
-    blank = jnp.zeros((PATCH, LANE), jnp.float32)
+class Patches:
+    def __init__(self, x, y, p, z, near, far, tables):
+        self.x, self.y, self.p, self.z, self.tables = x, y, p, z, tables
+        self.near, self.far, self.count = near, far, near.shape[0]
+        self.lane = lax.broadcasted_iota(jnp.int32, (ROWS, LANE), 1)
+
+    def window(self, ext, slice_at, corner, start):
+        top, tile, shift = corner_of(*corner)
+        turn, inside = lax.rem(LANE - shift, LANE), self.lane < LANE - shift
+        rows = pl.ds(top + start, ROWS)
+        parts = []
+        for plane in (2 * slice_at, 2 * slice_at + 1):
+            moved = [pltpu.roll(ext[plane, tile + j, rows, :], turn, 1) for j in range(3)]
+            parts.append([jnp.where(inside, moved[j], moved[j + 1]) for j in range(2)])
+        return parts
+
+    def deposit(self, acc, slice_at, corner, start, block, live):
+        top, tile, shift = corner_of(*corner)
+        inside, rows = self.lane >= shift, pl.ds(top + start, ROWS)
+        for part in range(2):
+            moved = [pltpu.roll(jnp.where(live, b, 0.0), shift, 1) for b in block[part]]
+            sums = [
+                jnp.where(inside, moved[0], 0.0),
+                jnp.where(inside, moved[1], moved[0]),
+                jnp.where(inside, 0.0, moved[1]),
+            ]
+            for j in range(3):
+                acc[2 * slice_at + part, tile + j, rows, :] += sums[j]
+
+    def fill(self, i, row, blocks):
+        for part in range(2):
+            for k in range(2):
+                low, high = blocks[0][part][k], blocks[1][part][k]
+                rows, lanes = at_rows(part * HALF + row), at_lanes(2 * i + k)
+                self.x[0, rows, lanes] = (low + high).astype(jnp.bfloat16)
+                self.x[1, rows, lanes] = (low - high).astype(jnp.bfloat16)
+
+    def multiply_left(self, *tables):
+        for odd, table in enumerate(tables):
+            for i in range(self.count):
+                part = slice(i * PATCH, (i + 1) * PATCH)
+                self.y[odd, :, part] = times(table, self.x[odd, :, part])
+            yield
+
+    def multiply_right(self, *tables):
+        for odd, table in enumerate(tables):
+            self.z[odd] = times(self.p[odd], table)
+            yield
+
+    def to_frequencies(self):
+        yield from self.multiply_left(self.tables[0], self.tables[1])
+        for i in range(self.count):
+            for a in range(2):
+                for row in range(0, HALF, ROWS):
+                    for part in range(2):
+                        rows = at_rows(part * HALF + row)
+                        low, high = [self.y[a, rows, at_lanes(2 * i + k)] for k in range(2)]
+                        rows = at_rows((2 * i + a) * HALF + row)
+                        self.p[0, rows, at_lanes(part)] = (low + high).astype(jnp.bfloat16)
+                        self.p[1, rows, at_lanes(part)] = (low - high).astype(jnp.bfloat16)
+            yield
+        yield from self.multiply_right(self.tables[2], self.tables[3])
+
+    def change(self, function):
+        for i in range(self.count):
+            for a in range(2):
+                for row in range(0, HALF, ROWS):
+                    rows = at_rows((2 * i + a) * HALF + row)
+                    for b in range(2):
+                        value = [self.z[b, rows, at_lanes(part)] for part in range(2)]
+                        result = function(i, b, a * HALF + row, value)
+                        for part in range(2):
+                            to = at_rows(part * HALF + row)
+                            self.x[a, to, at_lanes(2 * i + b)] = result[part].astype(jnp.bfloat16)
+            yield
+
+    def from_frequencies(self):
+        yield from self.multiply_left(self.tables[2], self.tables[3])
+        for i in range(self.count):
+            for b in range(2):
+                for row in range(0, HALF, ROWS):
+                    for part in range(2):
+                        rows = at_rows(part * HALF + row)
+                        even, odd = [self.y[a, rows, at_lanes(2 * i + b)] for a in range(2)]
+                        rows = [at_rows((2 * i + half) * HALF + row) for half in range(2)]
+                        self.p[b, rows[0], at_lanes(part)] = (even + odd).astype(jnp.bfloat16)
+                        self.p[b, rows[1], at_lanes(part)] = (even - odd).astype(jnp.bfloat16)
+            yield
+        yield from self.multiply_right(self.tables[0], self.tables[1])
+
+    def result(self, i, half, row):
+        rows, parts = at_rows((2 * i + half) * HALF + row), []
+        for part in range(2):
+            even, odd = [self.z[b, rows, at_lanes(part)] for b in range(2)]
+            parts.append([even + odd, even - odd])
+        return parts
+
+    def last(self, row):
+        return row + ROWS == HALF
+
+    def blocks(self):
+        return [(i, row) for i in range(self.count) for row in range(0, HALF, ROWS)]
+
+
+def block_of(ref, i, half, row):
+    rows = at_rows(half * HALF + row)
+    return [[ref[i, part, rows, at_lanes(k)] for k in range(2)] for part in range(2)]
+
+
+def keep_block(ref, i, half, row, block):
+    rows = at_rows(half * HALF + row)
     for part in range(2):
-        moved = [
-            pltpu.roll(pair[part][:, j * LANE : (j + 1) * LANE], shift, 1) for j in range(2)
-        ]
-        moved = [blank, *moved, blank]
-        for j in range(3):
-            acc[2 * slice_at + part, tile + j, pl.ds(top, PATCH), :] += jnp.where(
-                inside, moved[j + 1], moved[j]
-            )
-
-
-def patch_gradients(ext, corners, intensities, probe, waves, tables, put):
-    lamp = (probe[0], probe[1])
-    prop = [(waves[0, odd], waves[1, odd]) for odd in range(2)]
-
-    def through_prop(multiply, spectra):
-        return [[multiply(h, z) for h, z in zip(prop, spectrum)] for spectrum in spectra]
-
-    entrance = [product(lamp, window(ext, 0, *corner)) for corner in corners]
-    arrived = from_frequencies(through_prop(product, to_frequencies(entrance, tables)), tables)
-    seconds = [window(ext, 1, *corner) for corner in corners]
-    far = to_frequencies([product(o, w) for o, w in zip(seconds, arrived)], tables)
-    residuals = []
-    for spectrum, intensity in zip(far, intensities):
-        misfits = [z[0] * z[0] + z[1] * z[1] - i for z, i in zip(spectrum, intensity)]
-        residuals.append([(m * z[0], m * z[1]) for m, z in zip(misfits, spectrum)])
-    back_seconds = from_frequencies(residuals, tables)
-    for i, (w, g) in enumerate(zip(arrived, back_seconds)):
-        put(i, 1, conj_product(w, g))
-    through = [conj_product(o, g) for o, g in zip(seconds, back_seconds)]
-    back_spectra = through_prop(conj_product, to_frequencies(through, tables))
-    for i, g in enumerate(from_frequencies(back_spectra, tables)):
-        put(i, 0, conj_product(lamp, g))
+        for k in range(2):
+            ref[i, part, rows, at_lanes(k)] = block[part][k]
+
+
+def patch_gradients(patches, ext, acc, corners, lives, intensity, probe, waves):
+    near, far = patches.near, patches.far
+
+    def lamp(half, row):
+        rows = at_rows(half * HALF + row)
+        return [[probe[part, rows, at_lanes(k)] for k in range(2)] for part in range(2)]
+
+    def prop(b, row):
+        return [waves[part, b, at_rows(row), :] for part in range(2)]
+
+    for i, row in patches.blocks():
+        patches.fill(
+            i,
+            row,
+            [
+                by_lanes(
+                    product, lamp(half, row), patches.window(ext, 0, corners[i], half * HALF + row)
+                )
+                for half in range(2)
+            ],
+        )
+        if patches.last(row):
+            yield
+    yield from patches.to_frequencies()
+    yield from patches.change(lambda i, b, row, z: product(prop(b, row), z))
+    yield from patches.from_frequencies()
+    for i, row in patches.blocks():
+        leaving = []
+        for half in range(2):
+            arrived = patches.result(i, half, row)
+            second = patches.window(ext, 1, corners[i], half * HALF + row)
+            keep_block(near, i, half, row, arrived)
+            keep_block(far, i, half, row, second)
+            leaving.append(by_lanes(product, second, arrived))
+        patches.fill(i, row, leaving)
+        if patches.last(row):
+            yield
+    yield from patches.to_frequencies()
+
+    def residual(i, b, row, z):
+        misfit = z[0] * z[0] + z[1] * z[1] - intensity[at_rows(i * PATCH + row), at_lanes(b)]
+        return misfit * z[0], misfit * z[1]
+
+    yield from patches.change(residual)
+    yield from patches.from_frequencies()
+    for i, row in patches.blocks():
+        through = []
+        for half in range(2):
+            back = patches.result(i, half, row)
+            start = half * HALF + row
+            grad = by_lanes(conj_product, block_of(near, i, half, row), back)
+            patches.deposit(acc, 1, corners[i], start, grad, lives[i])
+            through.append(by_lanes(conj_product, block_of(far, i, half, row), back))
+        patches.fill(i, row, through)
+        if patches.last(row):
+            yield
+    yield from patches.to_frequencies()
+    yield from patches.change(lambda i, b, row, z: conj_product(prop(b, row), z))
+    yield from patches.from_frequencies()
+    for i, row in patches.blocks():
+        for half in range(2):
+            grad = by_lanes(conj_product, lamp(half, row), patches.result(i, half, row))
+            patches.deposit(acc, 0, corners[i], half * HALF + row, grad, lives[i])
+        if patches.last(row):
+            yield
+
+
+def in_turns(first, second):
+    for _ in range(GROUP // 2):
+        next(first)
+    going = [first, second]
+    while going:
+        for group in list(going):
+            try:
+                next(group)
+            except StopIteration:
+                going.remove(group)
 
 
 def place_of(height):
@@ -267,7 +366,8 @@
     row_refs, refs = refs[: sides[0]], refs[sides[0] :]
     corner_refs, refs = refs[: sides[1]], refs[sides[1] :]
     own_info, peer_info, ext, own, probe, waves, tables, order = refs[:8]
-    outs, (acc, queue, sems) = refs[9:-3], refs[-3:]
+    outs, (acc, queue, *scratch, ordered, sems) = refs[9:-16], refs[-16:]
+    groups = [Patches(*scratch[:6], tables), Patches(*scratch[6:], tables)]
     tiles, height = ext.shape[1], ext.shape[2] - 2 * HALO
     half_rows = height // 2
     place = place_of(height)
@@ -310,17 +410,18 @@
         start = GROUP * turn_at
         items = [start] + [jnp.minimum(start + i, length - 1) for i in range(1, GROUP)]
         corners = [(queue[3 * i + 1], queue[3 * i + 2]) for i in items]
-        ordered = sort_frequencies([intensity(queue[3 * i]) for i in items], order)
-        rows = [ordered[i * PATCH : (i + 1) * PATCH] for i in range(GROUP)]
-        intensities = [(x[:, :HALF], x[:, HALF:]) for x in rows]
-
-        def put(i, slice_at, pair):
-            if i == 0:
-                deposit(acc, slice_at, *corners[i], pair)
-            else:
-                pl.when(start + i < length)(lambda: deposit(acc, slice_at, *corners[i], pair))
-
-        patch_gradients(ext, corners, intensities, probe, waves, tables, put)
+        lives = [start + i < length for i in range(GROUP)]
+        ordered[...] = sort_frequencies([intensity(queue[3 * i]) for i in items], order)
+        steps = []
+        for k, patches in enumerate(groups):
+            part = slice(k * patches.count, (k + 1) * patches.count)
+            intensities = ordered.at[pl.ds(k * patches.count * PATCH, patches.count * PATCH)]
+            steps.append(
+                patch_gradients(
+                    patches, ext, acc, corners[part], lives[part], intensities, probe, waves
+                )
+            )
+        in_turns(*steps)
         return carry
 
     lax.fori_loop(0, (length + GROUP - 1) // GROUP, step, 0)
@@ -382,30 +483,45 @@
         out[...] += strip[...]
 
 
-def final_kernel(height, sides, part, *refs):
+def gather_kernel(height, sides, part, *refs):
     place = place_of(height)
-    shut_got, open_got, strip, rims = refs[:2], refs[2:4], refs[4:6], refs[6 : 6 + sides]
-    out, work = refs[6 + sides :]
+    shut_got, open_got, strip, rims = refs[0], refs[1:3], refs[3:5], refs[5 : 5 + sides]
+    out, edge_out, work = refs[5 + sides :]
     work[...] = part[...]
     tiles = work.shape[1]
     add_rims(place, work, rims, pl.multiple_of(place[4], 8))
 
-    def add(at, inner, edge):
+    def add(at, inner, edge=None):
         rows = pl.ds(pl.multiple_of(at, 8), inner.shape[2])
         split = 1 + inner.shape[1]
         work[:, 1:split, rows, :] += inner[...]
-        work[:, 0:1, rows, :] += edge[:, 0:1]
-        work[:, split:, rows, :] += edge[:, 1:]
+        if edge is not None:
+            work[:, 0:1, rows, :] += edge[:, 0:1]
+            work[:, split:, rows, :] += edge[:, 1:]
 
     add(place[9], *open_got)
-    add(place[8], *shut_got)
+    add(place[8], shut_got)
 
     @pl.when(place[7] == 1)
     def _():
         add(place[8], *strip)
 
+    shut_rows = pl.ds(pl.multiple_of(place[8], 8), HALO)
+    edge_out[:, 0:1] = work[:, 0:1, shut_rows, :]
+    edge_out[:, 1:2] = work[:, tiles - 1 :, shut_rows, :]
     for t in range(tiles):
         out[:, :, t * LANE : (t + 1) * LANE] = work[:, t]
+
+
+def last_kernel(height, total, edge, got, out, work, sems):
+    place = place_of(height)
+    rows = pl.ds(pl.multiple_of(place[8], 8), HALO)
+    work[...] = edge[...] + got[...]
+    copies = Copies(sems)
+    for k in range(2):
+        lanes = pl.ds(k * (out.shape[2] - LANE), LANE)
+        copies.start(work.at[:, k], out.at[:, rows, lanes])
+    copies.wait()
 
 
 def half_kernel(height, sides, part, inner, edge, *refs):
@@ -434,7 +550,7 @@
     for _ in range(3):
         part = values.astype(jnp.bfloat16)
         values = values - part.astype(jnp.float32)
-        rows = times(order[1], part)
+        rows = times(order[1], part).astype(jnp.bfloat16)
         rows = side([rows[:, i * PATCH : (i + 1) * PATCH] for i in range(len(arrays))], 0)
         moved = times(rows, order[0])
         total = moved if total is None else total + moved
@@ -614,6 +730,19 @@
         [
             pltpu.VMEM(full, jnp.float32),
             pltpu.SMEM((3 * (2 * PMAX + 1),), jnp.int32),
+            *[
+                pltpu.VMEM(shape, dtype)
+                for _ in range(2)
+                for shape, dtype in (
+                    ((2, PATCH, GROUP // 2 * PATCH), jnp.bfloat16),
+                    ((2, PATCH, GROUP // 2 * PATCH), jnp.float32),
+                    ((2, GROUP // 2 * PATCH, PATCH), jnp.bfloat16),
+                    ((2, GROUP // 2 * PATCH, PATCH), jnp.float32),
+                    ((GROUP // 2, 2, PATCH, PATCH), jnp.float32),
+                    ((GROUP // 2, 2, PATCH, PATCH), jnp.float32),
+                )
+            ],
+            pltpu.VMEM((GROUP * PATCH, PATCH), jnp.float32),
             pltpu.SemaphoreType.DMA((copy_count,)),
         ],
         *arrivals,
@@ -697,16 +826,28 @@
         *got_rims,
     )
     got_shut.append(beside(shut_edge))
-    total = fold(
-        lambda *refs: final_kernel(refs[0], sides, *refs[1:]),
-        block(4, band, width),
+    bulk, shut_rest = fold(
+        lambda *refs: gather_kernel(refs[0], sides, *refs[1:]),
+        (block(4, band, width), block(4, 2, HALO, LANE)),
         pieces[6],
-        *got_shut,
+        got_shut[0],
         *got_open,
         got_inner,
         got_edge,
         *got_rims,
         scratch=[pltpu.VMEM((4, tiles, band, LANE), jnp.float32)],
+    )
+    total = call(
+        functools.partial(last_kernel, height),
+        block(4, band, width),
+        [ANY, VMEM, VMEM],
+        ANY,
+        [pltpu.VMEM((4, 2, HALO, LANE), jnp.float32), pltpu.SemaphoreType.DMA((2,))],
+        bulk,
+        shut_rest,
+        got_shut[1],
+        limit=VMEM_LITTLE,
+        aliases={0: 0},
     )
     return total.reshape(2, 2, band, width)
 

time: 76.2 us -> 74.6 us (0.979)
  waiting for transfers between devices: 31.7 us -> 30.5 us
    ppermute x4, waiting for transfers between devices: 11.4 us -> 9.29 us  [beside(): lax.ppermute(value, 'scan', [(i, i ^ mask) for i in range(shard_count)])]
    ppermute x7, waiting for transfers between devices: 4.44 us -> 5.3 us  [joint_permute(): lax.ppermute(value, tuple(names) if len(names) > 1 else names[0], route)]
    pallas_call x8 -> x9, Pallas kernels: 15.5 us -> 15.2 us  [call(): pl.pallas_call(kernel, out_shape=out_shapes, in_specs=in_specs, out_specs...]
  transfers between devices with their start and end apart: 13 -> 13, of which waited for: 7 -> 7; matrix products, arithmetic and copies ran while one was open for 4% -> 4% of each run, Pallas kernels for 5% -> 7%
where the time goes in v3:
time: 74.6 us; the launch traced here: 74.2 us
  waiting for transfers between devices  30.5 us (41%)
  starting transfers between devices  16.5 us (22%)
  Pallas kernels  15.2 us (20%)
  local copies, waits for them, and re-layouts  11.2 us (15%)
  between operations  0.8 us (1%)
    ppermute x2, waiting for transfers between devices, across(): lax.ppermute(value, 'scan', [(i, i ^ stride) for i in range(shard_count)])  15.9 us
    pallas_call x9, Pallas kernels, call(): pl.pallas_call(kernel, out_shape=out_shapes, in_specs=in_specs, out_specs...  15.2 us
    ppermute x7, starting transfers between devices, joint_permute(): lax.ppermute(value, tuple(names) if len(names) > 1 else names[0], route)  10.2 us
    ppermute x4, waiting for transfers between devices, beside(): lax.ppermute(value, 'scan', [(i, i ^ mask) for i in range(shard_count)])  9.29 us
    unnamed x12, local copies, waits for them, and re-layouts  8.53 us
    ppermute x7, waiting for transfers between devices, joint_permute(): lax.ppermute(value, tuple(names) if len(names) > 1 else names[0], route)  5.3 us
    ppermute x2, starting transfers between devices, across(): lax.ppermute(value, 'scan', [(i, i ^ stride) for i in range(shard_count)])  4.17 us
    ppermute x4, starting transfers between devices, beside(): lax.ppermute(value, 'scan', [(i, i ^ mask) for i in range(shard_count)])  2.15 us
  transfers between devices with their start and end apart: 13, of which 7 were waited for; matrix products, arithmetic and copies ran while one was open for 4% of the time, Pallas kernels for 7%

profile of v3, /device:TPU:0, one launch (start us, length us, event | category | flops | bytes accessed | tf_op | source)
XLA Modules:
  0.0 74.2 jit_solution(13188686155372278693)
XLA Ops:
  0.0 4.0 %collective-permute-start = (f32[3,256,256]{2,1,0:T(8,128)}, f32[3,256,256]{2,1,0:T(8,128)S(1)}, u32[]{:S(2)}, u32[]{:S(2)}) collective-permute-start(f32[3,256,256]{2,1,0:T(8,128)} %bitcast.10), channel_id=1, source_target_pairs={{0,2},{1,3},{2,0},{3,1},{4,6},{5,7},{6,4},{7,5},{8,10},{9,11},{10,... | collective-permute-start | bytes 2359304 | tf_op jit(solution)/shard_map/ppermute | solution.py:644
  4.0 0.0 copy-start
  4.0 2.2 %copy-done = f32[2,2,512,512]{3,2,1,0:T(8,128)S(1)} copy-done((f32[2,2,512,512]{3,2,1,0:T(8,128)S(1)}, f32[2,2,512,512]{3,2,1,0:T(8,128)}, u32[]{:S(2)}) %copy-start) | copy-done | bytes 4194328
  6.2 1.4 %shard_map.82 = (f32[4,64,512]{2,1,0:T(8,128)S(1)}, f32[4,64,512]{2,1,0:T(8,128)S(1)}, f32[2,512,128]{2,1,0:T(8,128)}) custom-call(f32[4,512,512]{2,1,0:T(8,128)S(1)} %bitcast.8), custom_call_target="tpu_custom_call" | custom-call | tf_op jit(solution)/shard_map/pallas_call | solution.py:611
  7.6 0.1 collective-permute-start.3
  7.7 1.6 %collective-permute-start.1 = (f32[4,64,512]{2,1,0:T(8,128)S(1)}, f32[4,64,512]{2,1,0:T(8,128)S(1)}, u32[]{:S(2)}, u32[]{:S(2)}) collective-permute-start(f32[4,64,512]{2,1,0:T(8,128)S(1)} %get-tuple-element.33), channel_id=1, source_target_pairs={{0,8},{8,0},{16,24},{24,16},{1,9},{9,1},{17,25},{25,17},{2,10},{10... | collective-permute-start | bytes 1572872 | tf_op jit(solution)/shard_map/ppermute | solution.py:59
  9.2 0.7 collective-permute-start.2
  10.6 0.8 %reshape.21 = s32[6]{0:T(128)S(1)} reshape(s32[2,3]{1,0:T(2,128)} %bitcast.12) | data formatting | bytes 48 | tf_op jit(solution)/shard_map/reshape | solution.py:640
  11.3 0.1 pad_add_fusion._.refs_3_
  11.4 1.9 %fusion = (f32[256,256]{1,0:T(8,128)S(1)}, f32[256,256]{1,0:T(8,128)S(1)}) fusion(f32[256,256]{1,0:T(8,128)} %param.10), kind=kLoop, calls=%fused_computation.1 | loop fusion | bytes 786432 | tf_op jit(solution)/shard_map/sin | solution.py:669
  13.3 0.0 collective-permute-done.3.refs_0_
  13.3 0.0 copy-start.1
  13.3 2.2 %copy-done.1 = f32[2,2,512,512]{3,2,1,0:T(8,128)S(1)} copy-done((f32[2,2,512,512]{3,2,1,0:T(8,128)S(1)}, f32[2,2,512,512]{3,2,1,0:T(8,128)}, u32[]{:S(2)}) %copy-start.1) | copy-done | bytes 4194328
  15.5 0.0 copy-start.2
  15.5 0.9 %copy-done.2 = bf16[2,256,256]{2,1,0:T(8,128)(2,1)S(1)} copy-done((bf16[2,256,256]{2,1,0:T(8,128)(2,1)S(1)}, bf16[2,256,256]{2,1,0:T(8,128)(2,1)}, u32[]{:S(2)}) %copy-start.2) | copy-done | bytes 262168
  16.4 0.0 copy-start.3
  16.4 1.1 %copy-done.3 = f32[1,1,1,3,256,256]{5,4,3,2,1,0:T(8,128)S(1)} copy-done((f32[1,1,1,3,256,256]{5,4,3,2,1,0:T(8,128)S(1)}, f32[1,1,1,3,256,256]{5,4,3,2,1,0:T(8,128)}, u32[]{:S(2)}) %copy-start.3) | copy-done | bytes 786456
  17.6 0.0 copy-start.4
  17.6 1.0 %copy-done.4 = f32[2,256,256]{2,1,0:T(8,128)S(1)} copy-done((f32[2,256,256]{2,1,0:T(8,128)S(1)}, f32[2,256,256]{2,1,0:T(8,128)}, u32[]{:S(2)}) %copy-start.4) | copy-done | bytes 524312
  18.6 0.0 copy-start.5
  18.6 1.0 %copy-done.5 = bf16[4,256,256]{2,1,0:T(8,128)(2,1)S(1)} copy-done((bf16[4,256,256]{2,1,0:T(8,128)(2,1)S(1)}, bf16[4,256,256]{2,1,0:T(8,128)(2,1)}, u32[]{:S(2)}) %copy-start.5) | copy-done | bytes 524312
  19.6 2.4 %shard_map.83 = (f32[4,6,640,128]{3,2,1,0:T(8,128)S(1)}, f32[2,2,256,128]{3,2,1,0:T(8,128)S(1)}, f32[2,256,256]{2,1,0:T(8,128)S(1)}, bf16[4,256,256]{2,1,0:T(8,1...) custom-call(s32[8]{0:T(128)S(1)} %pad_add_fusion._.refs_3_, f32[4,512,512]{2,1,0:T(8,128)S(1)} %bitcast.9, ...), custom_call_target="tpu_custom_call" | custom-call | tf_op jit(solution)/shard_map/pallas_call | solution.py:611
  22.1 0.4 collective-permute-done.1.refs_0_
  22.5 0.0 collective-permute-done.2.refs_1_
  22.5 0.1 shard_map.84
  22.6 0.1 collective-permute-start.4
  22.7 0.1 collective-permute-start.5
  22.8 15.9 %collective-permute-done.5.refs_4_ = s32[8]{0:T(128)S(1)} collective-permute-done((s32[8]{0:T(128)S(1)}, s32[8]{0:T(128)S(1)}, u32[]{:S(2)}, u32[]{:S(2)}) %collective-permute-start.5) | collective-permute-done | bytes 64 | tf_op jit(solution)/shard_map/ppermute | solution.py:644
  38.7 0.0 collective-permute-done.4.refs_2_
  38.7 0.0 collective-permute-done.peer
  38.7 9.1 %shard_map.85 = (f32[4,6,640,128]{3,2,1,0:T(8,128)S(1)}, f32[4,2,64,128]{3,2,1,0:T(8,128)S(1)}, f32[4,1,64,128]{3,2,1,0:T(8,128)S(1)}, f32[4,1,64,128]{3,2,1,0:T...) custom-call(f32[3,256,256]{2,1,0:T(8,128)S(1)} %collective-permute-d, ...), custom_call_target="tpu_custom_call", output_to_operand_aliasing={{0}: (6, {})} | custom-call | tf_op jit(solution)/shard_map/pallas_call | solution.py:611
  47.8 0.1 collective-permute-start.9
  47.9 1.0 %collective-permute-start.6 = (f32[4,2,64,128]{3,2,1,0:T(8,128)S(1)}, f32[4,2,64,128]{3,2,1,0:T(8,128)S(1)}, u32[]{:S(2)}, u32[]{:S(2)}) collective-permute-start(f32[4,2,64,128]{3,2,1,0:T(8,128)S(1)} %get-tuple-element.44), channel_id=1, source_target_pairs={{0,1},{1,0},{2,3},{3,2},{4,5},{5,4},{6,7},{7,6},{8,9},{9,8},{10,11... | collective-permute-start | bytes 786440 | tf_op jit(solution)/shard_map/ppermute | solution.py:768
  48.9 4.4 %collective-permute-start.7 = (f32[4,2,64,128]{3,2,1,0:T(8,128)S(1)}, f32[4,2,64,128]{3,2,1,0:T(8,128)S(1)}, u32[]{:S(2)}, u32[]{:S(2)}) collective-permute-start(f32[4,2,64,128]{3,2,1,0:T(8,128)S(1)} %get-tuple-element.45), channel_id=1, source_target_pairs={{0,8},{1,9},{8,16},{9,17},{10,2},{11,3},{16,24},{17,25},{18,10},{1... | collective-permute-start | bytes 786440 | tf_op jit(solution)/shard_map/ppermute | solution.py:59
  53.3 0.0 collective-permute-done.9.refs_4_.refs_6_.refs_3_
  53.3 0.1 shard_map.87
  53.3 0.4 collective-permute-start.10
  53.7 3.3 %collective-permute-start.11 = (f32[4,2,64,128]{3,2,1,0:T(8,128)S(1)}, f32[4,2,64,128]{3,2,1,0:T(8,128)S(1)}, u32[]{:S(2)}, u32[]{:S(2)}) collective-permute-start(f32[4,2,64,128]{3,2,1,0:T(8,128)S(1)} %get-tuple-element.54), channel_id=1, source_target_pairs={{0,8},{1,9},{8,16},{9,17},{10,2},{11,3},{16,24},{17,25},{18,10},{1... | collective-permute-start | bytes 786440 | tf_op jit(solution)/shard_map/ppermute | solution.py:59
  57.1 0.0 collective-permute-done.6.refs_2_
  57.1 2.8 %collective-permute-done.7.strip.refs_4_ = f32[4,2,64,128]{3,2,1,0:T(8,128)S(1)} collective-permute-done((f32[4,2,64,128]{3,2,1,0:T(8,128)S(1)}, f32[4,2,64,128]{3,2,1,0:T(8,128)S(1)}, u32[]{:S(2)}, u32[]{:S(2)}) %collective-permute-start.7) | collective-permute-done | bytes 262176 | tf_op jit(solution)/shard_map/ppermute | solution.py:59
  59.9 0.4 collective-permute-start.8
  60.3 2.4 %collective-permute-done.10.refs_3_ = f32[4,2,64,128]{3,2,1,0:T(8,128)S(1)} collective-permute-done((f32[4,2,64,128]{3,2,1,0:T(8,128)S(1)}, f32[4,2,64,128]{3,2,1,0:T(8,128)S(1)}, u32[]{:S(2)}, u32[]{:S(2)}) %collective-permute-start.10) | collective-permute-done | bytes 262176 | tf_op jit(solution)/shard_map/ppermute | solution.py:768
  62.7 2.1 %collective-permute-done.11.refs_5_.refs_2_ = f32[4,2,64,128]{3,2,1,0:T(8,128)S(1)} collective-permute-done((f32[4,2,64,128]{3,2,1,0:T(8,128)S(1)}, f32[4,2,64,128]{3,2,1,0:T(8,128)S(1)}, u32[]{:S(2)}, u32[]{:S(2)}) %collective-permute-start.11) | collective-permute-done | bytes 262176 | tf_op jit(solution)/shard_map/ppermute | solution.py:59
  64.8 0.4 collective-permute-start.12
  65.2 3.7 %collective-permute-done.8.refs_1_ = f32[4,2,64,128]{3,2,1,0:T(8,128)S(1)} collective-permute-done((f32[4,2,64,128]{3,2,1,0:T(8,128)S(1)}, f32[4,2,64,128]{3,2,1,0:T(8,128)S(1)}, u32[]{:S(2)}, u32[]{:S(2)}) %collective-permute-start.8) | collective-permute-done | bytes 262176 | tf_op jit(solution)/shard_map/ppermute | solution.py:768
  68.8 1.4 %shard_map.88 = (f32[4,128,512]{2,1,0:T(8,128)}, f32[4,2,64,128]{3,2,1,0:T(8,128)S(1)}) custom-call(f32[4,4,128,128]{3,2,1,0:T(8,128)S(1)} %get-tuple-element.42.refs_0_, f32[4,2,64,128]{3,2,1,0:T(8,128)S(1)} %collective-permute-done.8.refs_1_, f32[4,2,64,128]{3,2,1,0:T(8,128)S(1)} %collective-permute-done.6.refs_2_, ...), custom_call_target="tpu_custom_call" | custom-call | tf_op jit(solution)/shard_map/pallas_call | solution.py:611
  70.2 3.3 %collective-permute-done.12.got = f32[4,2,64,128]{3,2,1,0:T(8,128)S(1)} collective-permute-done((f32[4,2,64,128]{3,2,1,0:T(8,128)S(1)}, f32[4,2,64,128]{3,2,1,0:T(8,128)S(1)}, u32[]{:S(2)}, u32[]{:S(2)}) %collective-permute-start.12) | collective-permute-done | bytes 262176 | tf_op jit(solution)/shard_map/ppermute | solution.py:768
  73.5 0.7 %shard_map.90 = f32[4,128,512]{2,1,0:T(8,128)} custom-call(f32[4,128,512]{2,1,0:T(8,128)} %get-tuple-element.57.total, f32[4,2,64,128]{3,2,1,0:T(8,128)S(1)} %get-tuple-element.58.edge, f32[4,2,64,128]{3,2,1,0:T(8,128)S(1)} %collective-permute-done.12.got), custom_call_target="tpu_custom_call", output_to_operand_aliasing={{}: (0, {})} | custom-call | tf_op jit(solution)/shard_map/pallas_call | solution.py:611
  (2 shorter events, 0.1 us)
Async XLA Ops:
  0.0 38.7 %collective-permute-start = (f32[3,256,256]{2,1,0:T(8,128)}, f32[3,256,256]{2,1,0:T(8,128)S(1)}, u32[]{:S(2)}, u32[]{:S(2)}) collective-permute-start(f32[3,256,256]{2,1,0:T(8,128)} %bitcast.10), channel_id=1, source_target_pairs={{0,2},{1,3},{2,0},{3,1},{4,6},{5,7},{6,4},{7,5},{8,10},{9,11},{10,... | collective-permute-start | bytes 2359304 | tf_op jit(solution)/shard_map/ppermute | solution.py:644
  4.0 2.2 %copy-start = (f32[2,2,512,512]{3,2,1,0:T(8,128)S(1)}, f32[2,2,512,512]{3,2,1,0:T(8,128)}, u32[]{:S(2)}) copy-start(f32[2,2,512,512]{3,2,1,0:T(8,128)} %param.8) | copy-start | bytes 12582916
  7.6 5.7 %collective-permute-start.3 = (f32[2,512,128]{2,1,0:T(8,128)}, f32[2,512,128]{2,1,0:T(8,128)S(1)}, u32[]{:S(2)}, u32[]{:S(2)}) collective-permute-start(f32[2,512,128]{2,1,0:T(8,128)} %get-tuple-element.35), channel_id=1, source_target_pairs={{0,4},{4,0},{1,5},{5,1},{2,6},{6,2},{3,7},{7,3},{8,12},{12,8},{9,1... | collective-permute-start | bytes 1572872 | tf_op jit(solution)/shard_map/ppermute | solution.py:59
  7.7 14.8 %collective-permute-start.1 = (f32[4,64,512]{2,1,0:T(8,128)S(1)}, f32[4,64,512]{2,1,0:T(8,128)S(1)}, u32[]{:S(2)}, u32[]{:S(2)}) collective-permute-start(f32[4,64,512]{2,1,0:T(8,128)S(1)} %get-tuple-element.33), channel_id=1, source_target_pairs={{0,8},{8,0},{16,24},{24,16},{1,9},{9,1},{17,25},{25,17},{2,10},{10... | collective-permute-start | bytes 1572872 | tf_op jit(solution)/shard_map/ppermute | solution.py:59
  9.2 13.2 %collective-permute-start.2 = (f32[4,64,512]{2,1,0:T(8,128)S(1)}, f32[4,64,512]{2,1,0:T(8,128)S(1)}, u32[]{:S(2)}, u32[]{:S(2)}) collective-permute-start(f32[4,64,512]{2,1,0:T(8,128)S(1)} %get-tuple-element.34), channel_id=1, source_target_pairs={{8,16},{16,8},{9,17},{17,9},{10,18},{18,10},{11,19},{19,11},{12,20... | collective-permute-start | bytes 1572872 | tf_op jit(solution)/shard_map/ppermute | solution.py:59
  13.3 2.2 %copy-start.1 = (f32[2,2,512,512]{3,2,1,0:T(8,128)S(1)}, f32[2,2,512,512]{3,2,1,0:T(8,128)}, u32[]{:S(2)}) copy-start(f32[2,2,512,512]{3,2,1,0:T(8,128)} %param.8) | copy-start | bytes 12582916
  15.5 0.9 %copy-start.2 = (bf16[2,256,256]{2,1,0:T(8,128)(2,1)S(1)}, bf16[2,256,256]{2,1,0:T(8,128)(2,1)}, u32[]{:S(2)}) copy-start(bf16[2,256,256]{2,1,0:T(8,128)(2,1)} %constant.11.refs_3_.refs_7_) | copy-start | bytes 786436
  16.4 1.1 %copy-start.3 = (f32[1,1,1,3,256,256]{5,4,3,2,1,0:T(8,128)S(1)}, f32[1,1,1,3,256,256]{5,4,3,2,1,0:T(8,128)}, u32[]{:S(2)}) copy-start(f32[1,1,1,3,256,256]{5,4,3,2,1,0:T(8,128)} %param.11) | copy-start | bytes 2359300
  17.6 1.0 %copy-start.4 = (f32[2,256,256]{2,1,0:T(8,128)S(1)}, f32[2,256,256]{2,1,0:T(8,128)}, u32[]{:S(2)}) copy-start(f32[2,256,256]{2,1,0:T(8,128)} %refs_4_.1) | copy-start | bytes 1572868
  18.6 1.0 %copy-start.5 = (bf16[4,256,256]{2,1,0:T(8,128)(2,1)S(1)}, bf16[4,256,256]{2,1,0:T(8,128)(2,1)}, u32[]{:S(2)}) copy-start(bf16[4,256,256]{2,1,0:T(8,128)(2,1)} %constant.12.refs_5_) | copy-start | bytes 1572868
  22.6 16.1 %collective-permute-start.4 = (f32[2,2,64,128]{3,2,1,0:T(8,128)S(1)}, f32[2,2,64,128]{3,2,1,0:T(8,128)S(1)}, u32[]{:S(2)}, u32[]{:S(2)}) collective-permute-start(f32[2,2,64,128]{3,2,1,0:T(8,128)S(1)} %shard_map.84), channel_id=1, source_target_pairs={{0,4},{4,0},{1,5},{5,1},{2,6},{6,2},{3,7},{7,3},{8,12},{12,8},{9,1... | collective-permute-start | bytes 393224 | tf_op jit(solution)/shard_map/ppermute | solution.py:59
  22.7 16.0 %collective-permute-start.5 = (s32[8]{0:T(128)S(1)}, s32[8]{0:T(128)S(1)}, u32[]{:S(2)}, u32[]{:S(2)}) collective-permute-start(s32[8]{0:T(128)S(1)} %pad_add_fusion._.refs_3_), channel_id=1, source_target_pairs={{0,2},{1,3},{2,0},{3,1},{4,6},{5,7},{6,4},{7,5},{8,10},{9,11},{10,... | collective-permute-start | bytes 104 | tf_op jit(solution)/shard_map/ppermute | solution.py:644
  47.8 5.5 %collective-permute-start.9 = (f32[4,1,320,128]{3,2,1,0:T(8,128)S(1)}, f32[4,1,320,128]{3,2,1,0:T(8,128)S(1)}, u32[]{:S(2)}, u32[]{:S(2)}) collective-permute-start(f32[4,1,320,128]{3,2,1,0:T(8,128)S(1)} %get-tuple-element.52), channel_id=1, source_target_pairs={{0,4},{4,0},{1,5},{5,1},{2,6},{6,2},{3,7},{7,3},{8,12},{12,8},{9,1... | collective-permute-start | bytes 1966088 | tf_op jit(solution)/shard_map/ppermute | solution.py:59
  47.9 9.2 %collective-permute-start.6 = (f32[4,2,64,128]{3,2,1,0:T(8,128)S(1)}, f32[4,2,64,128]{3,2,1,0:T(8,128)S(1)}, u32[]{:S(2)}, u32[]{:S(2)}) collective-permute-start(f32[4,2,64,128]{3,2,1,0:T(8,128)S(1)} %get-tuple-element.44), channel_id=1, source_target_pairs={{0,1},{1,0},{2,3},{3,2},{4,5},{5,4},{6,7},{7,6},{8,9},{9,8},{10,11... | collective-permute-start | bytes 786440 | tf_op jit(solution)/shard_map/ppermute | solution.py:768
  48.9 11.0 %collective-permute-start.7 = (f32[4,2,64,128]{3,2,1,0:T(8,128)S(1)}, f32[4,2,64,128]{3,2,1,0:T(8,128)S(1)}, u32[]{:S(2)}, u32[]{:S(2)}) collective-permute-start(f32[4,2,64,128]{3,2,1,0:T(8,128)S(1)} %get-tuple-element.45), channel_id=1, source_target_pairs={{0,8},{1,9},{8,16},{9,17},{10,2},{11,3},{16,24},{17,25},{18,10},{1... | collective-permute-start | bytes 786440 | tf_op jit(solution)/shard_map/ppermute | solution.py:59
  53.3 9.3 %collective-permute-start.10 = (f32[4,2,64,128]{3,2,1,0:T(8,128)S(1)}, f32[4,2,64,128]{3,2,1,0:T(8,128)S(1)}, u32[]{:S(2)}, u32[]{:S(2)}) collective-permute-start(f32[4,2,64,128]{3,2,1,0:T(8,128)S(1)} %get-tuple-element.53), channel_id=1, source_target_pairs={{0,1},{1,0},{2,3},{3,2},{4,5},{5,4},{6,7},{7,6},{8,9},{9,8},{10,11... | collective-permute-start | bytes 786440 | tf_op jit(solution)/shard_map/ppermute | solution.py:768
  53.7 11.0 %collective-permute-start.11 = (f32[4,2,64,128]{3,2,1,0:T(8,128)S(1)}, f32[4,2,64,128]{3,2,1,0:T(8,128)S(1)}, u32[]{:S(2)}, u32[]{:S(2)}) collective-permute-start(f32[4,2,64,128]{3,2,1,0:T(8,128)S(1)} %get-tuple-element.54), channel_id=1, source_target_pairs={{0,8},{1,9},{8,16},{9,17},{10,2},{11,3},{16,24},{17,25},{18,10},{1... | collective-permute-start | bytes 786440 | tf_op jit(solution)/shard_map/ppermute | solution.py:59
  59.9 8.9 %collective-permute-start.8 = (f32[4,2,64,128]{3,2,1,0:T(8,128)S(1)}, f32[4,2,64,128]{3,2,1,0:T(8,128)S(1)}, u32[]{:S(2)}, u32[]{:S(2)}) collective-permute-start(f32[4,2,64,128]{3,2,1,0:T(8,128)S(1)} %shard_map.86), channel_id=1, source_target_pairs={{0,1},{1,0},{2,3},{3,2},{4,5},{5,4},{6,7},{7,6},{8,9},{9,8},{10,11... | collective-permute-start | bytes 786440 | tf_op jit(solution)/shard_map/ppermute | solution.py:768
  64.8 8.7 %collective-permute-start.12 = (f32[4,2,64,128]{3,2,1,0:T(8,128)S(1)}, f32[4,2,64,128]{3,2,1,0:T(8,128)S(1)}, u32[]{:S(2)}, u32[]{:S(2)}) collective-permute-start(f32[4,2,64,128]{3,2,1,0:T(8,128)S(1)} %shard_map.89), channel_id=1, source_target_pairs={{0,1},{1,0},{2,3},{3,2},{4,5},{5,4},{6,7},{7,6},{8,9},{9,8},{10,11... | collective-permute-start | bytes 786440 | tf_op jit(solution)/shard_map/ppermute | solution.py:768

commit v4 on v3

--- a/solution.py
+++ b/solution.py
@@ -362,41 +362,43 @@
     copies.wait()
 
 
-def patches_kernel(sides, cuts, peer, *refs):
+def ready_kernel(sides, *refs):
     row_refs, refs = refs[: sides[0]], refs[sides[0] :]
-    corner_refs, refs = refs[: sides[1]], refs[sides[1] :]
-    own_info, peer_info, ext, own, probe, waves, tables, order = refs[:8]
-    outs, (acc, queue, *scratch, ordered, sems) = refs[9:-16], refs[-16:]
+    corner_refs, (ext, _, acc) = refs[: sides[1]], refs[sides[1] :]
+    tiles, height = ext.shape[1], ext.shape[2] - 2 * HALO
+    place = place_of(height)
+
+    def far_row(phase):
+        return pl.ds(pl.multiple_of(jnp.where(place[2] == phase, height + HALO, 0), 8), HALO)
+
+    for i, ref in enumerate(row_refs):
+        for t in range(tiles - 2):
+            ext[:, t + 1, far_row(i), :] = ref[:, :, at_lanes(t)]
+    for j, ref in enumerate(corner_refs):
+        tile = far_tile(place, j, tiles)
+        for i in range(sides[0]):
+            for p in range(2):
+                for q, half in enumerate(unpacked(ref[i, p], place[3] != j)):
+                    ext[p + 2 * q, tile, far_row(i), :] = half
+    for start, count in ((place[0], height // 2), (place[1], HALO)):
+        rows = pl.ds(pl.multiple_of(start + HALO, 8), count)
+        acc[:, :, rows, :] = jnp.zeros((4, tiles, count, LANE), jnp.float32)
+
+
+def patches_kernel(cuts, peer, *refs):
+    own_info, peer_info, ext, acc, own, probe, waves, tables, order = refs[:9]
+    outs, (queue, *scratch, ordered, sems) = refs[10:-15], refs[-15:]
     groups = [Patches(*scratch[:6], tables), Patches(*scratch[6:], tables)]
     tiles, height = ext.shape[1], ext.shape[2] - 2 * HALO
     half_rows = height // 2
     place = place_of(height)
-    copies = Copies(sems)
-
-    def far_row(phase):
-        return pl.multiple_of(jnp.where(place[2] == phase, height + HALO, 0), 8)
-
-    for i, ref in enumerate(row_refs):
-        for t in range(tiles - 2):
-            part = ref.at[:, :, pl.ds(t * LANE, LANE)]
-            copies.start(part, ext.at[:, t + 1, pl.ds(far_row(i), HALO), :])
-    for j, ref in enumerate(corner_refs):
-        tile = far_tile(place, j, tiles)
-        for i in range(sides[0]):
-            rows = pl.ds(far_row(i), HALO)
-            for p in range(2):
-                for q, half in enumerate(unpacked(ref[i, p], place[3] != j)):
-                    ext[p + 2 * q, tile, rows, :] = half
     first = pl.multiple_of(place[0] + HALO, 8)
     outer = pl.multiple_of(place[1] + HALO, 8)
-    acc[:, :, pl.ds(first, half_rows), :] = jnp.zeros((4, tiles, half_rows, LANE), jnp.float32)
-    acc[:, :, pl.ds(outer, HALO), :] = jnp.zeros((4, tiles, HALO, LANE), jnp.float32)
 
     def intensity(index):
         mine, theirs = jnp.minimum(index, PMAX - 1), jnp.maximum(index - PMAX, 0)
         return jnp.where(index < PMAX, own[mine], peer[theirs])
 
-    copies.wait()
     length = jnp.int32(0)
     for index in range(2 * PMAX):
         info, slot = (own_info, index) if index < PMAX else (peer_info, index - PMAX)
@@ -718,17 +720,24 @@
         limit=VMEM_LITTLE,
     )
     corner_halos = [to_cols(ends, j) for j, ends in zip(col_sides, row_ends)]
-    arrivals = [peer, *row_halos, *corner_halos]
-    copy_count = max(
-        tiles * both[0], sum(len(parts) for _, parts in cuts)
+    ext, acc = call(
+        functools.partial(ready_kernel, both),
+        [block(*full), block(*full)],
+        [VMEM] * (both[0] + sides + 1),
+        [VMEM, VMEM],
+        [],
+        *row_halos,
+        *corner_halos,
+        ext,
+        limit=VMEM_LITTLE,
+        aliases={both[0] + sides: 0},
     )
     outs = call(
-        functools.partial(patches_kernel, both, [parts for _, parts in cuts]),
+        functools.partial(patches_kernel, [parts for _, parts in cuts]),
         [block(*full)] + [block(4, wide, sum(part[2] for part in parts), LANE) for wide, parts in cuts],
-        [VMEM] + [ANY] * both[0] + [VMEM] * sides + [SMEM, SMEM] + [VMEM] * 6,
+        [VMEM, SMEM, SMEM] + [VMEM] * 7,
         [VMEM] + [ANY] * len(cuts),
         [
-            pltpu.VMEM(full, jnp.float32),
             pltpu.SMEM((3 * (2 * PMAX + 1),), jnp.int32),
             *[
                 pltpu.VMEM(shape, dtype)
@@ -743,18 +752,19 @@
                 )
             ],
             pltpu.VMEM((GROUP * PATCH, PATCH), jnp.float32),
-            pltpu.SemaphoreType.DMA((copy_count,)),
+            pltpu.SemaphoreType.DMA((sum(len(parts) for _, parts in cuts),)),
         ],
-        *arrivals,
+        peer,
         own_info,
         peer_info,
         ext,
+        acc,
         near_own,
         lamp,
         waves,
         near_tables,
         near_order,
-        aliases={len(arrivals) + 2: 0},
+        aliases={4: 0},
     )[1:]
     outer_inner, outer_left, outer_right = outs[:3]
     rims, pieces = outs[3 : 3 + sides], outs[3 + sides :]

time: 74.6 us -> 74.2 us (level)
  waiting for transfers between devices: 30.5 us -> 29.7 us
    ppermute x2, waiting for transfers between devices: 15.9 us -> 14.1 us  [across(): lax.ppermute(value, 'scan', [(i, i ^ stride) for i in range(shard_count)])]
    ppermute x7, waiting for transfers between devices: 5.3 us -> 6.95 us  [joint_permute(): lax.ppermute(value, tuple(names) if len(names) > 1 else names[0], route)]
    pallas_call x9 -> x10, Pallas kernels: 15.2 us -> 15.1 us  [call(): pl.pallas_call(kernel, out_shape=out_shapes, in_specs=in_specs, out_specs...]
  transfers between devices with their start and end apart: 13 -> 13, of which waited for: 7 -> 8; matrix products, arithmetic and copies ran while one was open for 4% -> 4% of each run, Pallas kernels for 7% -> 8%
where the time goes in v4:
time: 74.2 us; the launch traced here: 73.7 us
  waiting for transfers between devices  29.7 us (40%)
  starting transfers between devices  16.8 us (23%)
  Pallas kernels  15.1 us (20%)
  local copies, waits for them, and re-layouts  11.2 us (15%)
  between operations  0.8 us (1%)
    pallas_call x10, Pallas kernels, call(): pl.pallas_call(kernel, out_shape=out_shapes, in_specs=in_specs, out_specs...  15.1 us
    ppermute x2, waiting for transfers between devices, across(): lax.ppermute(value, 'scan', [(i, i ^ stride) for i in range(shard_count)])  14.1 us
    ppermute x7, starting transfers between devices, joint_permute(): lax.ppermute(value, tuple(names) if len(names) > 1 else names[0], route)  9.85 us
    ppermute x4, waiting for transfers between devices, beside(): lax.ppermute(value, 'scan', [(i, i ^ mask) for i in range(shard_count)])  8.7 us
    unnamed x12, local copies, waits for them, and re-layouts  8.53 us
    ppermute x7, waiting for transfers between devices, joint_permute(): lax.ppermute(value, tuple(names) if len(names) > 1 else names[0], route)  6.95 us
    ppermute x2, starting transfers between devices, across(): lax.ppermute(value, 'scan', [(i, i ^ stride) for i in range(shard_count)])  4.11 us
    ppermute x4, starting transfers between devices, beside(): lax.ppermute(value, 'scan', [(i, i ^ mask) for i in range(shard_count)])  2.89 us
  transfers between devices with their start and end apart: 13, of which 8 were waited for; matrix products, arithmetic and copies ran while one was open for 4% of the time, Pallas kernels for 8%

profile of v4, /device:TPU:0, one launch (start us, length us, event | category | flops | bytes accessed | tf_op | source)
XLA Modules:
  0.0 73.7 jit_solution(6031936574215619423)
XLA Ops:
  0.0 4.0 %collective-permute-start = (f32[3,256,256]{2,1,0:T(8,128)}, f32[3,256,256]{2,1,0:T(8,128)S(1)}, u32[]{:S(2)}, u32[]{:S(2)}) collective-permute-start(f32[3,256,256]{2,1,0:T(8,128)} %bitcast.10), channel_id=1, source_target_pairs={{0,2},{1,3},{2,0},{3,1},{4,6},{5,7},{6,4},{7,5},{8,10},{9,11},{10,... | collective-permute-start | bytes 2359304 | tf_op jit(solution)/shard_map/ppermute | solution.py:646
  4.0 0.0 copy-start
  4.0 2.2 %copy-done = f32[2,2,512,512]{3,2,1,0:T(8,128)S(1)} copy-done((f32[2,2,512,512]{3,2,1,0:T(8,128)S(1)}, f32[2,2,512,512]{3,2,1,0:T(8,128)}, u32[]{:S(2)}) %copy-start) | copy-done | bytes 4194328
  6.2 1.4 %shard_map.82 = (f32[4,64,512]{2,1,0:T(8,128)}, f32[4,64,512]{2,1,0:T(8,128)S(1)}, f32[2,512,128]{2,1,0:T(8,128)}) custom-call(f32[4,512,512]{2,1,0:T(8,128)S(1)} %bitcast.8), custom_call_target="tpu_custom_call" | custom-call | tf_op jit(solution)/shard_map/pallas_call | solution.py:613
  7.6 0.1 collective-permute-start.4
  7.7 1.6 %collective-permute-start.2 = (f32[4,64,512]{2,1,0:T(8,128)}, f32[4,64,512]{2,1,0:T(8,128)S(1)}, u32[]{:S(2)}, u32[]{:S(2)}) collective-permute-start(f32[4,64,512]{2,1,0:T(8,128)} %get-tuple-element.35), channel_id=1, source_target_pairs={{0,8},{8,0},{16,24},{24,16},{1,9},{9,1},{17,25},{25,17},{2,10},{10... | collective-permute-start | bytes 1572872 | tf_op jit(solution)/shard_map/ppermute | solution.py:59
  9.2 0.7 collective-permute-start.3
  10.6 0.8 %reshape.20 = s32[6]{0:T(128)S(1)} reshape(s32[2,3]{1,0:T(2,128)} %bitcast.12) | data formatting | bytes 48 | tf_op jit(solution)/shard_map/reshape | solution.py:642
  11.3 0.1 pad_add_fusion._.refs_0_
  11.4 1.9 %fusion = (f32[256,256]{1,0:T(8,128)S(1)}, f32[256,256]{1,0:T(8,128)S(1)}) fusion(f32[256,256]{1,0:T(8,128)} %param.10), kind=kLoop, calls=%fused_computation.1 | loop fusion | bytes 786432 | tf_op jit(solution)/shard_map/sin | solution.py:671
  13.3 0.0 collective-permute-done.4.refs_0_
  13.3 0.0 copy-start.1
  13.3 2.2 %copy-done.1 = f32[2,2,512,512]{3,2,1,0:T(8,128)S(1)} copy-done((f32[2,2,512,512]{3,2,1,0:T(8,128)S(1)}, f32[2,2,512,512]{3,2,1,0:T(8,128)}, u32[]{:S(2)}) %copy-start.1) | copy-done | bytes 4194328
  15.5 0.0 copy-start.2
  15.5 0.9 %copy-done.2 = bf16[2,256,256]{2,1,0:T(8,128)(2,1)S(1)} copy-done((bf16[2,256,256]{2,1,0:T(8,128)(2,1)S(1)}, bf16[2,256,256]{2,1,0:T(8,128)(2,1)}, u32[]{:S(2)}) %copy-start.2) | copy-done | bytes 262168
  16.4 0.0 copy-start.3
  16.4 1.1 %copy-done.3 = f32[1,1,1,3,256,256]{5,4,3,2,1,0:T(8,128)S(1)} copy-done((f32[1,1,1,3,256,256]{5,4,3,2,1,0:T(8,128)S(1)}, f32[1,1,1,3,256,256]{5,4,3,2,1,0:T(8,128)}, u32[]{:S(2)}) %copy-start.3) | copy-done | bytes 786456
  17.6 0.0 copy-start.4
  17.6 1.0 %copy-done.4 = f32[2,256,256]{2,1,0:T(8,128)S(1)} copy-done((f32[2,256,256]{2,1,0:T(8,128)S(1)}, f32[2,256,256]{2,1,0:T(8,128)}, u32[]{:S(2)}) %copy-start.4) | copy-done | bytes 524312
  18.6 0.0 copy-start.5
  18.6 1.0 %copy-done.5 = bf16[4,256,256]{2,1,0:T(8,128)(2,1)S(1)} copy-done((bf16[4,256,256]{2,1,0:T(8,128)(2,1)S(1)}, bf16[4,256,256]{2,1,0:T(8,128)(2,1)}, u32[]{:S(2)}) %copy-start.5) | copy-done | bytes 524312
  19.7 2.4 %shard_map.83 = (f32[4,6,640,128]{3,2,1,0:T(8,128)S(1)}, f32[2,2,256,128]{3,2,1,0:T(8,128)S(1)}, f32[2,256,256]{2,1,0:T(8,128)S(1)}, bf16[4,256,256]{2,1,0:T(8,1...) custom-call(s32[8]{0:T(128)S(1)} %pad_add_fusion._.refs_0_, f32[4,512,512]{2,1,0:T(8,128)S(1)} %bitcast.9, ...), custom_call_target="tpu_custom_call" | custom-call | tf_op jit(solution)/shard_map/pallas_call | solution.py:613
  22.1 0.6 collective-permute-done.2.refs_0_
  22.7 0.0 collective-permute-done.3.refs_1_
  22.7 0.1 shard_map.84
  22.8 0.1 collective-permute-start.5
  22.9 0.1 collective-permute-start.1
  23.0 1.3 %collective-permute-done.5.refs_2_ = f32[2,2,64,128]{3,2,1,0:T(8,128)S(1)} collective-permute-done((f32[2,2,64,128]{3,2,1,0:T(8,128)S(1)}, f32[2,2,64,128]{3,2,1,0:T(8,128)S(1)}, u32[]{:S(2)}, u32[]{:S(2)}) %collective-permute-start.5) | collective-permute-done | bytes 131104 | tf_op jit(solution)/shard_map/ppermute | solution.py:59
  24.2 0.4 shard_map.85
  24.7 14.1 %collective-permute-done.1.refs_1_ = s32[8]{0:T(128)S(1)} collective-permute-done((s32[8]{0:T(128)S(1)}, s32[8]{0:T(128)S(1)}, u32[]{:S(2)}, u32[]{:S(2)}) %collective-permute-start.1) | collective-permute-done | bytes 64 | tf_op jit(solution)/shard_map/ppermute | solution.py:646
  38.7 0.0 collective-permute-done.peer
  38.7 8.6 %shard_map.86 = (f32[4,6,640,128]{3,2,1,0:T(8,128)S(1)}, f32[4,2,64,128]{3,2,1,0:T(8,128)S(1)}, f32[4,1,64,128]{3,2,1,0:T(8,128)S(1)}, f32[4,1,64,128]{3,2,1,0:T...) custom-call(f32[3,256,256]{2,1,0:T(8,128)S(1)} %collective-permute-d, ...), custom_call_target="tpu_custom_call", output_to_operand_aliasing={{0}: (4, {})} | custom-call | tf_op jit(solution)/shard_map/pallas_call | solution.py:613
  47.3 0.1 collective-permute-start.9
  47.4 1.0 %collective-permute-start.6 = (f32[4,2,64,128]{3,2,1,0:T(8,128)S(1)}, f32[4,2,64,128]{3,2,1,0:T(8,128)S(1)}, u32[]{:S(2)}, u32[]{:S(2)}) collective-permute-start(f32[4,2,64,128]{3,2,1,0:T(8,128)S(1)} %get-tuple-element.48), channel_id=1, source_target_pairs={{0,1},{1,0},{2,3},{3,2},{4,5},{5,4},{6,7},{7,6},{8,9},{9,8},{10,11... | collective-permute-start | bytes 786440 | tf_op jit(solution)/shard_map/ppermute | solution.py:778
  48.4 4.5 %collective-permute-start.7 = (f32[4,2,64,128]{3,2,1,0:T(8,128)S(1)}, f32[4,2,64,128]{3,2,1,0:T(8,128)S(1)}, u32[]{:S(2)}, u32[]{:S(2)}) collective-permute-start(f32[4,2,64,128]{3,2,1,0:T(8,128)S(1)} %get-tuple-element.49), channel_id=1, source_target_pairs={{0,8},{1,9},{8,16},{9,17},{10,2},{11,3},{16,24},{17,25},{18,10},{1... | collective-permute-start | bytes 786440 | tf_op jit(solution)/shard_map/ppermute | solution.py:59
  52.9 0.0 collective-permute-done.9.refs_4_.refs_6_.refs_3_
  52.9 0.1 shard_map.88
  53.0 0.6 collective-permute-start.10
  53.6 2.9 %collective-permute-start.11 = (f32[4,2,64,128]{3,2,1,0:T(8,128)S(1)}, f32[4,2,64,128]{3,2,1,0:T(8,128)S(1)}, u32[]{:S(2)}, u32[]{:S(2)}) collective-permute-start(f32[4,2,64,128]{3,2,1,0:T(8,128)S(1)} %get-tuple-element.58), channel_id=1, source_target_pairs={{0,8},{1,9},{8,16},{9,17},{10,2},{11,3},{16,24},{17,25},{18,10},{1... | collective-permute-start | bytes 786440 | tf_op jit(solution)/shard_map/ppermute | solution.py:59
  56.5 0.0 collective-permute-done.6.refs_2_
  56.5 3.0 %collective-permute-done.7.strip.refs_4_ = f32[4,2,64,128]{3,2,1,0:T(8,128)S(1)} collective-permute-done((f32[4,2,64,128]{3,2,1,0:T(8,128)S(1)}, f32[4,2,64,128]{3,2,1,0:T(8,128)S(1)}, u32[]{:S(2)}, u32[]{:S(2)}) %collective-permute-start.7) | collective-permute-done | bytes 262176 | tf_op jit(solution)/shard_map/ppermute | solution.py:59
  59.5 0.6 collective-permute-start.8
  60.2 2.1 %collective-permute-done.10.refs_3_ = f32[4,2,64,128]{3,2,1,0:T(8,128)S(1)} collective-permute-done((f32[4,2,64,128]{3,2,1,0:T(8,128)S(1)}, f32[4,2,64,128]{3,2,1,0:T(8,128)S(1)}, u32[]{:S(2)}, u32[]{:S(2)}) %collective-permute-start.10) | collective-permute-done | bytes 262176 | tf_op jit(solution)/shard_map/ppermute | solution.py:778
  62.3 2.1 %collective-permute-done.11.refs_5_.refs_2_ = f32[4,2,64,128]{3,2,1,0:T(8,128)S(1)} collective-permute-done((f32[4,2,64,128]{3,2,1,0:T(8,128)S(1)}, f32[4,2,64,128]{3,2,1,0:T(8,128)S(1)}, u32[]{:S(2)}, u32[]{:S(2)}) %collective-permute-start.11) | collective-permute-done | bytes 262176 | tf_op jit(solution)/shard_map/ppermute | solution.py:59
  64.4 0.6 collective-permute-start.12
  65.0 3.2 %collective-permute-done.8.refs_1_ = f32[4,2,64,128]{3,2,1,0:T(8,128)S(1)} collective-permute-done((f32[4,2,64,128]{3,2,1,0:T(8,128)S(1)}, f32[4,2,64,128]{3,2,1,0:T(8,128)S(1)}, u32[]{:S(2)}, u32[]{:S(2)}) %collective-permute-start.8) | collective-permute-done | bytes 262176 | tf_op jit(solution)/shard_map/ppermute | solution.py:778
  68.2 1.4 %shard_map.89 = (f32[4,128,512]{2,1,0:T(8,128)}, f32[4,2,64,128]{3,2,1,0:T(8,128)S(1)}) custom-call(f32[4,4,128,128]{3,2,1,0:T(8,128)S(1)} %get-tuple-element.46.refs_0_, f32[4,2,64,128]{3,2,1,0:T(8,128)S(1)} %collective-permute-done.8.refs_1_, f32[4,2,64,128]{3,2,1,0:T(8,128)S(1)} %collective-permute-done.6.refs_2_, ...), custom_call_target="tpu_custom_call" | custom-call | tf_op jit(solution)/shard_map/pallas_call | solution.py:613
  69.5 3.4 %collective-permute-done.12.got = f32[4,2,64,128]{3,2,1,0:T(8,128)S(1)} collective-permute-done((f32[4,2,64,128]{3,2,1,0:T(8,128)S(1)}, f32[4,2,64,128]{3,2,1,0:T(8,128)S(1)}, u32[]{:S(2)}, u32[]{:S(2)}) %collective-permute-start.12) | collective-permute-done | bytes 262176 | tf_op jit(solution)/shard_map/ppermute | solution.py:778
  72.9 0.7 %shard_map.91 = f32[4,128,512]{2,1,0:T(8,128)} custom-call(f32[4,128,512]{2,1,0:T(8,128)} %get-tuple-element.61.total, f32[4,2,64,128]{3,2,1,0:T(8,128)S(1)} %get-tuple-element.62.edge, f32[4,2,64,128]{3,2,1,0:T(8,128)S(1)} %collective-permute-done.12.got), custom_call_target="tpu_custom_call", output_to_operand_aliasing={{}: (0, {})} | custom-call | tf_op jit(solution)/shard_map/pallas_call | solution.py:613
  (2 shorter events, 0.1 us)
Async XLA Ops:
  0.0 38.7 %collective-permute-start = (f32[3,256,256]{2,1,0:T(8,128)}, f32[3,256,256]{2,1,0:T(8,128)S(1)}, u32[]{:S(2)}, u32[]{:S(2)}) collective-permute-start(f32[3,256,256]{2,1,0:T(8,128)} %bitcast.10), channel_id=1, source_target_pairs={{0,2},{1,3},{2,0},{3,1},{4,6},{5,7},{6,4},{7,5},{8,10},{9,11},{10,... | collective-permute-start | bytes 2359304 | tf_op jit(solution)/shard_map/ppermute | solution.py:646
  4.0 2.2 %copy-start = (f32[2,2,512,512]{3,2,1,0:T(8,128)S(1)}, f32[2,2,512,512]{3,2,1,0:T(8,128)}, u32[]{:S(2)}) copy-start(f32[2,2,512,512]{3,2,1,0:T(8,128)} %param.8) | copy-start | bytes 12582916
  7.6 5.7 %collective-permute-start.4 = (f32[2,512,128]{2,1,0:T(8,128)}, f32[2,512,128]{2,1,0:T(8,128)S(1)}, u32[]{:S(2)}, u32[]{:S(2)}) collective-permute-start(f32[2,512,128]{2,1,0:T(8,128)} %get-tuple-element.37), channel_id=1, source_target_pairs={{0,4},{4,0},{1,5},{5,1},{2,6},{6,2},{3,7},{7,3},{8,12},{12,8},{9,1... | collective-permute-start | bytes 1572872 | tf_op jit(solution)/shard_map/ppermute | solution.py:59
  7.7 15.0 %collective-permute-start.2 = (f32[4,64,512]{2,1,0:T(8,128)}, f32[4,64,512]{2,1,0:T(8,128)S(1)}, u32[]{:S(2)}, u32[]{:S(2)}) collective-permute-start(f32[4,64,512]{2,1,0:T(8,128)} %get-tuple-element.35), channel_id=1, source_target_pairs={{0,8},{8,0},{16,24},{24,16},{1,9},{9,1},{17,25},{25,17},{2,10},{10... | collective-permute-start | bytes 1572872 | tf_op jit(solution)/shard_map/ppermute | solution.py:59
  9.2 13.4 %collective-permute-start.3 = (f32[4,64,512]{2,1,0:T(8,128)S(1)}, f32[4,64,512]{2,1,0:T(8,128)S(1)}, u32[]{:S(2)}, u32[]{:S(2)}) collective-permute-start(f32[4,64,512]{2,1,0:T(8,128)S(1)} %get-tuple-element.36), channel_id=1, source_target_pairs={{8,16},{16,8},{9,17},{17,9},{10,18},{18,10},{11,19},{19,11},{12,20... | collective-permute-start | bytes 1572872 | tf_op jit(solution)/shard_map/ppermute | solution.py:59
  13.3 2.2 %copy-start.1 = (f32[2,2,512,512]{3,2,1,0:T(8,128)S(1)}, f32[2,2,512,512]{3,2,1,0:T(8,128)}, u32[]{:S(2)}) copy-start(f32[2,2,512,512]{3,2,1,0:T(8,128)} %param.8) | copy-start | bytes 12582916
  15.5 0.9 %copy-start.2 = (bf16[2,256,256]{2,1,0:T(8,128)(2,1)S(1)}, bf16[2,256,256]{2,1,0:T(8,128)(2,1)}, u32[]{:S(2)}) copy-start(bf16[2,256,256]{2,1,0:T(8,128)(2,1)} %constant.11.refs_3_.refs_7_) | copy-start | bytes 786436
  16.4 1.1 %copy-start.3 = (f32[1,1,1,3,256,256]{5,4,3,2,1,0:T(8,128)S(1)}, f32[1,1,1,3,256,256]{5,4,3,2,1,0:T(8,128)}, u32[]{:S(2)}) copy-start(f32[1,1,1,3,256,256]{5,4,3,2,1,0:T(8,128)} %param.11) | copy-start | bytes 2359300
  17.6 1.0 %copy-start.4 = (f32[2,256,256]{2,1,0:T(8,128)S(1)}, f32[2,256,256]{2,1,0:T(8,128)}, u32[]{:S(2)}) copy-start(f32[2,256,256]{2,1,0:T(8,128)} %refs_4_.1) | copy-start | bytes 1572868
  18.6 1.0 %copy-start.5 = (bf16[4,256,256]{2,1,0:T(8,128)(2,1)S(1)}, bf16[4,256,256]{2,1,0:T(8,128)(2,1)}, u32[]{:S(2)}) copy-start(bf16[4,256,256]{2,1,0:T(8,128)(2,1)} %constant.12.refs_5_) | copy-start | bytes 1572868
  22.8 1.4 %collective-permute-start.5 = (f32[2,2,64,128]{3,2,1,0:T(8,128)S(1)}, f32[2,2,64,128]{3,2,1,0:T(8,128)S(1)}, u32[]{:S(2)}, u32[]{:S(2)}) collective-permute-start(f32[2,2,64,128]{3,2,1,0:T(8,128)S(1)} %shard_map.84), channel_id=1, source_target_pairs={{0,4},{4,0},{1,5},{5,1},{2,6},{6,2},{3,7},{7,3},{8,12},{12,8},{9,1... | collective-permute-start | bytes 393224 | tf_op jit(solution)/shard_map/ppermute | solution.py:59
  22.9 15.8 %collective-permute-start.1 = (s32[8]{0:T(128)S(1)}, s32[8]{0:T(128)S(1)}, u32[]{:S(2)}, u32[]{:S(2)}) collective-permute-start(s32[8]{0:T(128)S(1)} %pad_add_fusion._.refs_0_), channel_id=1, source_target_pairs={{0,2},{1,3},{2,0},{3,1},{4,6},{5,7},{6,4},{7,5},{8,10},{9,11},{10,... | collective-permute-start | bytes 104 | tf_op jit(solution)/shard_map/ppermute | solution.py:646
  47.3 5.6 %collective-permute-start.9 = (f32[4,1,320,128]{3,2,1,0:T(8,128)S(1)}, f32[4,1,320,128]{3,2,1,0:T(8,128)S(1)}, u32[]{:S(2)}, u32[]{:S(2)}) collective-permute-start(f32[4,1,320,128]{3,2,1,0:T(8,128)S(1)} %get-tuple-element.56), channel_id=1, source_target_pairs={{0,4},{4,0},{1,5},{5,1},{2,6},{6,2},{3,7},{7,3},{8,12},{12,8},{9,1... | collective-permute-start | bytes 1966088 | tf_op jit(solution)/shard_map/ppermute | solution.py:59
  47.4 9.2 %collective-permute-start.6 = (f32[4,2,64,128]{3,2,1,0:T(8,128)S(1)}, f32[4,2,64,128]{3,2,1,0:T(8,128)S(1)}, u32[]{:S(2)}, u32[]{:S(2)}) collective-permute-start(f32[4,2,64,128]{3,2,1,0:T(8,128)S(1)} %get-tuple-element.48), channel_id=1, source_target_pairs={{0,1},{1,0},{2,3},{3,2},{4,5},{5,4},{6,7},{7,6},{8,9},{9,8},{10,11... | collective-permute-start | bytes 786440 | tf_op jit(solution)/shard_map/ppermute | solution.py:778
  48.4 11.1 %collective-permute-start.7 = (f32[4,2,64,128]{3,2,1,0:T(8,128)S(1)}, f32[4,2,64,128]{3,2,1,0:T(8,128)S(1)}, u32[]{:S(2)}, u32[]{:S(2)}) collective-permute-start(f32[4,2,64,128]{3,2,1,0:T(8,128)S(1)} %get-tuple-element.49), channel_id=1, source_target_pairs={{0,8},{1,9},{8,16},{9,17},{10,2},{11,3},{16,24},{17,25},{18,10},{1... | collective-permute-start | bytes 786440 | tf_op jit(solution)/shard_map/ppermute | solution.py:59
  53.0 9.3 %collective-permute-start.10 = (f32[4,2,64,128]{3,2,1,0:T(8,128)S(1)}, f32[4,2,64,128]{3,2,1,0:T(8,128)S(1)}, u32[]{:S(2)}, u32[]{:S(2)}) collective-permute-start(f32[4,2,64,128]{3,2,1,0:T(8,128)S(1)} %get-tuple-element.57), channel_id=1, source_target_pairs={{0,1},{1,0},{2,3},{3,2},{4,5},{5,4},{6,7},{7,6},{8,9},{9,8},{10,11... | collective-permute-start | bytes 786440 | tf_op jit(solution)/shard_map/ppermute | solution.py:778
  53.6 10.8 %collective-permute-start.11 = (f32[4,2,64,128]{3,2,1,0:T(8,128)S(1)}, f32[4,2,64,128]{3,2,1,0:T(8,128)S(1)}, u32[]{:S(2)}, u32[]{:S(2)}) collective-permute-start(f32[4,2,64,128]{3,2,1,0:T(8,128)S(1)} %get-tuple-element.58), channel_id=1, source_target_pairs={{0,8},{1,9},{8,16},{9,17},{10,2},{11,3},{16,24},{17,25},{18,10},{1... | collective-permute-start | bytes 786440 | tf_op jit(solution)/shard_map/ppermute | solution.py:59
  59.5 8.6 %collective-permute-start.8 = (f32[4,2,64,128]{3,2,1,0:T(8,128)S(1)}, f32[4,2,64,128]{3,2,1,0:T(8,128)S(1)}, u32[]{:S(2)}, u32[]{:S(2)}) collective-permute-start(f32[4,2,64,128]{3,2,1,0:T(8,128)S(1)} %shard_map.87), channel_id=1, source_target_pairs={{0,1},{1,0},{2,3},{3,2},{4,5},{5,4},{6,7},{7,6},{8,9},{9,8},{10,11... | collective-permute-start | bytes 786440 | tf_op jit(solution)/shard_map/ppermute | solution.py:778
  64.4 8.5 %collective-permute-start.12 = (f32[4,2,64,128]{3,2,1,0:T(8,128)S(1)}, f32[4,2,64,128]{3,2,1,0:T(8,128)S(1)}, u32[]{:S(2)}, u32[]{:S(2)}) collective-permute-start(f32[4,2,64,128]{3,2,1,0:T(8,128)S(1)} %shard_map.90), channel_id=1, source_target_pairs={{0,1},{1,0},{2,3},{3,2},{4,5},{5,4},{6,7},{7,6},{8,9},{9,8},{10,11... | collective-permute-start | bytes 786440 | tf_op jit(solution)/shard_map/ppermute | solution.py:778

commit v5 on v4

--- a/solution.py
+++ b/solution.py
@@ -364,25 +364,29 @@
 
 def ready_kernel(sides, *refs):
     row_refs, refs = refs[: sides[0]], refs[sides[0] :]
-    corner_refs, (ext, _, acc) = refs[: sides[1]], refs[sides[1] :]
+    corner_refs, (_, ext, acc, ends, sems) = refs[: sides[1]], refs[sides[1] :]
     tiles, height = ext.shape[1], ext.shape[2] - 2 * HALO
     place = place_of(height)
+    copies = Copies(sems)
 
     def far_row(phase):
         return pl.ds(pl.multiple_of(jnp.where(place[2] == phase, height + HALO, 0), 8), HALO)
 
     for i, ref in enumerate(row_refs):
         for t in range(tiles - 2):
-            ext[:, t + 1, far_row(i), :] = ref[:, :, at_lanes(t)]
+            part = ref.at[:, :, pl.ds(t * LANE, LANE)]
+            copies.start(part, ext.at[:, t + 1, far_row(i), :])
     for j, ref in enumerate(corner_refs):
         tile = far_tile(place, j, tiles)
         for i in range(sides[0]):
             for p in range(2):
                 for q, half in enumerate(unpacked(ref[i, p], place[3] != j)):
-                    ext[p + 2 * q, tile, far_row(i), :] = half
+                    ends[i, j, p + 2 * q] = half
+            copies.start(ends.at[i, j], ext.at[:, tile, far_row(i), :])
     for start, count in ((place[0], height // 2), (place[1], HALO)):
         rows = pl.ds(pl.multiple_of(start + HALO, 8), count)
         acc[:, :, rows, :] = jnp.zeros((4, tiles, count, LANE), jnp.float32)
+    copies.wait()
 
 
 def patches_kernel(cuts, peer, *refs):
@@ -723,9 +727,12 @@
     ext, acc = call(
         functools.partial(ready_kernel, both),
         [block(*full), block(*full)],
-        [VMEM] * (both[0] + sides + 1),
-        [VMEM, VMEM],
-        [],
+        [ANY] * both[0] + [VMEM] * sides + [ANY],
+        [ANY, VMEM],
+        [
+            pltpu.VMEM((*both, 4, HALO, LANE), jnp.float32),
+            pltpu.SemaphoreType.DMA((both[0] * (tiles + sides),)),
+        ],
         *row_halos,
         *corner_halos,
         ext,

time: 74.2 us -> 74.3 us (level)
  transfers between devices with their start and end apart: 13 -> 13, of which waited for: 8 -> 9; matrix products, arithmetic and copies ran while one was open for 4% -> 4% of each run, Pallas kernels for 8% -> 8%
where the time goes in v5:
time: 74.3 us; the launch traced here: 73.8 us
  waiting for transfers between devices  29.6 us (40%)
  starting transfers between devices  16.5 us (22%)
  Pallas kernels  15.6 us (21%)
  local copies, waits for them, and re-layouts  11.1 us (15%)
  between operations  0.81 us (1%)
    pallas_call x10, Pallas kernels, call(): pl.pallas_call(kernel, out_shape=out_shapes, in_specs=in_specs, out_specs...  15.6 us
    ppermute x2, waiting for transfers between devices, across(): lax.ppermute(value, 'scan', [(i, i ^ stride) for i in range(shard_count)])  13.7 us
    ppermute x7, starting transfers between devices, joint_permute(): lax.ppermute(value, tuple(names) if len(names) > 1 else names[0], route)  10.2 us
    ppermute x4, waiting for transfers between devices, beside(): lax.ppermute(value, 'scan', [(i, i ^ mask) for i in range(shard_count)])  9.03 us
    unnamed x12, local copies, waits for them, and re-layouts  8.53 us
    ppermute x7, waiting for transfers between devices, joint_permute(): lax.ppermute(value, tuple(names) if len(names) > 1 else names[0], route)  6.93 us
    ppermute x2, starting transfers between devices, across(): lax.ppermute(value, 'scan', [(i, i ^ stride) for i in range(shard_count)])  4.11 us
    ppermute x4, starting transfers between devices, beside(): lax.ppermute(value, 'scan', [(i, i ^ mask) for i in range(shard_count)])  2.21 us
  transfers between devices with their start and end apart: 13, of which 9 were waited for; matrix products, arithmetic and copies ran while one was open for 4% of the time, Pallas kernels for 8%

profile of v5, /device:TPU:0, one launch (start us, length us, event | category | flops | bytes accessed | tf_op | source)
XLA Modules:
  0.0 73.8 jit_solution(3693817588892627239)
XLA Ops:
  0.0 4.0 %collective-permute-start = (f32[3,256,256]{2,1,0:T(8,128)}, f32[3,256,256]{2,1,0:T(8,128)S(1)}, u32[]{:S(2)}, u32[]{:S(2)}) collective-permute-start(f32[3,256,256]{2,1,0:T(8,128)} %bitcast.10), channel_id=1, source_target_pairs={{0,2},{1,3},{2,0},{3,1},{4,6},{5,7},{6,4},{7,5},{8,10},{9,11},{10,... | collective-permute-start | bytes 2359304 | tf_op jit(solution)/shard_map/ppermute | solution.py:650
  4.0 0.0 copy-start
  4.0 2.2 %copy-done = f32[2,2,512,512]{3,2,1,0:T(8,128)S(1)} copy-done((f32[2,2,512,512]{3,2,1,0:T(8,128)S(1)}, f32[2,2,512,512]{3,2,1,0:T(8,128)}, u32[]{:S(2)}) %copy-start) | copy-done | bytes 4194328
  6.2 1.4 %shard_map.82 = (f32[4,64,512]{2,1,0:T(8,128)}, f32[4,64,512]{2,1,0:T(8,128)S(1)}, f32[2,512,128]{2,1,0:T(8,128)}) custom-call(f32[4,512,512]{2,1,0:T(8,128)S(1)} %bitcast.8), custom_call_target="tpu_custom_call" | custom-call | tf_op jit(solution)/shard_map/pallas_call | solution.py:617
  7.6 0.1 collective-permute-start.4
  7.7 1.6 %collective-permute-start.2 = (f32[4,64,512]{2,1,0:T(8,128)}, f32[4,64,512]{2,1,0:T(8,128)S(1)}, u32[]{:S(2)}, u32[]{:S(2)}) collective-permute-start(f32[4,64,512]{2,1,0:T(8,128)} %get-tuple-element.35), channel_id=1, source_target_pairs={{0,8},{8,0},{16,24},{24,16},{1,9},{9,1},{17,25},{25,17},{2,10},{10... | collective-permute-start | bytes 1572872 | tf_op jit(solution)/shard_map/ppermute | solution.py:59
  9.2 0.7 collective-permute-start.3
  10.6 0.8 %reshape.20 = s32[6]{0:T(128)S(1)} reshape(s32[2,3]{1,0:T(2,128)} %bitcast.12) | data formatting | bytes 48 | tf_op jit(solution)/shard_map/reshape | solution.py:646
  11.3 0.1 pad_add_fusion._.refs_0_
  11.4 1.9 %fusion = (f32[256,256]{1,0:T(8,128)S(1)}, f32[256,256]{1,0:T(8,128)S(1)}) fusion(f32[256,256]{1,0:T(8,128)} %param.10), kind=kLoop, calls=%fused_computation.1 | loop fusion | bytes 786432 | tf_op jit(solution)/shard_map/sin | solution.py:675
  13.3 0.0 collective-permute-done.4.refs_0_
  13.3 0.0 copy-start.1
  13.3 2.2 %copy-done.1 = f32[2,2,512,512]{3,2,1,0:T(8,128)S(1)} copy-done((f32[2,2,512,512]{3,2,1,0:T(8,128)S(1)}, f32[2,2,512,512]{3,2,1,0:T(8,128)}, u32[]{:S(2)}) %copy-start.1) | copy-done | bytes 4194328
  15.5 0.0 copy-start.2
  15.5 0.9 %copy-done.2 = bf16[2,256,256]{2,1,0:T(8,128)(2,1)S(1)} copy-done((bf16[2,256,256]{2,1,0:T(8,128)(2,1)S(1)}, bf16[2,256,256]{2,1,0:T(8,128)(2,1)}, u32[]{:S(2)}) %copy-start.2) | copy-done | bytes 262168
  16.4 0.0 copy-start.3
  16.4 1.1 %copy-done.3 = f32[1,1,1,3,256,256]{5,4,3,2,1,0:T(8,128)S(1)} copy-done((f32[1,1,1,3,256,256]{5,4,3,2,1,0:T(8,128)S(1)}, f32[1,1,1,3,256,256]{5,4,3,2,1,0:T(8,128)}, u32[]{:S(2)}) %copy-start.3) | copy-done | bytes 786456
  17.6 0.0 copy-start.4
  17.6 1.0 %copy-done.4 = f32[2,256,256]{2,1,0:T(8,128)S(1)} copy-done((f32[2,256,256]{2,1,0:T(8,128)S(1)}, f32[2,256,256]{2,1,0:T(8,128)}, u32[]{:S(2)}) %copy-start.4) | copy-done | bytes 524312
  18.6 0.0 copy-start.5
  18.6 1.0 %copy-done.5 = bf16[4,256,256]{2,1,0:T(8,128)(2,1)S(1)} copy-done((bf16[4,256,256]{2,1,0:T(8,128)(2,1)S(1)}, bf16[4,256,256]{2,1,0:T(8,128)(2,1)}, u32[]{:S(2)}) %copy-start.5) | copy-done | bytes 524312
  19.7 2.4 %shard_map.83 = (f32[4,6,640,128]{3,2,1,0:T(8,128)S(1)}, f32[2,2,256,128]{3,2,1,0:T(8,128)S(1)}, f32[2,256,256]{2,1,0:T(8,128)S(1)}, bf16[4,256,256]{2,1,0:T(8,1...) custom-call(s32[8]{0:T(128)S(1)} %pad_add_fusion._.refs_0_, f32[4,512,512]{2,1,0:T(8,128)S(1)} %bitcast.9, ...), custom_call_target="tpu_custom_call" | custom-call | tf_op jit(solution)/shard_map/pallas_call | solution.py:617
  22.1 0.6 collective-permute-done.2.refs_0_
  22.7 0.0 collective-permute-done.3.refs_1_
  22.7 0.1 shard_map.84
  22.8 0.1 collective-permute-start.5
  22.9 0.1 collective-permute-start.1
  23.0 1.3 %collective-permute-done.5.refs_2_ = f32[2,2,64,128]{3,2,1,0:T(8,128)S(1)} collective-permute-done((f32[2,2,64,128]{3,2,1,0:T(8,128)S(1)}, f32[2,2,64,128]{3,2,1,0:T(8,128)S(1)}, u32[]{:S(2)}, u32[]{:S(2)}) %collective-permute-start.5) | collective-permute-done | bytes 131104 | tf_op jit(solution)/shard_map/ppermute | solution.py:59
  24.2 0.8 %shard_map.85 = (f32[4,6,640,128]{3,2,1,0:T(8,128)S(1)}, f32[4,6,640,128]{3,2,1,0:T(8,128)S(1)}) custom-call(f32[4,64,512]{2,1,0:T(8,128)S(1)} %collective-permute-done.2.refs_0_, f32[4,64,512]{2,1,0:T(8,128)S(1)} %collective-permute-done.3.refs_1_, f32[2,2,64,128]{3,2,1,0:T(8,128)S(1)} %collective-permute-done.5.refs_2_, ...), custom_call_target="tpu_custom_call", output_to_operand_aliasing={{0}: (3, {})} | custom-call | tf_op jit(solution)/shard_map/pallas_call | solution.py:617
  25.0 13.7 %collective-permute-done.1.refs_1_ = s32[8]{0:T(128)S(1)} collective-permute-done((s32[8]{0:T(128)S(1)}, s32[8]{0:T(128)S(1)}, u32[]{:S(2)}, u32[]{:S(2)}) %collective-permute-start.1) | collective-permute-done | bytes 64 | tf_op jit(solution)/shard_map/ppermute | solution.py:650
  38.7 0.0 collective-permute-done.peer
  38.7 8.7 %shard_map.86 = (f32[4,6,640,128]{3,2,1,0:T(8,128)S(1)}, f32[4,2,64,128]{3,2,1,0:T(8,128)S(1)}, f32[4,1,64,128]{3,2,1,0:T(8,128)S(1)}, f32[4,1,64,128]{3,2,1,0:T...) custom-call(f32[3,256,256]{2,1,0:T(8,128)S(1)} %collective-permute-d, ...), custom_call_target="tpu_custom_call", output_to_operand_aliasing={{0}: (4, {})} | custom-call | tf_op jit(solution)/shard_map/pallas_call | solution.py:617
  47.4 0.1 collective-permute-start.9
  47.5 0.7 collective-permute-start.6
  48.2 4.8 %collective-permute-start.7 = (f32[4,2,64,128]{3,2,1,0:T(8,128)S(1)}, f32[4,2,64,128]{3,2,1,0:T(8,128)S(1)}, u32[]{:S(2)}, u32[]{:S(2)}) collective-permute-start(f32[4,2,64,128]{3,2,1,0:T(8,128)S(1)} %get-tuple-element.49), channel_id=1, source_target_pairs={{0,8},{1,9},{8,16},{9,17},{10,2},{11,3},{16,24},{17,25},{18,10},{1... | collective-permute-start | bytes 786440 | tf_op jit(solution)/shard_map/ppermute | solution.py:59
  53.0 0.0 collective-permute-done.9.refs_4_.refs_6_.refs_3_
  53.0 0.1 shard_map.88
  53.0 0.5 collective-permute-start.10
  53.5 3.0 %collective-permute-start.11 = (f32[4,2,64,128]{3,2,1,0:T(8,128)S(1)}, f32[4,2,64,128]{3,2,1,0:T(8,128)S(1)}, u32[]{:S(2)}, u32[]{:S(2)}) collective-permute-start(f32[4,2,64,128]{3,2,1,0:T(8,128)S(1)} %get-tuple-element.58), channel_id=1, source_target_pairs={{0,8},{1,9},{8,16},{9,17},{10,2},{11,3},{16,24},{17,25},{18,10},{1... | collective-permute-start | bytes 786440 | tf_op jit(solution)/shard_map/ppermute | solution.py:59
  56.6 0.1 collective-permute-done.6.refs_2_
  56.7 2.9 %collective-permute-done.7.strip.refs_4_ = f32[4,2,64,128]{3,2,1,0:T(8,128)S(1)} collective-permute-done((f32[4,2,64,128]{3,2,1,0:T(8,128)S(1)}, f32[4,2,64,128]{3,2,1,0:T(8,128)S(1)}, u32[]{:S(2)}, u32[]{:S(2)}) %collective-permute-start.7) | collective-permute-done | bytes 262176 | tf_op jit(solution)/shard_map/ppermute | solution.py:59
  59.6 0.5 collective-permute-start.8
  60.1 2.2 %collective-permute-done.10.refs_3_ = f32[4,2,64,128]{3,2,1,0:T(8,128)S(1)} collective-permute-done((f32[4,2,64,128]{3,2,1,0:T(8,128)S(1)}, f32[4,2,64,128]{3,2,1,0:T(8,128)S(1)}, u32[]{:S(2)}, u32[]{:S(2)}) %collective-permute-start.10) | collective-permute-done | bytes 262176 | tf_op jit(solution)/shard_map/ppermute | solution.py:785
  62.3 2.1 %collective-permute-done.11.refs_5_.refs_2_ = f32[4,2,64,128]{3,2,1,0:T(8,128)S(1)} collective-permute-done((f32[4,2,64,128]{3,2,1,0:T(8,128)S(1)}, f32[4,2,64,128]{3,2,1,0:T(8,128)S(1)}, u32[]{:S(2)}, u32[]{:S(2)}) %collective-permute-start.11) | collective-permute-done | bytes 262176 | tf_op jit(solution)/shard_map/ppermute | solution.py:59
  64.5 0.5 collective-permute-start.12
  65.0 3.4 %collective-permute-done.8.refs_1_ = f32[4,2,64,128]{3,2,1,0:T(8,128)S(1)} collective-permute-done((f32[4,2,64,128]{3,2,1,0:T(8,128)S(1)}, f32[4,2,64,128]{3,2,1,0:T(8,128)S(1)}, u32[]{:S(2)}, u32[]{:S(2)}) %collective-permute-start.8) | collective-permute-done | bytes 262176 | tf_op jit(solution)/shard_map/ppermute | solution.py:785
  68.4 1.4 %shard_map.89 = (f32[4,128,512]{2,1,0:T(8,128)}, f32[4,2,64,128]{3,2,1,0:T(8,128)S(1)}) custom-call(f32[4,4,128,128]{3,2,1,0:T(8,128)S(1)} %get-tuple-element.46.refs_0_, f32[4,2,64,128]{3,2,1,0:T(8,128)S(1)} %collective-permute-done.8.refs_1_, f32[4,2,64,128]{3,2,1,0:T(8,128)S(1)} %collective-permute-done.6.refs_2_, ...), custom_call_target="tpu_custom_call" | custom-call | tf_op jit(solution)/shard_map/pallas_call | solution.py:617
  69.8 3.3 %collective-permute-done.12.got = f32[4,2,64,128]{3,2,1,0:T(8,128)S(1)} collective-permute-done((f32[4,2,64,128]{3,2,1,0:T(8,128)S(1)}, f32[4,2,64,128]{3,2,1,0:T(8,128)S(1)}, u32[]{:S(2)}, u32[]{:S(2)}) %collective-permute-start.12) | collective-permute-done | bytes 262176 | tf_op jit(solution)/shard_map/ppermute | solution.py:785
  73.1 0.7 %shard_map.91 = f32[4,128,512]{2,1,0:T(8,128)} custom-call(f32[4,128,512]{2,1,0:T(8,128)} %get-tuple-element.61.total, f32[4,2,64,128]{3,2,1,0:T(8,128)S(1)} %get-tuple-element.62.edge, f32[4,2,64,128]{3,2,1,0:T(8,128)S(1)} %collective-permute-done.12.got), custom_call_target="tpu_custom_call", output_to_operand_aliasing={{}: (0, {})} | custom-call | tf_op jit(solution)/shard_map/pallas_call | solution.py:617
  (2 shorter events, 0.1 us)
Async XLA Ops:
  0.0 38.7 %collective-permute-start = (f32[3,256,256]{2,1,0:T(8,128)}, f32[3,256,256]{2,1,0:T(8,128)S(1)}, u32[]{:S(2)}, u32[]{:S(2)}) collective-permute-start(f32[3,256,256]{2,1,0:T(8,128)} %bitcast.10), channel_id=1, source_target_pairs={{0,2},{1,3},{2,0},{3,1},{4,6},{5,7},{6,4},{7,5},{8,10},{9,11},{10,... | collective-permute-start | bytes 2359304 | tf_op jit(solution)/shard_map/ppermute | solution.py:650
  4.0 2.2 %copy-start = (f32[2,2,512,512]{3,2,1,0:T(8,128)S(1)}, f32[2,2,512,512]{3,2,1,0:T(8,128)}, u32[]{:S(2)}) copy-start(f32[2,2,512,512]{3,2,1,0:T(8,128)} %param.8) | copy-start | bytes 12582916
  7.6 5.7 %collective-permute-start.4 = (f32[2,512,128]{2,1,0:T(8,128)}, f32[2,512,128]{2,1,0:T(8,128)S(1)}, u32[]{:S(2)}, u32[]{:S(2)}) collective-permute-start(f32[2,512,128]{2,1,0:T(8,128)} %get-tuple-element.37), channel_id=1, source_target_pairs={{0,4},{4,0},{1,5},{5,1},{2,6},{6,2},{3,7},{7,3},{8,12},{12,8},{9,1... | collective-permute-start | bytes 1572872 | tf_op jit(solution)/shard_map/ppermute | solution.py:59
  7.7 15.0 %collective-permute-start.2 = (f32[4,64,512]{2,1,0:T(8,128)}, f32[4,64,512]{2,1,0:T(8,128)S(1)}, u32[]{:S(2)}, u32[]{:S(2)}) collective-permute-start(f32[4,64,512]{2,1,0:T(8,128)} %get-tuple-element.35), channel_id=1, source_target_pairs={{0,8},{8,0},{16,24},{24,16},{1,9},{9,1},{17,25},{25,17},{2,10},{10... | collective-permute-start | bytes 1572872 | tf_op jit(solution)/shard_map/ppermute | solution.py:59
  9.2 13.4 %collective-permute-start.3 = (f32[4,64,512]{2,1,0:T(8,128)S(1)}, f32[4,64,512]{2,1,0:T(8,128)S(1)}, u32[]{:S(2)}, u32[]{:S(2)}) collective-permute-start(f32[4,64,512]{2,1,0:T(8,128)S(1)} %get-tuple-element.36), channel_id=1, source_target_pairs={{8,16},{16,8},{9,17},{17,9},{10,18},{18,10},{11,19},{19,11},{12,20... | collective-permute-start | bytes 1572872 | tf_op jit(solution)/shard_map/ppermute | solution.py:59
  13.3 2.2 %copy-start.1 = (f32[2,2,512,512]{3,2,1,0:T(8,128)S(1)}, f32[2,2,512,512]{3,2,1,0:T(8,128)}, u32[]{:S(2)}) copy-start(f32[2,2,512,512]{3,2,1,0:T(8,128)} %param.8) | copy-start | bytes 12582916
  15.5 0.9 %copy-start.2 = (bf16[2,256,256]{2,1,0:T(8,128)(2,1)S(1)}, bf16[2,256,256]{2,1,0:T(8,128)(2,1)}, u32[]{:S(2)}) copy-start(bf16[2,256,256]{2,1,0:T(8,128)(2,1)} %constant.11.refs_3_.refs_7_) | copy-start | bytes 786436
  16.4 1.1 %copy-start.3 = (f32[1,1,1,3,256,256]{5,4,3,2,1,0:T(8,128)S(1)}, f32[1,1,1,3,256,256]{5,4,3,2,1,0:T(8,128)}, u32[]{:S(2)}) copy-start(f32[1,1,1,3,256,256]{5,4,3,2,1,0:T(8,128)} %param.11) | copy-start | bytes 2359300
  17.6 1.0 %copy-start.4 = (f32[2,256,256]{2,1,0:T(8,128)S(1)}, f32[2,256,256]{2,1,0:T(8,128)}, u32[]{:S(2)}) copy-start(f32[2,256,256]{2,1,0:T(8,128)} %refs_4_.1) | copy-start | bytes 1572868
  18.6 1.0 %copy-start.5 = (bf16[4,256,256]{2,1,0:T(8,128)(2,1)S(1)}, bf16[4,256,256]{2,1,0:T(8,128)(2,1)}, u32[]{:S(2)}) copy-start(bf16[4,256,256]{2,1,0:T(8,128)(2,1)} %constant.12.refs_5_) | copy-start | bytes 1572868
  22.8 1.4 %collective-permute-start.5 = (f32[2,2,64,128]{3,2,1,0:T(8,128)S(1)}, f32[2,2,64,128]{3,2,1,0:T(8,128)S(1)}, u32[]{:S(2)}, u32[]{:S(2)}) collective-permute-start(f32[2,2,64,128]{3,2,1,0:T(8,128)S(1)} %shard_map.84), channel_id=1, source_target_pairs={{0,4},{4,0},{1,5},{5,1},{2,6},{6,2},{3,7},{7,3},{8,12},{12,8},{9,1... | collective-permute-start | bytes 393224 | tf_op jit(solution)/shard_map/ppermute | solution.py:59
  22.9 15.8 %collective-permute-start.1 = (s32[8]{0:T(128)S(1)}, s32[8]{0:T(128)S(1)}, u32[]{:S(2)}, u32[]{:S(2)}) collective-permute-start(s32[8]{0:T(128)S(1)} %pad_add_fusion._.refs_0_), channel_id=1, source_target_pairs={{0,2},{1,3},{2,0},{3,1},{4,6},{5,7},{6,4},{7,5},{8,10},{9,11},{10,... | collective-permute-start | bytes 104 | tf_op jit(solution)/shard_map/ppermute | solution.py:650
  47.4 5.5 %collective-permute-start.9 = (f32[4,1,320,128]{3,2,1,0:T(8,128)S(1)}, f32[4,1,320,128]{3,2,1,0:T(8,128)S(1)}, u32[]{:S(2)}, u32[]{:S(2)}) collective-permute-start(f32[4,1,320,128]{3,2,1,0:T(8,128)S(1)} %get-tuple-element.56), channel_id=1, source_target_pairs={{0,4},{4,0},{1,5},{5,1},{2,6},{6,2},{3,7},{7,3},{8,12},{12,8},{9,1... | collective-permute-start | bytes 1966088 | tf_op jit(solution)/shard_map/ppermute | solution.py:59
  47.5 9.2 %collective-permute-start.6 = (f32[4,2,64,128]{3,2,1,0:T(8,128)S(1)}, f32[4,2,64,128]{3,2,1,0:T(8,128)S(1)}, u32[]{:S(2)}, u32[]{:S(2)}) collective-permute-start(f32[4,2,64,128]{3,2,1,0:T(8,128)S(1)} %get-tuple-element.48), channel_id=1, source_target_pairs={{0,1},{1,0},{2,3},{3,2},{4,5},{5,4},{6,7},{7,6},{8,9},{9,8},{10,11... | collective-permute-start | bytes 786440 | tf_op jit(solution)/shard_map/ppermute | solution.py:785
  48.2 11.4 %collective-permute-start.7 = (f32[4,2,64,128]{3,2,1,0:T(8,128)S(1)}, f32[4,2,64,128]{3,2,1,0:T(8,128)S(1)}, u32[]{:S(2)}, u32[]{:S(2)}) collective-permute-start(f32[4,2,64,128]{3,2,1,0:T(8,128)S(1)} %get-tuple-element.49), channel_id=1, source_target_pairs={{0,8},{1,9},{8,16},{9,17},{10,2},{11,3},{16,24},{17,25},{18,10},{1... | collective-permute-start | bytes 786440 | tf_op jit(solution)/shard_map/ppermute | solution.py:59
  53.0 9.3 %collective-permute-start.10 = (f32[4,2,64,128]{3,2,1,0:T(8,128)S(1)}, f32[4,2,64,128]{3,2,1,0:T(8,128)S(1)}, u32[]{:S(2)}, u32[]{:S(2)}) collective-permute-start(f32[4,2,64,128]{3,2,1,0:T(8,128)S(1)} %get-tuple-element.57), channel_id=1, source_target_pairs={{0,1},{1,0},{2,3},{3,2},{4,5},{5,4},{6,7},{7,6},{8,9},{9,8},{10,11... | collective-permute-start | bytes 786440 | tf_op jit(solution)/shard_map/ppermute | solution.py:785
  53.5 10.9 %collective-permute-start.11 = (f32[4,2,64,128]{3,2,1,0:T(8,128)S(1)}, f32[4,2,64,128]{3,2,1,0:T(8,128)S(1)}, u32[]{:S(2)}, u32[]{:S(2)}) collective-permute-start(f32[4,2,64,128]{3,2,1,0:T(8,128)S(1)} %get-tuple-element.58), channel_id=1, source_target_pairs={{0,8},{1,9},{8,16},{9,17},{10,2},{11,3},{16,24},{17,25},{18,10},{1... | collective-permute-start | bytes 786440 | tf_op jit(solution)/shard_map/ppermute | solution.py:59
  59.6 8.8 %collective-permute-start.8 = (f32[4,2,64,128]{3,2,1,0:T(8,128)S(1)}, f32[4,2,64,128]{3,2,1,0:T(8,128)S(1)}, u32[]{:S(2)}, u32[]{:S(2)}) collective-permute-start(f32[4,2,64,128]{3,2,1,0:T(8,128)S(1)} %shard_map.87), channel_id=1, source_target_pairs={{0,1},{1,0},{2,3},{3,2},{4,5},{5,4},{6,7},{7,6},{8,9},{9,8},{10,11... | collective-permute-start | bytes 786440 | tf_op jit(solution)/shard_map/ppermute | solution.py:785
  64.5 8.6 %collective-permute-start.12 = (f32[4,2,64,128]{3,2,1,0:T(8,128)S(1)}, f32[4,2,64,128]{3,2,1,0:T(8,128)S(1)}, u32[]{:S(2)}, u32[]{:S(2)}) collective-permute-start(f32[4,2,64,128]{3,2,1,0:T(8,128)S(1)} %shard_map.90), channel_id=1, source_target_pairs={{0,1},{1,0},{2,3},{3,2},{4,5},{5,4},{6,7},{7,6},{8,9},{9,8},{10,11... | collective-permute-start | bytes 786440 | tf_op jit(solution)/shard_map/ppermute | solution.py:785
